TPU v7x, 32 devices: a whole 2x2x4 slice. The times are simulated.
32 devices in a mesh: gx: 4 (over z), gy: 8 (over y, x, core).
Axes of the slice: x: 2, y: 2, z: 4, core: 2. Of those that a mesh axis runs over, the one named last changes fastest.
Arguments:
- state: float32 [8, 2, 16, 4064], P(None, None, 'gx', 'gy'), may hold values from -1 to 5, as said below
- shear_offset: int32 [1], replicated, may hold values from 0 to 4063
- remap_shift: int32 [16], P('gx'), may hold values from 0 to 4063
- frac_index: int32 [16], P('gx'), may hold values from 0 to 15
Outputs:
- new_state: float32 [8, 2, 16, 4064], P(None, None, 'gx', 'gy')
Inputs may be any that keep to these rules, and one draw needn't show every extreme that they name: `state`: field 0 lies in 0.5 to 2, fields 1 to 3 and 5 to 7 within 1 in magnitude, field 4 in 1 to 5.
All inputs are finite; a program needn't handle non-finite values.
Results may differ from a plain program's by a relative error of at most 0.00002.
Values sent between devices are 32-bit elements; how exact they have to be, the bound alone decides.
No kernel may reach another device: no remote copies, remote signals or barrier semaphores. Data moves between devices by JAX's collectives and lax.ppermute only.
A program may use at most 64 MiB of HBM per device.

v0:
```python
import jax
import jax.numpy as jnp
from jax import lax
from jax.sharding import PartitionSpec as P

FRAC = 16


ADIABATIC = 5.0 / 3.0
ROTATION = 1.0
SHEAR_RATE = 1.5
MAX_SPEED = 5.0
TIME_STEP = 0.05


def with_halo(array, sides, width):
    for axis, dim in sides:
        peers, length = (lax.axis_size(axis), array.shape[dim])
        up = [(i, (i + 1) % peers) for i in range(peers)]
        down = [(j, i) for i, j in up]
        last = lax.slice_in_dim(array, length - width, length, axis=dim)
        leading = lax.slice_in_dim(array, 0, width, axis=dim)
        before = lax.ppermute(last, axis, up)
        after = lax.ppermute(leading, axis, down)
        array = jnp.concatenate([before, array, after], axis=dim)
    return array


def shifted_2(block, axis, distance):
    devices = range(lax.axis_size(axis))
    route = [((i - distance) % len(devices), i) for i in devices]
    return lax.ppermute(block, axis, route)


def next_cell(value, grid_axis):
    return jnp.roll(value, -1, grid_axis)


def prev_cell(value, grid_axis):
    return jnp.roll(value, 1, grid_axis)


def tendency(state):
    density, mom_x, mom_y, mom_z, energy, face_x, face_y, face_z = state
    cen_x = 0.5 * (face_x + next_cell(face_x, 1))
    cen_y = 0.5 * (face_y + next_cell(face_y, 2))
    cen_z = 0.5 * (face_z + next_cell(face_z, 0))
    vel_x = mom_x / density
    vel_y = mom_y / density
    vel_z = mom_z / density
    magnetic = 0.5 * (cen_x * cen_x + cen_y * cen_y + cen_z * cen_z)
    pressure = (ADIABATIC - 1.0) * (
        energy - 0.5 * (mom_x * vel_x + mom_y * vel_y + mom_z * vel_z) - magnetic
    ) + magnetic
    vel_dot = vel_x * cen_x + vel_y * cen_y + vel_z * cen_z
    conserved = (density, mom_x, mom_y, mom_z, energy)
    momenta = (mom_x, mom_y, mom_z)
    centred = (cen_x, cen_y, cen_z)
    velocity = (vel_x, vel_y, vel_z)
    change = [jnp.zeros_like(density) for member in range(5)]
    for normal, grid_axis in ((0, 1), (1, 2), (2, 0)):
        normal_speed = velocity[normal]
        across = centred[normal]
        fluxes = [momenta[normal]]
        for second in range(3):
            flux_term = momenta[second] * normal_speed - across * centred[second]
            if second == normal:
                flux_term = flux_term + pressure
            fluxes.append(flux_term)
        fluxes.append((energy + pressure) * normal_speed - across * vel_dot)
        for member in range(5):
            upwind = 0.5 * (
                prev_cell(fluxes[member], grid_axis) + fluxes[member]
            ) - 0.5 * MAX_SPEED * (conserved[member] - prev_cell(conserved[member], grid_axis))
            change[member] = change[member] - (next_cell(upwind, grid_axis) - upwind)
    change[1] = change[1] + 2.0 * ROTATION * mom_y
    change[2] = change[2] - (2.0 - SHEAR_RATE) * ROTATION * mom_x
    change[4] = change[4] + SHEAR_RATE * ROTATION * (mom_x * vel_y - cen_x * cen_y)
    elec_x = -(vel_y * cen_z - vel_z * cen_y)
    elec_y = -(vel_z * cen_x - vel_x * cen_z)
    elec_z = -(vel_x * cen_y - vel_y * cen_x)
    edge_x = 0.25 * (
        elec_x + prev_cell(elec_x, 2) + prev_cell(elec_x, 0) + prev_cell(prev_cell(elec_x, 2), 0)
    )
    edge_y = 0.25 * (
        elec_y + prev_cell(elec_y, 1) + prev_cell(elec_y, 0) + prev_cell(prev_cell(elec_y, 1), 0)
    )
    edge_z = 0.25 * (
        elec_z + prev_cell(elec_z, 1) + prev_cell(elec_z, 2) + prev_cell(prev_cell(elec_z, 1), 2)
    )
    delta_x = -(next_cell(edge_z, 2) - edge_z - (next_cell(edge_y, 0) - edge_y))
    delta_y = -(next_cell(edge_x, 0) - edge_x - (next_cell(edge_z, 1) - edge_z))
    delta_z = -(next_cell(edge_y, 1) - edge_y - (next_cell(edge_x, 2) - edge_x))
    return jnp.stack(change + [delta_x, delta_y, delta_z])


def fill_ghosts(state, width, offset):
    padded = with_halo(state, (("gx", 2),), width)
    left_strip = padded[:, :, :width, :]
    right_strip = padded[:, :, -width:, :]
    cells = state.shape[3]
    devices = lax.axis_size("gy")
    total = cells * devices
    amounts = (offset, (total - offset) % total)
    hop_counts = [amount // cells for amount in amounts]
    remainders = [amount % cells for amount in amounts]
    moved = (left_strip, right_strip)
    for bit_pos in range(devices.bit_length() - 1):
        shifted = shifted_2((moved[0], moved[1]), "gy", 1 << bit_pos)
        moved = tuple(
            (
                jnp.where(
                    hop_counts[member] // (1 << bit_pos) % 2 == 1, shifted[member], moved[member]
                )
                for member in range(2)
            )
        )
    earlier = shifted_2((moved[0], moved[1]), "gy", 1)
    windows = []
    for member in range(2):
        joined = jnp.concatenate([earlier[member], moved[member]], axis=3)
        windows.append(lax.dynamic_slice_in_dim(joined, cells - remainders[member], cells, axis=3))
    place = lax.axis_index("gx")
    new_left = jnp.where(place == 0, windows[0], left_strip)
    new_right = jnp.where(place == lax.axis_size("gx") - 1, windows[1], right_strip)
    radial = jnp.concatenate([new_left, padded[:, :, width:-width, :], new_right], axis=2)
    return with_halo(radial, (("gy", 3),), width)


def shards(state, shear_offset, remap_shift, frac_index):
    offset = shear_offset[0]
    padded = fill_ghosts(state, 4, offset)
    first = padded[:, :, 2:-2, 2:-2] + TIME_STEP * tendency(padded)[:, :, 2:-2, 2:-2]
    advanced = 0.5 * (
        state + (first[:, :, 2:-2, 2:-2] + TIME_STEP * tendency(first)[:, :, 2:-2, 2:-2])
    )
    fraction = (frac_index.astype(jnp.float32) + 0.5) / FRAC
    cells = advanced.shape[3]
    hop_counts = remap_shift // cells
    remainders = remap_shift % cells
    moved = advanced
    for bit_pos in range(lax.axis_size("gy").bit_length() - 1):
        shifted = shifted_2(moved, "gy", 1 << bit_pos)
        chosen = (hop_counts // (1 << bit_pos) % 2 == 1)[:, None]
        moved = jnp.where(chosen, shifted, moved)
    earlier = shifted_2(moved, "gy", 1)
    joined = jnp.concatenate([earlier, moved], axis=3)
    outputs = []
    for row_pos in range(joined.shape[2]):
        start = cells - 1 - remainders[row_pos]
        window = lax.dynamic_slice_in_dim(joined[:, :, row_pos, :], start, cells + 1, axis=2)
        weight = fraction[row_pos]
        outputs.append((1.0 - weight) * window[:, :, 1:] + weight * window[:, :, :-1])
    return jnp.stack(outputs, axis=2)


def solution(mesh):
    placed = (P(None, None, "gx", "gy"), P(), P("gx"), P("gx"))
    return jax.shard_map(
        shards, mesh=mesh, in_specs=placed, out_specs=P(None, None, "gx", "gy"), check_vma=False
    )
```

profile of v0, /device:TPU:0, one launch (start us, length us, event | category | flops | bytes accessed | tf_op | source)
XLA Modules:
  0.0 80.3 jit_solution(9083310122823432104)
XLA Ops:
  0.0 5.0 %collective-permute-start.5 = (f32[8,2,4,508]{3,2,1,0:T(4,128)}, f32[8,2,4,508]{3,2,1,0:T(4,128)S(1)}, u32[]{:S(2)}, u32[]{:S(2)}) collective-permute-start(f32[8,2,4,508]{3,2,1,0:T(4,128)} %param.4), channel_id=1, source_target_pairs={{8,0},{16,8},{24,16},{0,24},{9,1},{17,9},{25,17},{1,25},{10,2},{18... | collective-permute-start | bytes 390152 | tf_op jit(solution)/shard_map/ppermute | solution.py:24
  5.1 4.2 %collective-permute-done.5 = f32[8,2,4,508]{3,2,1,0:T(4,128)S(1)} collective-permute-done((f32[8,2,4,508]{3,2,1,0:T(4,128)}, f32[8,2,4,508]{3,2,1,0:T(4,128)S(1)}, u32[]{:S(2)}, u32[]{:S(2)}) %collective-permute-start.5) | collective-permute-done | bytes 130080 | tf_op jit(solution)/shard_map/ppermute | solution.py:24
  10.2 1.9 %collective-permute-done = f32[8,2,4,508]{3,2,1,0:T(4,128)S(1)} collective-permute-done((f32[8,2,4,508]{3,2,1,0:T(4,128)}, f32[8,2,4,508]{3,2,1,0:T(4,128)S(1)}, u32[]{:S(2)}, u32[]{:S(2)}) %collective-permute-start) | collective-permute-done | bytes 130080 | tf_op jit(solution)/shard_map/ppermute | solution.py:23
  12.0 2.5 %collective-permute-done.6 = f32[8,2,4,508]{3,2,1,0:T(4,128)S(1)} collective-permute-done((f32[8,2,4,508]{3,2,1,0:T(4,128)S(1)}, f32[8,2,4,508]{3,2,1,0:T(4,128)S(1)}, u32[]{:S(2)}, u32[]{:S(2)}) %collective-permute-start.6) | collective-permute-done | bytes 130080 | tf_op jit(solution)/shard_map/ppermute | solution.py:32
  14.6 0.6 collective-permute-start.7
  15.2 2.1 %collective-permute-done.1 = f32[8,2,4,508]{3,2,1,0:T(4,128)S(1)} collective-permute-done((f32[8,2,4,508]{3,2,1,0:T(4,128)S(1)}, f32[8,2,4,508]{3,2,1,0:T(4,128)S(1)}, u32[]{:S(2)}, u32[]{:S(2)}) %collective-permute-start.1) | collective-permute-done | bytes 130080 | tf_op jit(solution)/shard_map/ppermute | solution.py:32
  17.3 0.6 collective-permute-start.2
  18.0 3.9 %collective-permute-done.7 = f32[8,2,4,508]{3,2,1,0:T(4,128)S(1)} collective-permute-done((f32[8,2,4,508]{3,2,1,0:T(4,128)S(1)}, f32[8,2,4,508]{3,2,1,0:T(4,128)S(1)}, u32[]{:S(2)}, u32[]{:S(2)}) %collective-permute-start.7) | collective-permute-done | bytes 130080 | tf_op jit(solution)/shard_map/ppermute | solution.py:32
  21.9 1.6 %collective-permute-start.8 = (f32[8,2,4,508]{3,2,1,0:T(4,128)S(1)}, f32[8,2,4,508]{3,2,1,0:T(4,128)S(1)}, u32[]{:S(2)}, u32[]{:S(2)}) collective-permute-start(f32[8,2,4,508]{3,2,1,0:T(4,128)S(1)} %bitcast.750), channel_id=1, source_target_pairs={{4,0},{5,1},{6,2},{7,3},{0,4},{1,5},{2,6},{3,7},{12,8},{13,9},{14,... | collective-permute-start | bytes 390152 | tf_op jit(solution)/shard_map/ppermute | solution.py:32
  23.6 1.5 %collective-permute-start.3 = (f32[8,2,4,508]{3,2,1,0:T(4,128)S(1)}, f32[8,2,4,508]{3,2,1,0:T(4,128)S(1)}, u32[]{:S(2)}, u32[]{:S(2)}) collective-permute-start(f32[8,2,4,508]{3,2,1,0:T(4,128)S(1)} %bitcast.751), channel_id=1, source_target_pairs={{4,0},{5,1},{6,2},{7,3},{0,4},{1,5},{2,6},{3,7},{12,8},{13,9},{14,... | collective-permute-start | bytes 390152 | tf_op jit(solution)/shard_map/ppermute | solution.py:32
  25.0 2.5 %collective-permute-done.8 = f32[8,2,4,508]{3,2,1,0:T(4,128)S(1)} collective-permute-done((f32[8,2,4,508]{3,2,1,0:T(4,128)S(1)}, f32[8,2,4,508]{3,2,1,0:T(4,128)S(1)}, u32[]{:S(2)}, u32[]{:S(2)}) %collective-permute-start.8) | collective-permute-done | bytes 130080 | tf_op jit(solution)/shard_map/ppermute | solution.py:32
  27.6 1.3 %collective-permute-done.3 = f32[8,2,4,508]{3,2,1,0:T(4,128)S(1)} collective-permute-done((f32[8,2,4,508]{3,2,1,0:T(4,128)S(1)}, f32[8,2,4,508]{3,2,1,0:T(4,128)S(1)}, u32[]{:S(2)}, u32[]{:S(2)}) %collective-permute-start.3) | collective-permute-done | bytes 130080 | tf_op jit(solution)/shard_map/ppermute | solution.py:32
  29.0 3.9 %collective-permute-done.9 = f32[8,2,4,508]{3,2,1,0:T(4,128)S(1)} collective-permute-done((f32[8,2,4,508]{3,2,1,0:T(4,128)S(1)}, f32[8,2,4,508]{3,2,1,0:T(4,128)S(1)}, u32[]{:S(2)}, u32[]{:S(2)}) %collective-permute-start.9) | collective-permute-done | bytes 130080 | tf_op jit(solution)/shard_map/ppermute | solution.py:32
  33.1 1.2 %collective-permute-done.4 = f32[8,2,4,508]{3,2,1,0:T(4,128)S(1)} collective-permute-done((f32[8,2,4,508]{3,2,1,0:T(4,128)S(1)}, f32[8,2,4,508]{3,2,1,0:T(4,128)S(1)}, u32[]{:S(2)}, u32[]{:S(2)}) %collective-permute-start.4) | collective-permute-done | bytes 130080 | tf_op jit(solution)/shard_map/ppermute | solution.py:32
  34.7 0.5 collective-permute-start.10
  35.4 3.1 %collective-permute-done.11 = f32[8,2,12,4]{3,2,1,0:T(8,128)S(1)} collective-permute-done((f32[8,2,12,4]{3,2,1,0:T(8,128)S(1)}, f32[8,2,12,4]{3,2,1,0:T(8,128)S(1)}, u32[]{:S(2)}, u32[]{:S(2)}) %collective-permute-start.11) | collective-permute-done | bytes 3104 | tf_op jit(solution)/shard_map/ppermute | solution.py:24
  38.4 1.6 %collective-permute-done.10 = f32[8,2,12,4]{3,2,1,0:T(8,128)S(1)} collective-permute-done((f32[8,2,12,4]{3,2,1,0:T(8,128)S(1)}, f32[8,2,12,4]{3,2,1,0:T(8,128)S(1)}, u32[]{:S(2)}, u32[]{:S(2)}) %collective-permute-start.10) | collective-permute-done | bytes 3104 | tf_op jit(solution)/shard_map/ppermute | solution.py:23
  40.1 0.4 pad_maximum_fusion
  44.7 0.3 fusion.46
  50.8 5.3 %collective-permute-done.12 = f32[8,2,4,508]{3,2,1,0:T(4,128)S(1)} collective-permute-done((f32[8,2,4,508]{3,2,1,0:T(4,128)S(1)}, f32[8,2,4,508]{3,2,1,0:T(4,128)S(1)}, u32[]{:S(2)}, u32[]{:S(2)}) %collective-permute-start.12) | collective-permute-done | bytes 130080 | tf_op jit(solution)/shard_map/ppermute | solution.py:32
  56.2 5.9 %collective-permute-done.13 = f32[8,2,4,508]{3,2,1,0:T(4,128)S(1)} collective-permute-done((f32[8,2,4,508]{3,2,1,0:T(4,128)S(1)}, f32[8,2,4,508]{3,2,1,0:T(4,128)S(1)}, u32[]{:S(2)}, u32[]{:S(2)}) %collective-permute-start.13) | collective-permute-done | bytes 130080 | tf_op jit(solution)/shard_map/ppermute | solution.py:32
  62.2 1.6 %collective-permute-start.14 = (f32[8,2,4,508]{3,2,1,0:T(4,128)S(1)}, f32[8,2,4,508]{3,2,1,0:T(4,128)S(1)}, u32[]{:S(2)}, u32[]{:S(2)}) collective-permute-start(f32[8,2,4,508]{3,2,1,0:T(4,128)S(1)} %broadcast_select_fusion.1), channel_id=1, source_target_pairs={{4,0},{5,1},{6,2},{7,3},{0,4},{1,5},{2,6},{3,7},{12,8},{13,9},{14,... | collective-permute-start | bytes 390152 | tf_op jit(solution)/shard_map/ppermute | solution.py:32
  63.8 0.6 fusion.335
  64.5 2.8 %collective-permute-done.14 = f32[8,2,4,508]{3,2,1,0:T(4,128)S(1)} collective-permute-done((f32[8,2,4,508]{3,2,1,0:T(4,128)S(1)}, f32[8,2,4,508]{3,2,1,0:T(4,128)S(1)}, u32[]{:S(2)}, u32[]{:S(2)}) %collective-permute-start.14) | collective-permute-done | bytes 130080 | tf_op jit(solution)/shard_map/ppermute | solution.py:32
  67.4 0.6 fusion.334
  75.4 0.3 pad_slice_fusion.1
  75.7 0.2 fusion.150
  76.8 0.6 fusion.165
  77.4 0.7 fusion.167
  78.2 0.6 fusion.169
  78.8 0.8 fusion.171
  79.6 0.7 copy.146
  (265 shorter events, 10.9 us)
Async XLA Ops:
  0.0 9.3 %collective-permute-start.5 = (f32[8,2,4,508]{3,2,1,0:T(4,128)}, f32[8,2,4,508]{3,2,1,0:T(4,128)S(1)}, u32[]{:S(2)}, u32[]{:S(2)}) collective-permute-start(f32[8,2,4,508]{3,2,1,0:T(4,128)} %param.4), channel_id=1, source_target_pairs={{8,0},{16,8},{24,16},{0,24},{9,1},{17,9},{25,17},{1,25},{10,2},{18... | collective-permute-start | bytes 390152 | tf_op jit(solution)/shard_map/ppermute | solution.py:24
  5.0 7.0 %collective-permute-start = (f32[8,2,4,508]{3,2,1,0:T(4,128)}, f32[8,2,4,508]{3,2,1,0:T(4,128)S(1)}, u32[]{:S(2)}, u32[]{:S(2)}) collective-permute-start(f32[8,2,4,508]{3,2,1,0:T(4,128)} %param.4), channel_id=1, source_target_pairs={{0,8},{8,16},{16,24},{24,0},{1,9},{9,17},{17,25},{25,1},{2,10},{10... | collective-permute-start | bytes 390152 | tf_op jit(solution)/shard_map/ppermute | solution.py:23
  9.3 5.3 %collective-permute-start.6 = (f32[8,2,4,508]{3,2,1,0:T(4,128)S(1)}, f32[8,2,4,508]{3,2,1,0:T(4,128)S(1)}, u32[]{:S(2)}, u32[]{:S(2)}) collective-permute-start(f32[8,2,4,508]{3,2,1,0:T(4,128)S(1)} %collective-permute-done.5), channel_id=1, source_target_pairs={{7,0},{0,1},{1,2},{2,3},{3,4},{4,5},{5,6},{6,7},{15,8},{8,9},{9,10... | collective-permute-start | bytes 390152 | tf_op jit(solution)/shard_map/ppermute | solution.py:32
  12.0 5.3 %collective-permute-start.1 = (f32[8,2,4,508]{3,2,1,0:T(4,128)S(1)}, f32[8,2,4,508]{3,2,1,0:T(4,128)S(1)}, u32[]{:S(2)}, u32[]{:S(2)}) collective-permute-start(f32[8,2,4,508]{3,2,1,0:T(4,128)S(1)} %collective-permute-done), channel_id=1, source_target_pairs={{7,0},{0,1},{1,2},{2,3},{3,4},{4,5},{5,6},{6,7},{15,8},{8,9},{9,10... | collective-permute-start | bytes 390152 | tf_op jit(solution)/shard_map/ppermute | solution.py:32
  14.6 7.3 %collective-permute-start.7 = (f32[8,2,4,508]{3,2,1,0:T(4,128)S(1)}, f32[8,2,4,508]{3,2,1,0:T(4,128)S(1)}, u32[]{:S(2)}, u32[]{:S(2)}) collective-permute-start(f32[8,2,4,508]{3,2,1,0:T(4,128)S(1)} %bitcast.753), channel_id=1, source_target_pairs={{6,0},{7,1},{0,2},{1,3},{2,4},{3,5},{4,6},{5,7},{14,8},{15,9},{8,1... | collective-permute-start | bytes 390152 | tf_op jit(solution)/shard_map/ppermute | solution.py:32
  17.3 6.2 %collective-permute-start.2 = (f32[8,2,4,508]{3,2,1,0:T(4,128)S(1)}, f32[8,2,4,508]{3,2,1,0:T(4,128)S(1)}, u32[]{:S(2)}, u32[]{:S(2)}) collective-permute-start(f32[8,2,4,508]{3,2,1,0:T(4,128)S(1)} %bitcast.752), channel_id=1, source_target_pairs={{6,0},{7,1},{0,2},{1,3},{2,4},{3,5},{4,6},{5,7},{14,8},{15,9},{8,1... | collective-permute-start | bytes 390152 | tf_op jit(solution)/shard_map/ppermute | solution.py:32
  21.9 5.6 %collective-permute-start.8 = (f32[8,2,4,508]{3,2,1,0:T(4,128)S(1)}, f32[8,2,4,508]{3,2,1,0:T(4,128)S(1)}, u32[]{:S(2)}, u32[]{:S(2)}) collective-permute-start(f32[8,2,4,508]{3,2,1,0:T(4,128)S(1)} %bitcast.750), channel_id=1, source_target_pairs={{4,0},{5,1},{6,2},{7,3},{0,4},{1,5},{2,6},{3,7},{12,8},{13,9},{14,... | collective-permute-start | bytes 390152 | tf_op jit(solution)/shard_map/ppermute | solution.py:32
  23.6 5.4 %collective-permute-start.3 = (f32[8,2,4,508]{3,2,1,0:T(4,128)S(1)}, f32[8,2,4,508]{3,2,1,0:T(4,128)S(1)}, u32[]{:S(2)}, u32[]{:S(2)}) collective-permute-start(f32[8,2,4,508]{3,2,1,0:T(4,128)S(1)} %bitcast.751), channel_id=1, source_target_pairs={{4,0},{5,1},{6,2},{7,3},{0,4},{1,5},{2,6},{3,7},{12,8},{13,9},{14,... | collective-permute-start | bytes 390152 | tf_op jit(solution)/shard_map/ppermute | solution.py:32
  27.5 5.3 %collective-permute-start.9 = (f32[8,2,4,508]{3,2,1,0:T(4,128)S(1)}, f32[8,2,4,508]{3,2,1,0:T(4,128)S(1)}, u32[]{:S(2)}, u32[]{:S(2)}) collective-permute-start(f32[8,2,4,508]{3,2,1,0:T(4,128)S(1)} %bitcast.756), channel_id=1, source_target_pairs={{7,0},{0,1},{1,2},{2,3},{3,4},{4,5},{5,6},{6,7},{15,8},{8,9},{9,10... | collective-permute-start | bytes 390152 | tf_op jit(solution)/shard_map/ppermute | solution.py:32
  29.0 5.3 %collective-permute-start.4 = (f32[8,2,4,508]{3,2,1,0:T(4,128)S(1)}, f32[8,2,4,508]{3,2,1,0:T(4,128)S(1)}, u32[]{:S(2)}, u32[]{:S(2)}) collective-permute-start(f32[8,2,4,508]{3,2,1,0:T(4,128)S(1)} %bitcast.758), channel_id=1, source_target_pairs={{7,0},{0,1},{1,2},{2,3},{3,4},{4,5},{5,6},{6,7},{15,8},{8,9},{9,10... | collective-permute-start | bytes 390152 | tf_op jit(solution)/shard_map/ppermute | solution.py:32
  33.1 1.4 %copy-start = (f32[8,2,4,508]{3,2,1,0:T(4,128)S(1)}, f32[8,2,4,508]{3,2,1,0:T(4,128)}, u32[]{:S(2)}) copy-start(f32[8,2,4,508]{3,2,1,0:T(4,128)} %param.4) | copy-start | bytes 390148
  34.7 0.7 copy-start.1
  34.7 3.8 %collective-permute-start.11 = (f32[8,2,12,4]{3,2,1,0:T(8,128)S(1)}, f32[8,2,12,4]{3,2,1,0:T(8,128)S(1)}, u32[]{:S(2)}, u32[]{:S(2)}) collective-permute-start(f32[8,2,12,4]{3,2,1,0:T(8,128)S(1)} %get-tuple-element.113), channel_id=1, source_target_pairs={{1,0},{2,1},{3,2},{4,3},{5,4},{6,5},{7,6},{0,7},{9,8},{10,9},{11,1... | collective-permute-start | bytes 9224 | tf_op jit(solution)/shard_map/ppermute | solution.py:24
  34.7 5.3 %collective-permute-start.10 = (f32[8,2,12,4]{3,2,1,0:T(8,128)S(1)}, f32[8,2,12,4]{3,2,1,0:T(8,128)S(1)}, u32[]{:S(2)}, u32[]{:S(2)}) collective-permute-start(f32[8,2,12,4]{3,2,1,0:T(8,128)S(1)} %get-tuple-element.112), channel_id=1, source_target_pairs={{0,1},{1,2},{2,3},{3,4},{4,5},{5,6},{6,7},{7,0},{8,9},{9,10},{10,1... | collective-permute-start | bytes 9224 | tf_op jit(solution)/shard_map/ppermute | solution.py:23
  50.7 5.3 %collective-permute-start.12 = (f32[8,2,4,508]{3,2,1,0:T(4,128)S(1)}, f32[8,2,4,508]{3,2,1,0:T(4,128)S(1)}, u32[]{:S(2)}, u32[]{:S(2)}) collective-permute-start(f32[8,2,4,508]{3,2,1,0:T(4,128)S(1)} %fusion.7), channel_id=1, source_target_pairs={{7,0},{0,1},{1,2},{2,3},{3,4},{4,5},{5,6},{6,7},{15,8},{8,9},{9,10... | collective-permute-start | bytes 390152 | tf_op jit(solution)/shard_map/ppermute | solution.py:32
  56.1 6.0 %collective-permute-start.13 = (f32[8,2,4,508]{3,2,1,0:T(4,128)S(1)}, f32[8,2,4,508]{3,2,1,0:T(4,128)S(1)}, u32[]{:S(2)}, u32[]{:S(2)}) collective-permute-start(f32[8,2,4,508]{3,2,1,0:T(4,128)S(1)} %broadcast_select_fusion), channel_id=1, source_target_pairs={{6,0},{7,1},{0,2},{1,3},{2,4},{3,5},{4,6},{5,7},{14,8},{15,9},{8,1... | collective-permute-start | bytes 390152 | tf_op jit(solution)/shard_map/ppermute | solution.py:32
  62.1 1.7 %copy-start.2 = (s32[4]{0:T(128)S(1)}, s32[4]{0:T(128)}, u32[]{:S(2)}) copy-start(s32[4]{0:T(128)} %param.7) | copy-start | bytes 52
  62.2 5.0 %collective-permute-start.14 = (f32[8,2,4,508]{3,2,1,0:T(4,128)S(1)}, f32[8,2,4,508]{3,2,1,0:T(4,128)S(1)}, u32[]{:S(2)}, u32[]{:S(2)}) collective-permute-start(f32[8,2,4,508]{3,2,1,0:T(4,128)S(1)} %broadcast_select_fusion.1), channel_id=1, source_target_pairs={{4,0},{5,1},{6,2},{7,3},{0,4},{1,5},{2,6},{3,7},{12,8},{13,9},{14,... | collective-permute-start | bytes 390152 | tf_op jit(solution)/shard_map/ppermute | solution.py:32
  67.4 8.4 %collective-permute-start.15 = (f32[8,2,4,508]{3,2,1,0:T(4,128)S(1)}, f32[8,2,4,508]{3,2,1,0:T(4,128)S(1)}, u32[]{:S(2)}, u32[]{:S(2)}) collective-permute-start(f32[8,2,4,508]{3,2,1,0:T(4,128)S(1)} %broadcast_select_fusion.2), channel_id=1, source_target_pairs={{7,0},{0,1},{1,2},{2,3},{3,4},{4,5},{5,6},{6,7},{15,8},{8,9},{9,10... | collective-permute-start | bytes 390152 | tf_op jit(solution)/shard_map/ppermute | solution.py:32
where the time goes:
time: 80.9 us; the launch traced here: 80.3 us
  waiting for transfers between devices  42.2 us (52%)
  starting transfers between devices  11.8 us (15%)
  other arithmetic  10.1 us (12%)
  between operations  9.67 us (12%)
  local copies, waits for them, and re-layouts  6.48 us (8%)
    ppermute x12, waiting for transfers between devices, shifted_2(): return lax.ppermute(block, axis, route)  31.4 us
    ppermute x2, waiting for transfers between devices, with_halo(): after = lax.ppermute(leading, axis, down)  7.31 us
    ppermute x12, starting transfers between devices, shifted_2(): return lax.ppermute(block, axis, route)  6.22 us
    ppermute x2, starting transfers between devices, with_halo(): after = lax.ppermute(leading, axis, down)  5.11 us
    ppermute x2, waiting for transfers between devices, with_halo(): before = lax.ppermute(last, axis, up)  3.51 us
    another operation x5, other arithmetic, shards(): return jnp.stack(outputs, axis=2)  2.78 us
    concatenate x92, local copies, waits for them, and re-layouts, prev_cell(): return jnp.roll(value, 1, grid_axis)  2.27 us
    unnamed x14, other arithmetic  2.04 us
  transfers between devices with their start and end apart: 16, of which 14 were waited for; matrix products, arithmetic and copies ran while one was open for 2% of the time, Pallas kernels for 0%

commit v1 on v0

v1 whole, which is shorter than its diff:
```python
import jax
import jax.numpy as jnp
from jax import lax
from jax.experimental import pallas as pl
from jax.experimental.pallas import tpu as pltpu
from jax.sharding import PartitionSpec as P

FRAC = 16

ADIABATIC = 5.0 / 3.0
ROTATION = 1.0
SHEAR_RATE = 1.5
MAX_SPEED = 5.0
TIME_STEP = 0.05

LANES = 128
FIELDS = 8
PLANES = 2
BELOW = 3
ABOVE = 3
SENT = 2
SLOT = FIELDS * PLANES * SENT
HALF_STEP = 0.5 * TIME_STEP
DIFFUSE = 0.5 * MAX_SPEED * TIME_STEP
EDGE = 0.25 * TIME_STEP


def lane_index(shape):
    return lax.broadcasted_iota(jnp.int32, shape, 1)


def row_index(shape):
    return lax.broadcasted_iota(jnp.int32, shape, 0)


def after(value):
    return pltpu.roll(value, LANES - 1, 1)


def before(value):
    return pltpu.roll(value, 1, 1)


def roll_tiles(tiles, amount):
    count = len(tiles)
    part = amount % LANES
    whole = amount // LANES
    turned = [pltpu.roll(tile, part, 1) for tile in tiles]
    low = lane_index(tiles[0].shape) < part
    tiles = [jnp.where(low, turned[i - 1], turned[i]) for i in range(count)]
    bit = 1
    while bit < count:
        tiles = [
            jnp.where((whole // bit) % 2 == 1, tiles[(i - bit) % count], tiles[i])
            for i in range(count)
        ]
        bit *= 2
    return tiles


def shift_cells(tiles, amount, cells):
    total = len(tiles) * LANES
    high = roll_tiles(tiles, amount)
    low = roll_tiles(tiles, (amount + total - cells) % total)
    lane = lane_index(tiles[0].shape)
    return [
        jnp.where(lane + i * LANES >= amount, high[i], low[i]) for i in range(len(tiles))
    ]


def shear_amounts(shear, cells, peers):
    total = cells * peers
    return shear, (total - shear) % total


def pack_kernel(cells, peers, chunk, shear_ref, state_ref, first_ref, second_ref):
    width = chunk + BELOW + ABOVE
    half = width // 2
    rows = state_ref.shape[2]
    place = lax.axis_index("gx")
    places = lax.axis_size("gx")
    lower, upper = shear_amounts(shear_ref[0], cells, peers)
    up_turn = jnp.where(place == places - 1, lower % cells, 0)
    down_turn = jnp.where(place == 0, upper % cells, 0)
    odd = place % 2
    own_first = odd * (peers * SLOT)
    own_second = (1 - odd) * (peers * SLOT)

    def stacked(pieces):
        return jnp.concatenate(pieces, axis=0)

    def tiles_of(value):
        spare = -cells % LANES
        pad = jnp.zeros((value.shape[0], spare), value.dtype)
        value = jnp.concatenate([value, pad], axis=1)
        return [value[:, i : i + LANES] for i in range(0, cells + spare, LANES)]

    def turned(value, amount):
        return jnp.concatenate(shift_cells(tiles_of(value), amount, cells), axis=1)[:, :cells]

    def windows(value):
        top = peers * chunk + ABOVE - cells
        wide = jnp.concatenate([value[:, cells - BELOW :], value, value[:, :top]], axis=1)
        return [wide[:, k * chunk : k * chunk + width] for k in range(peers)]

    per_group = 8 // SENT
    groups = FIELDS * PLANES // per_group
    for group in range(groups):
        members = range(group * per_group, (group + 1) * per_group)
        blocks = [state_ref[fz // PLANES, fz % PLANES] for fz in members]
        bottom = stacked([b[:SENT] for b in blocks])
        top = stacked([b[rows - SENT :] for b in blocks])
        to_up = windows(turned(top, up_turn))
        to_down = windows(turned(bottom, down_turn))
        if group == 0:
            faces = [state_ref[5, z][SENT : SENT + 1] for z in range(PLANES)]
            pieces = [faces[i // SENT] for i in range(PLANES * SENT)]
            faces = windows(turned(stacked(pieces * (8 // len(pieces))), down_turn))
            to_down = [
                jnp.concatenate(
                    [
                        value,
                        jnp.where(
                            row_index((8, half)) % SENT == 0, face[:, :half], face[:, half:]
                        ),
                    ],
                    axis=1,
                )
                for value, face in zip(to_down, faces)
            ]

        def put(ref, base, values):
            for k, value in enumerate(values):
                at = pl.multiple_of(base + (k * SLOT + group * 8), 8)
                ref[pl.ds(at, 8), 0 : value.shape[1]] = value

        put(first_ref, own_first, windows(bottom))
        put(second_ref, own_second, windows(top))

        @pl.when(odd == 0)
        def _():
            put(first_ref, own_second, to_up)
            put(second_ref, own_first, to_down)

        @pl.when(odd == 1)
        def _():
            put(first_ref, own_second, to_down)
            put(second_ref, own_first, to_up)


def cell_terms(state, next_face_x):
    planes = range(PLANES)
    face_z = state[7]
    out = []
    for z in planes:
        density, mom_x, mom_y, mom_z, energy, face_x, face_y = (state[f][z] for f in range(7))
        cen_x = 0.5 * (face_x + next_face_x[z])
        cen_y = 0.5 * (face_y + after(face_y))
        cen_z = 0.5 * (face_z[z] + face_z[(z + 1) % PLANES])
        inverse = 1.0 / density
        vel_x, vel_y, vel_z = (mom_x * inverse, mom_y * inverse, mom_z * inverse)
        magnetic = 0.5 * (cen_x * cen_x + cen_y * cen_y + cen_z * cen_z)
        kinetic = 0.5 * (mom_x * vel_x + mom_y * vel_y + mom_z * vel_z)
        pressure = (ADIABATIC - 1.0) * (energy - kinetic - magnetic) + magnetic
        vel_dot = vel_x * cen_x + vel_y * cen_y + vel_z * cen_z
        scaled_p = HALF_STEP * pressure
        total = energy + pressure
        sv_x, sv_y, sv_z = (HALF_STEP * vel_x, HALF_STEP * vel_y, HALF_STEP * vel_z)
        sb_x, sb_y, sb_z = (HALF_STEP * cen_x, HALF_STEP * cen_y, HALF_STEP * cen_z)
        xx = mom_x * sv_x - cen_x * sb_x + scaled_p
        yy = mom_y * sv_y - cen_y * sb_y + scaled_p
        zz = mom_z * sv_z - cen_z * sb_z + scaled_p
        xy = mom_x * sv_y - cen_x * sb_y
        xz = mom_x * sv_z - cen_x * sb_z
        yz = mom_y * sv_z - cen_y * sb_z
        diffuse = [DIFFUSE * state[f][z] for f in range(5)]
        flux_x = [HALF_STEP * mom_x, xx, xy, xz, total * sv_x - sb_x * vel_dot]
        flux_y = [HALF_STEP * mom_y, xy, yy, yz, total * sv_y - sb_y * vel_dot]
        flux_z = [HALF_STEP * mom_z, xz, yz, zz, total * sv_z - sb_z * vel_dot]
        out.append(
            dict(
                diffuse=diffuse,
                low_x=[f + d for f, d in zip(flux_x, diffuse)],
                high_x=[f - d for f, d in zip(flux_x, diffuse)],
                low_y=[f + d for f, d in zip(flux_y, diffuse)],
                high_y=[f - d for f, d in zip(flux_y, diffuse)],
                flux_z=flux_z,
                shear=xy,
                e_x=EDGE * (vel_z * cen_y - vel_y * cen_z),
                e_y=EDGE * (vel_x * cen_z - vel_z * cen_x),
                e_z=EDGE * (vel_y * cen_x - vel_x * cen_y),
            )
        )
    return out


def plane_sum(terms, name):
    total = terms[0][name]
    for z in range(1, PLANES):
        total = total + terms[z][name]
    return total


def face_x_change(here, low):
    edge_y = plane_sum(here, "e_y") + plane_sum(low, "e_y")
    edge_y = [edge_y] * PLANES
    out = []
    for z in range(PLANES):
        pair = here[z]["e_z"] + low[z]["e_z"]
        out.append((edge_y[(z + 1) % PLANES] - edge_y[z]) - (after(pair) - before(pair)))
    return out


def row_step(state, low, here, high):
    new = [[None] * PLANES for f in range(FIELDS)]
    faces = [
        [
            (here[z - 1]["flux_z"][f] + here[z]["flux_z"][f])
            - (here[z]["diffuse"][f] - here[z - 1]["diffuse"][f])
            for f in range(5)
        ]
        for z in range(PLANES)
    ]
    for z in range(PLANES):
        cell = here[z]
        for f in range(5):
            along_x = high[z]["high_x"][f] - low[z]["low_x"][f]
            along_y = after(cell["high_y"][f]) - before(cell["low_y"][f])
            along_z = faces[(z + 1) % PLANES][f] - faces[z][f]
            kept = state[f][z] - 4.0 * cell["diffuse"][f]
            new[f][z] = kept - (along_x + along_y + along_z)
        mom_x, mom_y = (state[1][z], state[2][z])
        new[1][z] = new[1][z] + (TIME_STEP * 2.0 * ROTATION) * mom_y
        new[2][z] = new[2][z] - (TIME_STEP * (2.0 - SHEAR_RATE) * ROTATION) * mom_x
        new[4][z] = new[4][z] + (2.0 * SHEAR_RATE * ROTATION) * cell["shear"]
    change_x = face_x_change(here, low)
    exz = plane_sum(here, "e_x")
    edge_x = [exz + before(exz)] * PLANES
    along_y = after(exz) - before(exz)
    along_x = plane_sum(high, "e_y") - plane_sum(low, "e_y")
    for z in range(PLANES):
        pair = here[z]["e_z"] + low[z]["e_z"]
        pair_up = high[z]["e_z"] + here[z]["e_z"]
        edge = pair + before(pair)
        edge_up = pair_up + before(pair_up)
        new[5][z] = state[5][z] + change_x[z]
        new[6][z] = state[6][z] + ((edge_up - edge) - (edge_x[(z + 1) % PLANES] - edge_x[z]))
        new[7][z] = state[7][z] + (along_y - along_x)
    return new


def step_kernel(
    cells, peers, chunk, rows,
    shear_ref, shift_ref, frac_ref, first_ref, second_ref,
    out_ref, state_ref, mid_ref,
):
    width = chunk + BELOW + ABOVE
    half = width // 2
    place = lax.axis_index("gx")
    places = lax.axis_size("gx")
    part = lax.axis_index("gy")
    odd = place % 2
    even = odd == 0
    shape = (peers, LANES)
    lane = lane_index(shape)
    lower, upper = shear_amounts(shear_ref[0], cells, peers)
    lower = jnp.where(place == 0, lower, 0)
    upper = jnp.where(place == places - 1, upper, 0)
    column = part * chunk - BELOW + lane

    def load(ref, position, row):
        return ref[pl.ds(position * (peers * SLOT) + row, peers, stride=SLOT), :]

    def turn(value, amount):
        return pltpu.roll(value, amount, 0)

    def strips(value, amount):
        hop = amount // cells
        source = column - amount % cells
        pick = turn(value, hop % peers)
        pick = jnp.where(source < 0, turn(value, (hop + 1) % peers), pick)
        pick = jnp.where(source < -cells, turn(value, (hop + 2) % peers), pick)
        return jnp.where(source >= cells, turn(value, (hop + peers - 1) % peers), pick)

    def own_strips(value):
        pick = jnp.where(column < 0, turn(value, 1), value)
        return jnp.where(column >= cells, turn(value, peers - 1), pick)

    for f in range(FIELDS):
        for z in range(PLANES):
            for g in range(SENT):
                at = (f * PLANES + z) * SENT + g
                first = [load(first_ref, p, at) for p in range(2)]
                second = [load(second_ref, p, at) for p in range(2)]
                own_low = jnp.where(even, first[0], first[1])
                own_high = jnp.where(even, second[1], second[0])
                from_first = jnp.where(even, first[1], first[0])
                from_second = jnp.where(even, second[0], second[1])
                ghost_low = jnp.where(even, from_second, from_first)
                ghost_high = jnp.where(even, from_first, from_second)
                state_ref[g, f, z] = strips(ghost_low, lower)
                state_ref[SENT + g, f, z] = own_strips(own_low)
                state_ref[rows + g, f, z] = own_strips(own_high)
                state_ref[SENT + rows + g, f, z] = strips(ghost_high, upper)
    face_high = []
    for z in range(PLANES):
        parts = []
        for g in range(SENT):
            at = z * SENT + g
            ghost = jnp.where(even, load(first_ref, 1, at), load(second_ref, 1, at))
            parts.append(pltpu.roll(ghost, LANES - width + g * half, 1))
        face_high.append(strips(jnp.where(lane < half, parts[0], parts[1]), upper))

    def row_of(ref, index):
        return [[ref[index, f, z] for z in range(PLANES)] for f in range(FIELDS)]

    def faces_of(ref, index):
        return [ref[index, 5, z] for z in range(PLANES)]

    count = rows + 2 * SENT
    low = cell_terms(row_of(state_ref, 0), faces_of(state_ref, 1))
    here = cell_terms(row_of(state_ref, 1), faces_of(state_ref, 2))
    for index in range(1, count - 1):
        beyond = face_high if index + 2 == count else faces_of(state_ref, index + 2)
        high = cell_terms(row_of(state_ref, index + 1), beyond)
        new = row_step(row_of(state_ref, index), low, here, high)
        for f in range(FIELDS):
            for z in range(PLANES):
                mid_ref[index - 1, f, z] = new[f][z]
        low, here = here, high
    change = face_x_change(here, low)
    mid_face = [state_ref[count - 1, 5, z] + change[z] for z in range(PLANES)]

    count = rows + 2
    low = cell_terms(row_of(mid_ref, 0), faces_of(mid_ref, 1))
    here = cell_terms(row_of(mid_ref, 1), faces_of(mid_ref, 2))
    for index in range(1, count - 1):
        beyond = mid_face if index + 2 == count else faces_of(mid_ref, index + 2)
        high = cell_terms(row_of(mid_ref, index + 1), beyond)
        new = row_step(row_of(mid_ref, index), low, here, high)
        row = index - 1
        shift = shift_ref[row]
        hop = shift // cells
        crossing = part * chunk + lane % chunk + shift % cells >= cells
        weight = (frac_ref[row].astype(jnp.float32) + 0.5) / FRAC
        for f in range(FIELDS):
            packed = None
            for z in range(PLANES):
                done = 0.5 * (state_ref[index + 1, f, z] + new[f][z])
                mixed = (1.0 - weight) * done + weight * before(done)
                moved = pltpu.roll(mixed, (z * chunk - BELOW) % LANES, 1)
                packed = moved if z == 0 else jnp.where(lane < z * chunk, packed, moved)
            sent = jnp.where(crossing, turn(packed, (hop + 1) % peers), turn(packed, hop % peers))
            out_ref[pl.ds(f * rows + row, peers, stride=FIELDS * rows), :] = sent
        low, here = here, high


def place_kernel(cells, peers, chunk, shift_ref, in_ref, out_ref):
    rows = out_ref.shape[2]
    block = FIELDS * rows
    per_group = 8 // rows
    amounts = [shift_ref[x] % cells for x in range(rows)]
    lanes = peers * chunk
    member = row_index((8, LANES)) % rows
    for group in range(FIELDS // per_group):
        pieces = [in_ref[k * block + group * 8 : k * block + group * 8 + 8, :] for k in range(peers)]
        for z in range(PLANES):
            joined = jnp.concatenate(
                [piece[:, z * chunk : (z + 1) * chunk] for piece in pieces], axis=1
            )
            tiles = [joined[:, i : i + LANES] for i in range(0, lanes, LANES)]
            result = shift_cells(tiles, amounts[0], cells)
            for x in range(1, rows):
                moved = shift_cells(tiles, amounts[x], cells)
                result = [jnp.where(member == x, m, r) for m, r in zip(moved, result)]
            result = jnp.concatenate(result, axis=1)[:, :cells]
            for g in range(per_group):
                out_ref[group * per_group + g, z] = result[g * rows : (g + 1) * rows]


def solution(mesh):
    places, peers = (mesh.shape["gx"], mesh.shape["gy"])

    def groups_from(start):
        return [
            [(start + pair + p) % places * peers + k for p in range(2) for k in range(peers)]
            for pair in range(0, places, 2)
        ]

    smem = pl.BlockSpec(memory_space=pltpu.SMEM)
    vmem = pl.BlockSpec(memory_space=pltpu.VMEM)

    def shards(state, shear_offset, remap_shift, frac_index):
        rows, cells = state.shape[2:]
        chunk = -(-cells // peers)
        message = jax.ShapeDtypeStruct((2 * peers * SLOT, LANES), jnp.float32)
        first, second = pl.pallas_call(
            lambda *refs: pack_kernel(cells, peers, chunk, *refs),
            out_shape=(message, message),
            in_specs=[smem, vmem],
            out_specs=(vmem, vmem),
            name="pack",
        )(shear_offset, state)
        axes = ("gx", "gy")
        first = lax.all_to_all(
            first, axes, 0, 0, axis_index_groups=groups_from(0), tiled=True
        )
        second = lax.all_to_all(
            second, axes, 0, 0, axis_index_groups=groups_from(1), tiled=True
        )
        block = FIELDS * rows
        moved = pl.pallas_call(
            lambda *refs: step_kernel(cells, peers, chunk, rows, *refs),
            out_shape=jax.ShapeDtypeStruct((peers * block, LANES), jnp.float32),
            in_specs=[smem, smem, smem, vmem, vmem],
            out_specs=vmem,
            scratch_shapes=[
                pltpu.VMEM((rows + 2 * SENT, FIELDS, PLANES, peers, LANES), jnp.float32),
                pltpu.VMEM((rows + 2, FIELDS, PLANES, peers, LANES), jnp.float32),
            ],
            name="step",
        )(shear_offset, remap_shift, frac_index, first, second)
        moved = lax.all_to_all(moved, "gy", 0, 0, tiled=True)
        return pl.pallas_call(
            lambda *refs: place_kernel(cells, peers, chunk, *refs),
            out_shape=jax.ShapeDtypeStruct(state.shape, jnp.float32),
            in_specs=[smem, vmem],
            out_specs=vmem,
            name="place",
        )(remap_shift, moved)

    placed = (P(None, None, "gx", "gy"), P(), P("gx"), P("gx"))
    return jax.shard_map(
        shards, mesh=mesh, in_specs=placed, out_specs=P(None, None, "gx", "gy"), check_vma=False
    )
```

time: 80.9 us -> 46.4 us (0.57)
  waiting for transfers between devices: 42.2 us -> 0 us
  blocking collectives: 0 us -> 37.2 us
  starting transfers between devices: 11.8 us -> 0 us
  other arithmetic: 10.1 us -> 0 us
  between operations: 9.67 us -> 0.66 us
  Pallas kernels: 0 us -> 8.2 us
  local copies, waits for them, and re-layouts: 6.48 us -> 0.01 us
    ppermute x16 -> x0, waiting for transfers between devices: 42.2 us -> none  [the longest x12 31.4 us: shifted_2(): return lax.ppermute(block, axis, route)]
    all_to_all x0 -> x3, blocking collectives: none -> 37.2 us  [the longest x1 15.7 us: shards(): lax.all_to_all(second, axes, 0, 0, axis_index_groups=groups_from(1), tile...]
    ppermute x16 -> x0, starting transfers between devices: 11.8 us -> none  [the longest x12 6.22 us: shifted_2(): return lax.ppermute(block, axis, route)]
    pallas_call x0 -> x3, Pallas kernels: none -> 8.2 us  [the longest x1 3.01 us: shards(): pl.pallas_call(lambda *refs: step_kernel(cells, peers, chunk, rows, *refs...]
    concatenate x166 -> x0, local copies, waits for them, and re-layouts: 3.72 us -> none  [the longest x92 2.27 us: prev_cell(): return jnp.roll(value, 1, grid_axis)]
    another operation x7 -> x0, other arithmetic: 2.96 us -> none  [the longest x5 2.78 us: shards(): return jnp.stack(outputs, axis=2)]
    unnamed x14 -> x0, other arithmetic: 2.04 us -> none
    slice x8 -> x0, local copies, waits for them, and re-layouts: 1.82 us -> none  [the longest x1 0.64 us: shards(): start = cells - 1 - remainders[row_pos]]
  transfers between devices with their start and end apart: 16 -> 0, of which waited for: 14 -> 0; matrix products, arithmetic and copies ran while one was open for 2% -> 0% of each run, Pallas kernels for 0% -> 0%
where the time goes in v1:
time: 46.4 us; the launch traced here: 46 us
  blocking collectives  37.2 us (80%)
  Pallas kernels  8.2 us (18%)
  between operations  0.66 us (1%)
    all_to_all x1, blocking collectives, shards(): lax.all_to_all(second, axes, 0, 0, axis_index_groups=groups_from(1), tile...  15.7 us
    all_to_all x1, blocking collectives, shards(): lax.all_to_all(first, axes, 0, 0, axis_index_groups=groups_from(0), tiled...  11.9 us
    all_to_all x1, blocking collectives, shards(): moved = lax.all_to_all(moved, 'gy', 0, 0, tiled=True)  9.51 us
    pallas_call x1, Pallas kernels, shards(): pl.pallas_call(lambda *refs: step_kernel(cells, peers, chunk, rows, *refs...  3.01 us
    pallas_call x1, Pallas kernels, shards(): pl.pallas_call(lambda *refs: pack_kernel(cells, peers, chunk, *refs), out...  2.86 us
    pallas_call x1, Pallas kernels, shards(): pl.pallas_call(lambda *refs: place_kernel(cells, peers, chunk, *refs), ou...  2.33 us

profile of v1, /device:TPU:0, one launch (start us, length us, event | category | flops | bytes accessed | tf_op | source)
XLA Modules:
  0.0 46.0 jit_solution(12969800891392570969)
XLA Ops:
  0.7 2.9 %pack.1 = (f32[512,128]{1,0:T(8,128)}, f32[512,128]{1,0:T(8,128)}) custom-call(s32[1]{0:T(128)S(6)} %copy.5.refs_0_, f32[8,2,4,508]{3,2,1,0:T(4,128)} %refs_1_.2), custom_call_target="tpu_custom_call" | custom-call | tf_op jit(solution)/shard_map/pack/pallas_call | solution.py:397
  3.5 0.0 copy-start
  3.5 15.7 %all_to_all.33 = f32[16,32,128]{2,1,0:T(8,128)} all-to-all(f32[16,32,128]{2,1,0:T(8,128)} %bitcast.11), channel_id=1, replica_groups={{8,9,10,11,12,13,14,15,16,17,18,19,20,21,22,23},{24,25,26,27,28,29,30,3..., dimensions={0} | all-to-all | bytes 524288 | tf_op jit(solution)/shard_map/all_to_all | solution.py:408
  19.2 0.0 copy-done
  19.2 11.9 %all_to_all.34 = f32[16,32,128]{2,1,0:T(8,128)} all-to-all(f32[16,32,128]{2,1,0:T(8,128)S(1)} %bitcast.10), channel_id=1, replica_groups={{0,1,2,3,4,5,6,7,8,9,10,11,12,13,14,15},{16,17,18,19,20,21,22,23,24,25,..., dimensions={0} | all-to-all | bytes 524288 | tf_op jit(solution)/shard_map/all_to_all | solution.py:405
  31.2 3.0 %step.1 = f32[256,128]{1,0:T(8,128)} custom-call(s32[1]{0:T(128)S(6)} %copy.5.refs_0_, s32[4]{0:T(128)} %refs_0_.3, s32[4]{0:T(128)} %refs_2_.1, f32[512,128]{1,0:T(8,128)} %bitcast.7, f32[512,128]{1,0:T(8,128)} %bitcast.6), custom_call_target="tpu_custom_call" | custom-call | tf_op jit(solution)/shard_map/step/pallas_call | solution.py:412
  34.2 9.5 %all_to_all.35 = f32[8,32,128]{2,1,0:T(8,128)} all-to-all(f32[8,32,128]{2,1,0:T(8,128)} %bitcast.9), channel_id=1, replica_groups=mesh['gx'=4,'gy'=8] {'gy'}, dimensions={0} | all-to-all | bytes 262144 | tf_op jit(solution)/shard_map/all_to_all | solution.py:423
  43.7 2.3 %place.1 = f32[8,2,4,508]{3,2,1,0:T(4,128)} custom-call(s32[4]{0:T(128)} %refs_0_.3, f32[256,128]{1,0:T(8,128)} %bitcast.8), custom_call_target="tpu_custom_call" | custom-call | tf_op jit(solution)/shard_map/place/pallas_call | solution.py:424
Async XLA Ops:
  3.5 15.7 %copy-start = (f32[512,128]{1,0:T(8,128)S(1)}, f32[512,128]{1,0:T(8,128)}, u32[]{:S(2)}) copy-start(f32[512,128]{1,0:T(8,128)} %get-tuple-element.7) | copy-start | bytes 786436

commit v2 on v1

--- a/solution.py
+++ b/solution.py
@@ -73,18 +73,18 @@
     return shear, (total - shear) % total
 
 
-def pack_kernel(cells, peers, chunk, shear_ref, state_ref, first_ref, second_ref):
+def pack_kernel(cells, peers, chunk, shear_ref, state_ref, *refs):
+    up_refs, down_refs, own_refs = (refs[i * peers : (i + 1) * peers] for i in range(3))
+    up_ref, down_ref, own_ref = refs[3 * peers :]
     width = chunk + BELOW + ABOVE
     half = width // 2
     rows = state_ref.shape[2]
     place = lax.axis_index("gx")
     places = lax.axis_size("gx")
+    part = lax.axis_index("gy")
     lower, upper = shear_amounts(shear_ref[0], cells, peers)
     up_turn = jnp.where(place == places - 1, lower % cells, 0)
     down_turn = jnp.where(place == 0, upper % cells, 0)
-    odd = place % 2
-    own_first = odd * (peers * SLOT)
-    own_second = (1 - odd) * (peers * SLOT)
 
     def stacked(pieces):
         return jnp.concatenate(pieces, axis=0)
@@ -102,6 +102,10 @@
         top = peers * chunk + ABOVE - cells
         wide = jnp.concatenate([value[:, cells - BELOW :], value, value[:, :top]], axis=1)
         return [wide[:, k * chunk : k * chunk + width] for k in range(peers)]
+
+    def put(ref, row, values):
+        for k, value in enumerate(values):
+            ref[k, row : row + 8, 0 : value.shape[1]] = value
 
     per_group = 8 // SENT
     groups = FIELDS * PLANES // per_group
@@ -110,7 +114,6 @@
         blocks = [state_ref[fz // PLANES, fz % PLANES] for fz in members]
         bottom = stacked([b[:SENT] for b in blocks])
         top = stacked([b[rows - SENT :] for b in blocks])
-        to_up = windows(turned(top, up_turn))
         to_down = windows(turned(bottom, down_turn))
         if group == 0:
             faces = [state_ref[5, z][SENT : SENT + 1] for z in range(PLANES)]
@@ -128,24 +131,15 @@
                 )
                 for value, face in zip(to_down, faces)
             ]
-
-        def put(ref, base, values):
-            for k, value in enumerate(values):
-                at = pl.multiple_of(base + (k * SLOT + group * 8), 8)
-                ref[pl.ds(at, 8), 0 : value.shape[1]] = value
-
-        put(first_ref, own_first, windows(bottom))
-        put(second_ref, own_second, windows(top))
-
-        @pl.when(odd == 0)
-        def _():
-            put(first_ref, own_second, to_up)
-            put(second_ref, own_first, to_down)
-
-        @pl.when(odd == 1)
-        def _():
-            put(first_ref, own_second, to_down)
-            put(second_ref, own_first, to_up)
+        put(up_ref, group * 8, windows(turned(top, up_turn)))
+        put(down_ref, group * 8, to_down)
+        put(own_ref, group * 8, windows(bottom))
+        put(own_ref, SLOT + group * 8, windows(top))
+    for d in range(peers):
+        target = part ^ d
+        up_refs[d][...] = up_ref[target]
+        down_refs[d][...] = down_ref[target]
+        own_refs[d][...] = own_ref[target]
 
 
 def cell_terms(state, next_face_x):
@@ -249,18 +243,15 @@
     return new
 
 
-def step_kernel(
-    cells, peers, chunk, rows,
-    shear_ref, shift_ref, frac_ref, first_ref, second_ref,
-    out_ref, state_ref, mid_ref,
-):
+def step_kernel(cells, peers, chunk, rows, shear_ref, shift_ref, frac_ref, *refs):
+    messages = [refs[i * peers : (i + 1) * peers] for i in range(3)]
+    out_refs = refs[3 * peers : 4 * peers]
+    low_ref, high_ref, own_ref, out_ref, state_ref, mid_ref = refs[4 * peers :]
     width = chunk + BELOW + ABOVE
     half = width // 2
     place = lax.axis_index("gx")
     places = lax.axis_size("gx")
     part = lax.axis_index("gy")
-    odd = place % 2
-    even = odd == 0
     shape = (peers, LANES)
     lane = lane_index(shape)
     lower, upper = shear_amounts(shear_ref[0], cells, peers)
@@ -268,8 +259,14 @@
     upper = jnp.where(place == places - 1, upper, 0)
     column = part * chunk - BELOW + lane
 
-    def load(ref, position, row):
-        return ref[pl.ds(position * (peers * SLOT) + row, peers, stride=SLOT), :]
+    for kind, ref in enumerate((low_ref, high_ref, own_ref)):
+        size = ref.shape[0] // peers
+        for d in range(peers):
+            at = pl.multiple_of((part ^ d) * size, 8)
+            ref[pl.ds(at, size), :] = messages[kind][d][...]
+
+    def load(ref, row):
+        return ref[pl.ds(row, peers, stride=ref.shape[0] // peers), :]
 
     def turn(value, amount):
         return pltpu.roll(value, amount, 0)
@@ -290,25 +287,16 @@
         for z in range(PLANES):
             for g in range(SENT):
                 at = (f * PLANES + z) * SENT + g
-                first = [load(first_ref, p, at) for p in range(2)]
-                second = [load(second_ref, p, at) for p in range(2)]
-                own_low = jnp.where(even, first[0], first[1])
-                own_high = jnp.where(even, second[1], second[0])
-                from_first = jnp.where(even, first[1], first[0])
-                from_second = jnp.where(even, second[0], second[1])
-                ghost_low = jnp.where(even, from_second, from_first)
-                ghost_high = jnp.where(even, from_first, from_second)
-                state_ref[g, f, z] = strips(ghost_low, lower)
-                state_ref[SENT + g, f, z] = own_strips(own_low)
-                state_ref[rows + g, f, z] = own_strips(own_high)
-                state_ref[SENT + rows + g, f, z] = strips(ghost_high, upper)
+                state_ref[g, f, z] = strips(load(low_ref, at), lower)
+                state_ref[SENT + g, f, z] = own_strips(load(own_ref, at))
+                state_ref[rows + g, f, z] = own_strips(load(own_ref, SLOT + at))
+                state_ref[SENT + rows + g, f, z] = strips(load(high_ref, at), upper)
     face_high = []
     for z in range(PLANES):
-        parts = []
-        for g in range(SENT):
-            at = z * SENT + g
-            ghost = jnp.where(even, load(first_ref, 1, at), load(second_ref, 1, at))
-            parts.append(pltpu.roll(ghost, LANES - width + g * half, 1))
+        parts = [
+            pltpu.roll(load(high_ref, z * SENT + g), LANES - width + g * half, 1)
+            for g in range(SENT)
+        ]
         face_high.append(strips(jnp.where(lane < half, parts[0], parts[1]), upper))
 
     def row_of(ref, index):
@@ -353,11 +341,19 @@
             sent = jnp.where(crossing, turn(packed, (hop + 1) % peers), turn(packed, hop % peers))
             out_ref[pl.ds(f * rows + row, peers, stride=FIELDS * rows), :] = sent
         low, here = here, high
-
-
-def place_kernel(cells, peers, chunk, shift_ref, in_ref, out_ref):
+    size = FIELDS * rows
+    for d in range(peers):
+        at = pl.multiple_of((part ^ d) * size, 8)
+        out_refs[d][...] = out_ref[pl.ds(at, size), :]
+
+
+def place_kernel(cells, peers, chunk, shift_ref, *refs):
+    in_refs, out_ref, in_ref = (refs[:peers], refs[peers], refs[peers + 1])
     rows = out_ref.shape[2]
     block = FIELDS * rows
+    part = lax.axis_index("gy")
+    for d in range(peers):
+        in_ref[pl.ds(pl.multiple_of((part ^ d) * block, 8), block), :] = in_refs[d][...]
     per_group = 8 // rows
     amounts = [shift_ref[x] % cells for x in range(rows)]
     lanes = peers * chunk
@@ -380,54 +376,65 @@
 
 def solution(mesh):
     places, peers = (mesh.shape["gx"], mesh.shape["gy"])
-
-    def groups_from(start):
-        return [
-            [(start + pair + p) % places * peers + k for p in range(2) for k in range(peers)]
-            for pair in range(0, places, 2)
-        ]
-
     smem = pl.BlockSpec(memory_space=pltpu.SMEM)
     vmem = pl.BlockSpec(memory_space=pltpu.VMEM)
+
+    def array(*shape):
+        return jax.ShapeDtypeStruct(shape, jnp.float32)
+
+    def scratch(*shape):
+        return pltpu.VMEM(shape, jnp.float32)
+
+    def exchange(message, step, bits):
+        if step == 0 and bits == 0:
+            return message
+        route = [
+            (x * peers + y, (x + step) % places * peers + (y ^ bits))
+            for x in range(places)
+            for y in range(peers)
+        ]
+        return lax.ppermute(message, ("gx", "gy"), route)
 
     def shards(state, shear_offset, remap_shift, frac_index):
         rows, cells = state.shape[2:]
         chunk = -(-cells // peers)
-        message = jax.ShapeDtypeStruct((2 * peers * SLOT, LANES), jnp.float32)
-        first, second = pl.pallas_call(
+        own = FIELDS * PLANES * rows
+        messages = pl.pallas_call(
             lambda *refs: pack_kernel(cells, peers, chunk, *refs),
-            out_shape=(message, message),
+            out_shape=[array(size, LANES) for size in (SLOT, SLOT, own) for d in range(peers)],
             in_specs=[smem, vmem],
-            out_specs=(vmem, vmem),
+            out_specs=[vmem] * (3 * peers),
+            scratch_shapes=[scratch(peers, size, LANES) for size in (SLOT, SLOT, own)],
             name="pack",
         )(shear_offset, state)
-        axes = ("gx", "gy")
-        first = lax.all_to_all(
-            first, axes, 0, 0, axis_index_groups=groups_from(0), tiled=True
-        )
-        second = lax.all_to_all(
-            second, axes, 0, 0, axis_index_groups=groups_from(1), tiled=True
-        )
+        steps = [step for step in (1, -1, 0) for d in range(peers)]
+        bits = list(range(peers)) * 3
+        messages = [exchange(*each) for each in zip(messages, steps, bits)]
         block = FIELDS * rows
         moved = pl.pallas_call(
             lambda *refs: step_kernel(cells, peers, chunk, rows, *refs),
-            out_shape=jax.ShapeDtypeStruct((peers * block, LANES), jnp.float32),
-            in_specs=[smem, smem, smem, vmem, vmem],
-            out_specs=vmem,
+            out_shape=[array(block, LANES) for d in range(peers)],
+            in_specs=[smem] * 3 + [vmem] * (3 * peers),
+            out_specs=[vmem] * peers,
             scratch_shapes=[
-                pltpu.VMEM((rows + 2 * SENT, FIELDS, PLANES, peers, LANES), jnp.float32),
-                pltpu.VMEM((rows + 2, FIELDS, PLANES, peers, LANES), jnp.float32),
+                scratch(peers * SLOT, LANES),
+                scratch(peers * SLOT, LANES),
+                scratch(peers * own, LANES),
+                scratch(peers * block, LANES),
+                scratch(rows + 2 * SENT, FIELDS, PLANES, peers, LANES),
+                scratch(rows + 2, FIELDS, PLANES, peers, LANES),
             ],
             name="step",
-        )(shear_offset, remap_shift, frac_index, first, second)
-        moved = lax.all_to_all(moved, "gy", 0, 0, tiled=True)
+        )(shear_offset, remap_shift, frac_index, *messages)
+        moved = [exchange(message, 0, d) for d, message in enumerate(moved)]
         return pl.pallas_call(
             lambda *refs: place_kernel(cells, peers, chunk, *refs),
-            out_shape=jax.ShapeDtypeStruct(state.shape, jnp.float32),
-            in_specs=[smem, vmem],
+            out_shape=array(*state.shape),
+            in_specs=[smem] + [vmem] * peers,
             out_specs=vmem,
+            scratch_shapes=[scratch(peers * block, LANES)],
             name="place",
-        )(remap_shift, moved)
+        )(remap_shift, *moved)
 
     placed = (P(None, None, "gx", "gy"), P(), P("gx"), P("gx"))
     return jax.shard_map(

time: 46.4 us -> 58.6 us (1.26)
  starting transfers between devices: 0 us -> 41.3 us
  blocking collectives: 37.2 us -> 0 us
  waiting for transfers between devices: 0 us -> 7.29 us
  local copies, waits for them, and re-layouts: 0.01 us -> 1.1 us
    ppermute x0 -> x30, starting transfers between devices: none -> 41.3 us  [exchange(): return lax.ppermute(message, ('gx', 'gy'), route)]
    all_to_all x3 -> x0, blocking collectives: 37.2 us -> none  [the longest x1 15.7 us: shards(): lax.all_to_all(second, axes, 0, 0, axis_index_groups=groups_from(1), tile...]
    ppermute x0 -> x30, waiting for transfers between devices: none -> 7.29 us  [exchange(): return lax.ppermute(message, ('gx', 'gy'), route)]
    unnamed x2 -> x62, local copies, waits for them, and re-layouts: 0.01 us -> 1.1 us
  transfers between devices with their start and end apart: 0 -> 30, of which waited for: 0 -> 7; matrix products, arithmetic and copies ran while one was open for 0% -> 0% of each run, Pallas kernels for 0% -> 0%
where the time goes in v2:
time: 58.6 us; the launch traced here: 58.3 us
  starting transfers between devices  41.3 us (70%)
  Pallas kernels  7.63 us (13%)
  waiting for transfers between devices  7.29 us (12%)
  local copies, waits for them, and re-layouts  1.1 us (2%)
  between operations  0.93 us (2%)
    ppermute x30, starting transfers between devices, exchange(): return lax.ppermute(message, ('gx', 'gy'), route)  41.3 us
    ppermute x30, waiting for transfers between devices, exchange(): return lax.ppermute(message, ('gx', 'gy'), route)  7.29 us
    pallas_call x1, Pallas kernels, shards(): pl.pallas_call(lambda *refs: step_kernel(cells, peers, chunk, rows, *refs...  3.02 us
    pallas_call x1, Pallas kernels, shards(): pl.pallas_call(lambda *refs: pack_kernel(cells, peers, chunk, *refs), out...  2.4 us
    pallas_call x1, Pallas kernels, shards(): pl.pallas_call(lambda *refs: place_kernel(cells, peers, chunk, *refs), ou...  2.21 us
  transfers between devices with their start and end apart: 30, of which 7 were waited for; matrix products, arithmetic and copies ran while one was open for 0% of the time, Pallas kernels for 0%

profile of v2, /device:TPU:0, one launch (start us, length us, event | category | flops | bytes accessed | tf_op | source)
XLA Modules:
  0.0 58.3 jit_solution(16992514964089490048)
XLA Ops:
  0.7 2.4 %pack.1 = (f32[32,128]{1,0:T(8,128)}, f32[32,128]{1,0:T(8,128)}, f32[32,128]{1,0:T(8,128)}, f32[32,128]{1,0:T(8,128)}, f32[32,128]{1,0:T(8,128)}, /*index=5*/f32...) custom-call(s32[1]{0:T(128)S(6)} %copy.5.refs_0_, ...), custom_call_target="tpu_custom_call" | custom-call | tf_op jit(solution)/shard_map/pack/pallas_call | solution.py:402
  3.1 3.1 %collective-permute-start = (f32[32,128]{1,0:T(8,128)}, f32[32,128]{1,0:T(8,128)S(1)}, u32[]{:S(2)}, u32[]{:S(2)}) collective-permute-start(f32[32,128]{1,0:T(8,128)} %get-tuple-element.37), channel_id=1, source_target_pairs={{0,8},{1,9},{2,10},{3,11},{4,12},{5,13},{6,14},{7,15},{8,16},{9,17... | collective-permute-start | bytes 49160 | tf_op jit(solution)/shard_map/ppermute | solution.py:396
  6.1 0.7 %collective-permute-start.1 = (f32[32,128]{1,0:T(8,128)}, f32[32,128]{1,0:T(8,128)S(1)}, u32[]{:S(2)}, u32[]{:S(2)}) collective-permute-start(f32[32,128]{1,0:T(8,128)} %get-tuple-element.38), channel_id=1, source_target_pairs={{0,9},{1,8},{2,11},{3,10},{4,13},{5,12},{6,15},{7,14},{8,17},{9,16... | collective-permute-start | bytes 49160 | tf_op jit(solution)/shard_map/ppermute | solution.py:396
  6.9 2.5 %collective-permute-start.2 = (f32[32,128]{1,0:T(8,128)}, f32[32,128]{1,0:T(8,128)S(1)}, u32[]{:S(2)}, u32[]{:S(2)}) collective-permute-start(f32[32,128]{1,0:T(8,128)} %get-tuple-element.39), channel_id=1, source_target_pairs={{0,10},{1,11},{2,8},{3,9},{4,14},{5,15},{6,12},{7,13},{8,18},{9,19... | collective-permute-start | bytes 49160 | tf_op jit(solution)/shard_map/ppermute | solution.py:396
  9.4 0.6 %collective-permute-start.3 = (f32[32,128]{1,0:T(8,128)}, f32[32,128]{1,0:T(8,128)S(1)}, u32[]{:S(2)}, u32[]{:S(2)}) collective-permute-start(f32[32,128]{1,0:T(8,128)} %get-tuple-element.40), channel_id=1, source_target_pairs={{0,11},{1,10},{2,9},{3,8},{4,15},{5,14},{6,13},{7,12},{8,19},{9,18... | collective-permute-start | bytes 49160 | tf_op jit(solution)/shard_map/ppermute | solution.py:396
  10.0 2.4 %collective-permute-start.4 = (f32[32,128]{1,0:T(8,128)}, f32[32,128]{1,0:T(8,128)S(1)}, u32[]{:S(2)}, u32[]{:S(2)}) collective-permute-start(f32[32,128]{1,0:T(8,128)} %get-tuple-element.41), channel_id=1, source_target_pairs={{0,12},{1,13},{2,14},{3,15},{4,8},{5,9},{6,10},{7,11},{8,20},{9,21... | collective-permute-start | bytes 49160 | tf_op jit(solution)/shard_map/ppermute | solution.py:396
  12.4 0.7 %collective-permute-start.5 = (f32[32,128]{1,0:T(8,128)}, f32[32,128]{1,0:T(8,128)S(1)}, u32[]{:S(2)}, u32[]{:S(2)}) collective-permute-start(f32[32,128]{1,0:T(8,128)} %get-tuple-element.42), channel_id=1, source_target_pairs={{0,13},{1,12},{2,15},{3,14},{4,9},{5,8},{6,11},{7,10},{8,21},{9,20... | collective-permute-start | bytes 49160 | tf_op jit(solution)/shard_map/ppermute | solution.py:396
  13.1 3.5 %collective-permute-start.6 = (f32[32,128]{1,0:T(8,128)}, f32[32,128]{1,0:T(8,128)S(1)}, u32[]{:S(2)}, u32[]{:S(2)}) collective-permute-start(f32[32,128]{1,0:T(8,128)} %get-tuple-element.43), channel_id=1, source_target_pairs={{0,14},{1,15},{2,12},{3,13},{4,10},{5,11},{6,8},{7,9},{8,22},{9,23... | collective-permute-start | bytes 49160 | tf_op jit(solution)/shard_map/ppermute | solution.py:396
  16.5 0.6 %collective-permute-start.7 = (f32[32,128]{1,0:T(8,128)}, f32[32,128]{1,0:T(8,128)S(1)}, u32[]{:S(2)}, u32[]{:S(2)}) collective-permute-start(f32[32,128]{1,0:T(8,128)} %get-tuple-element.44), channel_id=1, source_target_pairs={{0,15},{1,14},{2,13},{3,12},{4,11},{5,10},{6,9},{7,8},{8,23},{9,22... | collective-permute-start | bytes 49160 | tf_op jit(solution)/shard_map/ppermute | solution.py:396
  17.2 3.4 %collective-permute-start.8 = (f32[32,128]{1,0:T(8,128)}, f32[32,128]{1,0:T(8,128)S(1)}, u32[]{:S(2)}, u32[]{:S(2)}) collective-permute-start(f32[32,128]{1,0:T(8,128)} %get-tuple-element.45), channel_id=1, source_target_pairs={{0,24},{1,25},{2,26},{3,27},{4,28},{5,29},{6,30},{7,31},{8,0},{9,1... | collective-permute-start | bytes 49160 | tf_op jit(solution)/shard_map/ppermute | solution.py:396
  20.6 1.4 %collective-permute-start.10 = (f32[32,128]{1,0:T(8,128)}, f32[32,128]{1,0:T(8,128)S(1)}, u32[]{:S(2)}, u32[]{:S(2)}) collective-permute-start(f32[32,128]{1,0:T(8,128)} %get-tuple-element.47), channel_id=1, source_target_pairs={{0,26},{1,27},{2,24},{3,25},{4,30},{5,31},{6,28},{7,29},{8,2},{9,3... | collective-permute-start | bytes 49160 | tf_op jit(solution)/shard_map/ppermute | solution.py:396
  22.5 1.0 %collective-permute-done.7.refs_10_ = f32[32,128]{1,0:T(8,128)S(1)} collective-permute-done((f32[32,128]{1,0:T(8,128)}, f32[32,128]{1,0:T(8,128)S(1)}, u32[]{:S(2)}, u32[]{:S(2)}) %collective-permute-start.7) | collective-permute-done | bytes 16416 | tf_op jit(solution)/shard_map/ppermute | solution.py:396
  23.5 3.3 %collective-permute-start.12 = (f32[32,128]{1,0:T(8,128)}, f32[32,128]{1,0:T(8,128)S(1)}, u32[]{:S(2)}, u32[]{:S(2)}) collective-permute-start(f32[32,128]{1,0:T(8,128)} %get-tuple-element.49), channel_id=1, source_target_pairs={{0,28},{1,29},{2,30},{3,31},{4,24},{5,25},{6,26},{7,27},{8,4},{9,5... | collective-permute-start | bytes 49160 | tf_op jit(solution)/shard_map/ppermute | solution.py:396
  26.9 1.6 %collective-permute-start.17 = (f32[64,128]{1,0:T(8,128)}, f32[64,128]{1,0:T(8,128)S(1)}, u32[]{:S(2)}, u32[]{:S(2)}) collective-permute-start(f32[64,128]{1,0:T(8,128)} %get-tuple-element.55), channel_id=1, source_target_pairs={{0,2},{1,3},{2,0},{3,1},{4,6},{5,7},{6,4},{7,5},{8,10},{9,11},{10,... | collective-permute-start | bytes 98312 | tf_op jit(solution)/shard_map/ppermute | solution.py:396
  28.8 1.2 %collective-permute-start.14 = (f32[32,128]{1,0:T(8,128)}, f32[32,128]{1,0:T(8,128)S(1)}, u32[]{:S(2)}, u32[]{:S(2)}) collective-permute-start(f32[32,128]{1,0:T(8,128)} %get-tuple-element.51), channel_id=1, source_target_pairs={{0,30},{1,31},{2,28},{3,29},{4,26},{5,27},{6,24},{7,25},{8,6},{9,7... | collective-permute-start | bytes 49160 | tf_op jit(solution)/shard_map/ppermute | solution.py:396
  30.0 2.7 %collective-permute-start.15 = (f32[32,128]{1,0:T(8,128)}, f32[32,128]{1,0:T(8,128)S(1)}, u32[]{:S(2)}, u32[]{:S(2)}) collective-permute-start(f32[32,128]{1,0:T(8,128)} %get-tuple-element.52), channel_id=1, source_target_pairs={{0,31},{1,30},{2,29},{3,28},{4,27},{5,26},{6,25},{7,24},{8,7},{9,6... | collective-permute-start | bytes 49160 | tf_op jit(solution)/shard_map/ppermute | solution.py:396
  32.7 2.0 %collective-permute-start.18 = (f32[64,128]{1,0:T(8,128)}, f32[64,128]{1,0:T(8,128)S(1)}, u32[]{:S(2)}, u32[]{:S(2)}) collective-permute-start(f32[64,128]{1,0:T(8,128)} %get-tuple-element.56), channel_id=1, source_target_pairs={{0,3},{1,2},{2,1},{3,0},{4,7},{5,6},{6,5},{7,4},{8,11},{9,10},{10,... | collective-permute-start | bytes 98312 | tf_op jit(solution)/shard_map/ppermute | solution.py:396
  34.7 1.2 %collective-permute-start.19 = (f32[64,128]{1,0:T(8,128)}, f32[64,128]{1,0:T(8,128)S(1)}, u32[]{:S(2)}, u32[]{:S(2)}) collective-permute-start(f32[64,128]{1,0:T(8,128)} %get-tuple-element.57), channel_id=1, source_target_pairs={{0,4},{1,5},{2,6},{3,7},{4,0},{5,1},{6,2},{7,3},{8,12},{9,13},{10,... | collective-permute-start | bytes 98312 | tf_op jit(solution)/shard_map/ppermute | solution.py:396
  36.0 1.9 %collective-permute-start.21 = (f32[64,128]{1,0:T(8,128)}, f32[64,128]{1,0:T(8,128)S(1)}, u32[]{:S(2)}, u32[]{:S(2)}) collective-permute-start(f32[64,128]{1,0:T(8,128)} %get-tuple-element.59), channel_id=1, source_target_pairs={{0,6},{1,7},{2,4},{3,5},{4,2},{5,3},{6,0},{7,1},{8,14},{9,15},{10,... | collective-permute-start | bytes 98312 | tf_op jit(solution)/shard_map/ppermute | solution.py:396
  37.9 1.3 %collective-permute-start.22 = (f32[64,128]{1,0:T(8,128)S(1)}, f32[64,128]{1,0:T(8,128)S(1)}, u32[]{:S(2)}, u32[]{:S(2)}) collective-permute-start(f32[64,128]{1,0:T(8,128)S(1)} %copy-done.30), channel_id=1, source_target_pairs={{0,7},{1,6},{2,5},{3,4},{4,3},{5,2},{6,1},{7,0},{8,15},{9,14},{10,... | collective-permute-start | bytes 98312 | tf_op jit(solution)/shard_map/ppermute | solution.py:396
  39.7 1.6 %collective-permute-done.21.refs_25_ = f32[64,128]{1,0:T(8,128)S(1)} collective-permute-done((f32[64,128]{1,0:T(8,128)}, f32[64,128]{1,0:T(8,128)S(1)}, u32[]{:S(2)}, u32[]{:S(2)}) %collective-permute-start.21) | collective-permute-done | bytes 32800 | tf_op jit(solution)/shard_map/ppermute | solution.py:396
  41.3 0.9 %collective-permute-done.22.refs_26_ = f32[64,128]{1,0:T(8,128)S(1)} collective-permute-done((f32[64,128]{1,0:T(8,128)S(1)}, f32[64,128]{1,0:T(8,128)S(1)}, u32[]{:S(2)}, u32[]{:S(2)}) %collective-permute-start.22) | collective-permute-done | bytes 32800 | tf_op jit(solution)/shard_map/ppermute | solution.py:396
  42.8 3.0 %step.1 = (f32[32,128]{1,0:T(8,128)}, f32[32,128]{1,0:T(8,128)}, f32[32,128]{1,0:T(8,128)}, f32[32,128]{1,0:T(8,128)}, f32[32,128]{1,0:T(8,128)}, /*index=5*/f32...) custom-call(s32[1]{0:T(128)S(6)} %copy.5.refs_0_, s32[4]{0:T(128)} %refs_0_.3, s32[4]{0:T(128)} %refs_2_.1, ...), custom_call_target="tpu_custom_call" | custom-call | tf_op jit(solution)/shard_map/step/pallas_call | solution.py:414
  46.1 1.2 %collective-permute-start.24 = (f32[32,128]{1,0:T(8,128)}, f32[32,128]{1,0:T(8,128)S(1)}, u32[]{:S(2)}, u32[]{:S(2)}) collective-permute-start(f32[32,128]{1,0:T(8,128)} %get-tuple-element.63), channel_id=1, source_target_pairs={{0,2},{1,3},{2,0},{3,1},{4,6},{5,7},{6,4},{7,5},{8,10},{9,11},{10,... | collective-permute-start | bytes 49160 | tf_op jit(solution)/shard_map/ppermute | solution.py:396
  47.8 1.2 %collective-permute-start.26 = (f32[32,128]{1,0:T(8,128)}, f32[32,128]{1,0:T(8,128)S(1)}, u32[]{:S(2)}, u32[]{:S(2)}) collective-permute-start(f32[32,128]{1,0:T(8,128)} %get-tuple-element.65), channel_id=1, source_target_pairs={{0,4},{1,5},{2,6},{3,7},{4,0},{5,1},{6,2},{7,3},{8,12},{9,13},{10,... | collective-permute-start | bytes 49160 | tf_op jit(solution)/shard_map/ppermute | solution.py:396
  49.0 0.6 collective-permute-start.27
  49.6 1.5 %collective-permute-start.28 = (f32[32,128]{1,0:T(8,128)}, f32[32,128]{1,0:T(8,128)S(1)}, u32[]{:S(2)}, u32[]{:S(2)}) collective-permute-start(f32[32,128]{1,0:T(8,128)} %get-tuple-element.67), channel_id=1, source_target_pairs={{0,6},{1,7},{2,4},{3,5},{4,2},{5,3},{6,0},{7,1},{8,14},{9,15},{10,... | collective-permute-start | bytes 49160 | tf_op jit(solution)/shard_map/ppermute | solution.py:396
  51.1 1.1 %collective-permute-start.29 = (f32[32,128]{1,0:T(8,128)}, f32[32,128]{1,0:T(8,128)S(1)}, u32[]{:S(2)}, u32[]{:S(2)}) collective-permute-start(f32[32,128]{1,0:T(8,128)} %get-tuple-element.68), channel_id=1, source_target_pairs={{0,7},{1,6},{2,5},{3,4},{4,3},{5,2},{6,1},{7,0},{8,15},{9,14},{10,... | collective-permute-start | bytes 49160 | tf_op jit(solution)/shard_map/ppermute | solution.py:396
  52.4 2.0 %collective-permute-done.28.refs_7_ = f32[32,128]{1,0:T(8,128)S(1)} collective-permute-done((f32[32,128]{1,0:T(8,128)}, f32[32,128]{1,0:T(8,128)S(1)}, u32[]{:S(2)}, u32[]{:S(2)}) %collective-permute-start.28) | collective-permute-done | bytes 16416 | tf_op jit(solution)/shard_map/ppermute | solution.py:396
  54.4 1.0 %collective-permute-done.29.refs_8_ = f32[32,128]{1,0:T(8,128)S(1)} collective-permute-done((f32[32,128]{1,0:T(8,128)}, f32[32,128]{1,0:T(8,128)S(1)}, u32[]{:S(2)}, u32[]{:S(2)}) %collective-permute-start.29) | collective-permute-done | bytes 16416 | tf_op jit(solution)/shard_map/ppermute | solution.py:396
  55.5 0.6 copy-done.29
  56.1 2.2 %place.1 = f32[8,2,4,508]{3,2,1,0:T(4,128)} custom-call(s32[4]{0:T(128)} %refs_0_.3, f32[32,128]{1,0:T(8,128)} %get-tuple-element.61.refs_1_, f32[32,128]{1,0:T(8,128)} %copy-done.23, f32[32,128]{1,0:T(8,128)} %copy-done.24, f32[32,128]{1,0:T(8,128)} %copy-done.25, f32[32,128]{1,0:T(8,128)} %copy-done.26, f32[32,128]{1,0:T(8,128)} %copy-done.27, ...), custom_call_target="tpu_custom_call" | custom-call | tf_op jit(solution)/shard_map/place/pallas_call | solution.py:430
  (93 shorter events, 2.9 us)
Async XLA Ops:
  3.0 34.9 %copy-start.30 = (f32[64,128]{1,0:T(8,128)S(1)}, f32[64,128]{1,0:T(8,128)}, u32[]{:S(2)}) copy-start(f32[64,128]{1,0:T(8,128)} %get-tuple-element.60) | copy-start | bytes 98308
  3.1 9.3 %collective-permute-start = (f32[32,128]{1,0:T(8,128)}, f32[32,128]{1,0:T(8,128)S(1)}, u32[]{:S(2)}, u32[]{:S(2)}) collective-permute-start(f32[32,128]{1,0:T(8,128)} %get-tuple-element.37), channel_id=1, source_target_pairs={{0,8},{1,9},{2,10},{3,11},{4,12},{5,13},{6,14},{7,15},{8,16},{9,17... | collective-permute-start | bytes 49160 | tf_op jit(solution)/shard_map/ppermute | solution.py:396
  6.1 6.9 %collective-permute-start.1 = (f32[32,128]{1,0:T(8,128)}, f32[32,128]{1,0:T(8,128)S(1)}, u32[]{:S(2)}, u32[]{:S(2)}) collective-permute-start(f32[32,128]{1,0:T(8,128)} %get-tuple-element.38), channel_id=1, source_target_pairs={{0,9},{1,8},{2,11},{3,10},{4,13},{5,12},{6,15},{7,14},{8,17},{9,16... | collective-permute-start | bytes 49160 | tf_op jit(solution)/shard_map/ppermute | solution.py:396
  6.9 9.7 %collective-permute-start.2 = (f32[32,128]{1,0:T(8,128)}, f32[32,128]{1,0:T(8,128)S(1)}, u32[]{:S(2)}, u32[]{:S(2)}) collective-permute-start(f32[32,128]{1,0:T(8,128)} %get-tuple-element.39), channel_id=1, source_target_pairs={{0,10},{1,11},{2,8},{3,9},{4,14},{5,15},{6,12},{7,13},{8,18},{9,19... | collective-permute-start | bytes 49160 | tf_op jit(solution)/shard_map/ppermute | solution.py:396
  9.4 7.8 %collective-permute-start.3 = (f32[32,128]{1,0:T(8,128)}, f32[32,128]{1,0:T(8,128)S(1)}, u32[]{:S(2)}, u32[]{:S(2)}) collective-permute-start(f32[32,128]{1,0:T(8,128)} %get-tuple-element.40), channel_id=1, source_target_pairs={{0,11},{1,10},{2,9},{3,8},{4,15},{5,14},{6,13},{7,12},{8,19},{9,18... | collective-permute-start | bytes 49160 | tf_op jit(solution)/shard_map/ppermute | solution.py:396
  10.0 10.6 %collective-permute-start.4 = (f32[32,128]{1,0:T(8,128)}, f32[32,128]{1,0:T(8,128)S(1)}, u32[]{:S(2)}, u32[]{:S(2)}) collective-permute-start(f32[32,128]{1,0:T(8,128)} %get-tuple-element.41), channel_id=1, source_target_pairs={{0,12},{1,13},{2,14},{3,15},{4,8},{5,9},{6,10},{7,11},{8,20},{9,21... | collective-permute-start | bytes 49160 | tf_op jit(solution)/shard_map/ppermute | solution.py:396
  12.4 8.2 %collective-permute-start.5 = (f32[32,128]{1,0:T(8,128)}, f32[32,128]{1,0:T(8,128)S(1)}, u32[]{:S(2)}, u32[]{:S(2)}) collective-permute-start(f32[32,128]{1,0:T(8,128)} %get-tuple-element.42), channel_id=1, source_target_pairs={{0,13},{1,12},{2,15},{3,14},{4,9},{5,8},{6,11},{7,10},{8,21},{9,20... | collective-permute-start | bytes 49160 | tf_op jit(solution)/shard_map/ppermute | solution.py:396
  13.1 9.0 %collective-permute-start.6 = (f32[32,128]{1,0:T(8,128)}, f32[32,128]{1,0:T(8,128)S(1)}, u32[]{:S(2)}, u32[]{:S(2)}) collective-permute-start(f32[32,128]{1,0:T(8,128)} %get-tuple-element.43), channel_id=1, source_target_pairs={{0,14},{1,15},{2,12},{3,13},{4,10},{5,11},{6,8},{7,9},{8,22},{9,23... | collective-permute-start | bytes 49160 | tf_op jit(solution)/shard_map/ppermute | solution.py:396
  16.5 25.7 %copy-start.9 = (f32[32,128]{1,0:T(8,128)}, f32[32,128]{1,0:T(8,128)S(1)}, u32[]{:S(2)}) copy-start(f32[32,128]{1,0:T(8,128)S(1)} %collective-permute-done.2.refs_5_) | copy-start | bytes 49156
  16.5 7.0 %collective-permute-start.7 = (f32[32,128]{1,0:T(8,128)}, f32[32,128]{1,0:T(8,128)S(1)}, u32[]{:S(2)}, u32[]{:S(2)}) collective-permute-start(f32[32,128]{1,0:T(8,128)} %get-tuple-element.44), channel_id=1, source_target_pairs={{0,15},{1,14},{2,13},{3,12},{4,11},{5,10},{6,9},{7,8},{8,23},{9,22... | collective-permute-start | bytes 49160 | tf_op jit(solution)/shard_map/ppermute | solution.py:396
  17.2 9.7 %collective-permute-start.8 = (f32[32,128]{1,0:T(8,128)}, f32[32,128]{1,0:T(8,128)S(1)}, u32[]{:S(2)}, u32[]{:S(2)}) collective-permute-start(f32[32,128]{1,0:T(8,128)} %get-tuple-element.45), channel_id=1, source_target_pairs={{0,24},{1,25},{2,26},{3,27},{4,28},{5,29},{6,30},{7,31},{8,0},{9,1... | collective-permute-start | bytes 49160 | tf_op jit(solution)/shard_map/ppermute | solution.py:396
  20.6 6.3 %collective-permute-start.9 = (f32[32,128]{1,0:T(8,128)}, f32[32,128]{1,0:T(8,128)S(1)}, u32[]{:S(2)}, u32[]{:S(2)}) collective-permute-start(f32[32,128]{1,0:T(8,128)} %get-tuple-element.46), channel_id=1, source_target_pairs={{0,25},{1,24},{2,27},{3,26},{4,29},{5,28},{6,31},{7,30},{8,1},{9,0... | collective-permute-start | bytes 49160 | tf_op jit(solution)/shard_map/ppermute | solution.py:396
  20.6 7.8 %collective-permute-start.10 = (f32[32,128]{1,0:T(8,128)}, f32[32,128]{1,0:T(8,128)S(1)}, u32[]{:S(2)}, u32[]{:S(2)}) collective-permute-start(f32[32,128]{1,0:T(8,128)} %get-tuple-element.47), channel_id=1, source_target_pairs={{0,26},{1,27},{2,24},{3,25},{4,30},{5,31},{6,28},{7,29},{8,2},{9,3... | collective-permute-start | bytes 49160 | tf_op jit(solution)/shard_map/ppermute | solution.py:396
  22.0 6.8 %collective-permute-start.11 = (f32[32,128]{1,0:T(8,128)}, f32[32,128]{1,0:T(8,128)S(1)}, u32[]{:S(2)}, u32[]{:S(2)}) collective-permute-start(f32[32,128]{1,0:T(8,128)} %get-tuple-element.48), channel_id=1, source_target_pairs={{0,27},{1,26},{2,25},{3,24},{4,31},{5,30},{6,29},{7,28},{8,3},{9,2... | collective-permute-start | bytes 49160 | tf_op jit(solution)/shard_map/ppermute | solution.py:396
  23.5 6.5 %collective-permute-start.12 = (f32[32,128]{1,0:T(8,128)}, f32[32,128]{1,0:T(8,128)S(1)}, u32[]{:S(2)}, u32[]{:S(2)}) collective-permute-start(f32[32,128]{1,0:T(8,128)} %get-tuple-element.49), channel_id=1, source_target_pairs={{0,28},{1,29},{2,30},{3,31},{4,24},{5,25},{6,26},{7,27},{8,4},{9,5... | collective-permute-start | bytes 49160 | tf_op jit(solution)/shard_map/ppermute | solution.py:396
  26.8 9.1 %collective-permute-start.16 = (f32[64,128]{1,0:T(8,128)}, f32[64,128]{1,0:T(8,128)S(1)}, u32[]{:S(2)}, u32[]{:S(2)}) collective-permute-start(f32[64,128]{1,0:T(8,128)} %get-tuple-element.54), channel_id=1, source_target_pairs={{0,1},{1,0},{2,3},{3,2},{4,5},{5,4},{6,7},{7,6},{8,9},{9,8},{10,11... | collective-permute-start | bytes 98312 | tf_op jit(solution)/shard_map/ppermute | solution.py:396
  26.9 11.0 %collective-permute-start.17 = (f32[64,128]{1,0:T(8,128)}, f32[64,128]{1,0:T(8,128)S(1)}, u32[]{:S(2)}, u32[]{:S(2)}) collective-permute-start(f32[64,128]{1,0:T(8,128)} %get-tuple-element.55), channel_id=1, source_target_pairs={{0,2},{1,3},{2,0},{3,1},{4,6},{5,7},{6,4},{7,5},{8,10},{9,11},{10,... | collective-permute-start | bytes 98312 | tf_op jit(solution)/shard_map/ppermute | solution.py:396
  28.4 4.3 %collective-permute-start.13 = (f32[32,128]{1,0:T(8,128)}, f32[32,128]{1,0:T(8,128)S(1)}, u32[]{:S(2)}, u32[]{:S(2)}) collective-permute-start(f32[32,128]{1,0:T(8,128)} %get-tuple-element.50), channel_id=1, source_target_pairs={{0,29},{1,28},{2,31},{3,30},{4,25},{5,24},{6,27},{7,26},{8,5},{9,4... | collective-permute-start | bytes 49160 | tf_op jit(solution)/shard_map/ppermute | solution.py:396
  28.8 5.9 %collective-permute-start.14 = (f32[32,128]{1,0:T(8,128)}, f32[32,128]{1,0:T(8,128)S(1)}, u32[]{:S(2)}, u32[]{:S(2)}) collective-permute-start(f32[32,128]{1,0:T(8,128)} %get-tuple-element.51), channel_id=1, source_target_pairs={{0,30},{1,31},{2,28},{3,29},{4,26},{5,27},{6,24},{7,25},{8,6},{9,7... | collective-permute-start | bytes 49160 | tf_op jit(solution)/shard_map/ppermute | solution.py:396
  30.0 5.9 %collective-permute-start.15 = (f32[32,128]{1,0:T(8,128)}, f32[32,128]{1,0:T(8,128)S(1)}, u32[]{:S(2)}, u32[]{:S(2)}) collective-permute-start(f32[32,128]{1,0:T(8,128)} %get-tuple-element.52), channel_id=1, source_target_pairs={{0,31},{1,30},{2,29},{3,28},{4,27},{5,26},{6,25},{7,24},{8,7},{9,6... | collective-permute-start | bytes 49160 | tf_op jit(solution)/shard_map/ppermute | solution.py:396
  32.7 6.5 %collective-permute-start.18 = (f32[64,128]{1,0:T(8,128)}, f32[64,128]{1,0:T(8,128)S(1)}, u32[]{:S(2)}, u32[]{:S(2)}) collective-permute-start(f32[64,128]{1,0:T(8,128)} %get-tuple-element.56), channel_id=1, source_target_pairs={{0,3},{1,2},{2,1},{3,0},{4,7},{5,6},{6,5},{7,4},{8,11},{9,10},{10,... | collective-permute-start | bytes 98312 | tf_op jit(solution)/shard_map/ppermute | solution.py:396
  34.7 4.6 %collective-permute-start.19 = (f32[64,128]{1,0:T(8,128)}, f32[64,128]{1,0:T(8,128)S(1)}, u32[]{:S(2)}, u32[]{:S(2)}) collective-permute-start(f32[64,128]{1,0:T(8,128)} %get-tuple-element.57), channel_id=1, source_target_pairs={{0,4},{1,5},{2,6},{3,7},{4,0},{5,1},{6,2},{7,3},{8,12},{9,13},{10,... | collective-permute-start | bytes 98312 | tf_op jit(solution)/shard_map/ppermute | solution.py:396
  35.9 3.8 %collective-permute-start.20 = (f32[64,128]{1,0:T(8,128)}, f32[64,128]{1,0:T(8,128)S(1)}, u32[]{:S(2)}, u32[]{:S(2)}) collective-permute-start(f32[64,128]{1,0:T(8,128)} %get-tuple-element.58), channel_id=1, source_target_pairs={{0,5},{1,4},{2,7},{3,6},{4,1},{5,0},{6,3},{7,2},{8,13},{9,12},{10,... | collective-permute-start | bytes 98312 | tf_op jit(solution)/shard_map/ppermute | solution.py:396
  36.0 5.3 %collective-permute-start.21 = (f32[64,128]{1,0:T(8,128)}, f32[64,128]{1,0:T(8,128)S(1)}, u32[]{:S(2)}, u32[]{:S(2)}) collective-permute-start(f32[64,128]{1,0:T(8,128)} %get-tuple-element.59), channel_id=1, source_target_pairs={{0,6},{1,7},{2,4},{3,5},{4,2},{5,3},{6,0},{7,1},{8,14},{9,15},{10,... | collective-permute-start | bytes 98312 | tf_op jit(solution)/shard_map/ppermute | solution.py:396
  37.9 4.3 %collective-permute-start.22 = (f32[64,128]{1,0:T(8,128)S(1)}, f32[64,128]{1,0:T(8,128)S(1)}, u32[]{:S(2)}, u32[]{:S(2)}) collective-permute-start(f32[64,128]{1,0:T(8,128)S(1)} %copy-done.30), channel_id=1, source_target_pairs={{0,7},{1,6},{2,5},{3,4},{4,3},{5,2},{6,1},{7,0},{8,15},{9,14},{10,... | collective-permute-start | bytes 98312 | tf_op jit(solution)/shard_map/ppermute | solution.py:396
  45.9 3.7 %collective-permute-start.23 = (f32[32,128]{1,0:T(8,128)}, f32[32,128]{1,0:T(8,128)S(1)}, u32[]{:S(2)}, u32[]{:S(2)}) collective-permute-start(f32[32,128]{1,0:T(8,128)} %get-tuple-element.62), channel_id=1, source_target_pairs={{0,1},{1,0},{2,3},{3,2},{4,5},{5,4},{6,7},{7,6},{8,9},{9,8},{10,11... | collective-permute-start | bytes 49160 | tf_op jit(solution)/shard_map/ppermute | solution.py:396
  46.1 5.0 %collective-permute-start.24 = (f32[32,128]{1,0:T(8,128)}, f32[32,128]{1,0:T(8,128)S(1)}, u32[]{:S(2)}, u32[]{:S(2)}) collective-permute-start(f32[32,128]{1,0:T(8,128)} %get-tuple-element.63), channel_id=1, source_target_pairs={{0,2},{1,3},{2,0},{3,1},{4,6},{5,7},{6,4},{7,5},{8,10},{9,11},{10,... | collective-permute-start | bytes 49160 | tf_op jit(solution)/shard_map/ppermute | solution.py:396
  47.3 4.9 %collective-permute-start.25 = (f32[32,128]{1,0:T(8,128)}, f32[32,128]{1,0:T(8,128)S(1)}, u32[]{:S(2)}, u32[]{:S(2)}) collective-permute-start(f32[32,128]{1,0:T(8,128)} %get-tuple-element.64), channel_id=1, source_target_pairs={{0,3},{1,2},{2,1},{3,0},{4,7},{5,6},{6,5},{7,4},{8,11},{9,10},{10,... | collective-permute-start | bytes 49160 | tf_op jit(solution)/shard_map/ppermute | solution.py:396
  47.8 4.4 %collective-permute-start.26 = (f32[32,128]{1,0:T(8,128)}, f32[32,128]{1,0:T(8,128)S(1)}, u32[]{:S(2)}, u32[]{:S(2)}) collective-permute-start(f32[32,128]{1,0:T(8,128)} %get-tuple-element.65), channel_id=1, source_target_pairs={{0,4},{1,5},{2,6},{3,7},{4,0},{5,1},{6,2},{7,3},{8,12},{9,13},{10,... | collective-permute-start | bytes 49160 | tf_op jit(solution)/shard_map/ppermute | solution.py:396
  49.0 3.4 %collective-permute-start.27 = (f32[32,128]{1,0:T(8,128)}, f32[32,128]{1,0:T(8,128)S(1)}, u32[]{:S(2)}, u32[]{:S(2)}) collective-permute-start(f32[32,128]{1,0:T(8,128)} %get-tuple-element.66), channel_id=1, source_target_pairs={{0,5},{1,4},{2,7},{3,6},{4,1},{5,0},{6,3},{7,2},{8,13},{9,12},{10,... | collective-permute-start | bytes 49160 | tf_op jit(solution)/shard_map/ppermute | solution.py:396
  49.6 4.8 %collective-permute-start.28 = (f32[32,128]{1,0:T(8,128)}, f32[32,128]{1,0:T(8,128)S(1)}, u32[]{:S(2)}, u32[]{:S(2)}) collective-permute-start(f32[32,128]{1,0:T(8,128)} %get-tuple-element.67), channel_id=1, source_target_pairs={{0,6},{1,7},{2,4},{3,5},{4,2},{5,3},{6,0},{7,1},{8,14},{9,15},{10,... | collective-permute-start | bytes 49160 | tf_op jit(solution)/shard_map/ppermute | solution.py:396
  51.1 4.4 %collective-permute-start.29 = (f32[32,128]{1,0:T(8,128)}, f32[32,128]{1,0:T(8,128)S(1)}, u32[]{:S(2)}, u32[]{:S(2)}) collective-permute-start(f32[32,128]{1,0:T(8,128)} %get-tuple-element.68), channel_id=1, source_target_pairs={{0,7},{1,6},{2,5},{3,4},{4,3},{5,2},{6,1},{7,0},{8,15},{9,14},{10,... | collective-permute-start | bytes 49160 | tf_op jit(solution)/shard_map/ppermute | solution.py:396
  (29 other events, 293.3 us)

commit v3 on v2

--- a/solution.py
+++ b/solution.py
@@ -73,18 +73,15 @@
     return shear, (total - shear) % total
 
 
-def pack_kernel(cells, peers, chunk, shear_ref, state_ref, *refs):
-    up_refs, down_refs, own_refs = (refs[i * peers : (i + 1) * peers] for i in range(3))
-    up_ref, down_ref, own_ref = refs[3 * peers :]
+def pack_kernel(cells, peers, chunk, shear_ref, state_ref, low_ref, high_ref, out_ref):
     width = chunk + BELOW + ABOVE
     half = width // 2
     rows = state_ref.shape[2]
     place = lax.axis_index("gx")
     places = lax.axis_size("gx")
-    part = lax.axis_index("gy")
     lower, upper = shear_amounts(shear_ref[0], cells, peers)
-    up_turn = jnp.where(place == places - 1, lower % cells, 0)
-    down_turn = jnp.where(place == 0, upper % cells, 0)
+    low_turn = jnp.where(place == 0, lower % cells, 0)
+    high_turn = jnp.where(place == places - 1, upper % cells, 0)
 
     def stacked(pieces):
         return jnp.concatenate(pieces, axis=0)
@@ -103,43 +100,31 @@
         wide = jnp.concatenate([value[:, cells - BELOW :], value, value[:, :top]], axis=1)
         return [wide[:, k * chunk : k * chunk + width] for k in range(peers)]
 
-    def put(ref, row, values):
+    def put(row, values):
         for k, value in enumerate(values):
-            ref[k, row : row + 8, 0 : value.shape[1]] = value
+            out_ref[k, row : row + 8, 0 : value.shape[1]] = value
 
     per_group = 8 // SENT
     groups = FIELDS * PLANES // per_group
     for group in range(groups):
-        members = range(group * per_group, (group + 1) * per_group)
-        blocks = [state_ref[fz // PLANES, fz % PLANES] for fz in members]
-        bottom = stacked([b[:SENT] for b in blocks])
-        top = stacked([b[rows - SENT :] for b in blocks])
-        to_down = windows(turned(bottom, down_turn))
+        members = [divmod(m, PLANES) for m in range(group * per_group, (group + 1) * per_group)]
+        blocks = [state_ref[f, z] for f, z in members]
+        put(group * 8, windows(stacked([b[:SENT] for b in blocks])))
+        put(SLOT + group * 8, windows(stacked([b[rows - SENT :] for b in blocks])))
+        low = stacked([low_ref[f, z] for f, z in members])
+        put(2 * SLOT + group * 8, windows(turned(low, low_turn)))
+        blocks = [high_ref[f, z] for f, z in members]
+        high = windows(turned(stacked([b[:SENT] for b in blocks]), high_turn))
         if group == 0:
-            faces = [state_ref[5, z][SENT : SENT + 1] for z in range(PLANES)]
+            faces = [high_ref[5, z][SENT : SENT + 1] for z in range(PLANES)]
             pieces = [faces[i // SENT] for i in range(PLANES * SENT)]
-            faces = windows(turned(stacked(pieces * (8 // len(pieces))), down_turn))
-            to_down = [
-                jnp.concatenate(
-                    [
-                        value,
-                        jnp.where(
-                            row_index((8, half)) % SENT == 0, face[:, :half], face[:, half:]
-                        ),
-                    ],
-                    axis=1,
-                )
-                for value, face in zip(to_down, faces)
+            faces = windows(turned(stacked(pieces * (8 // len(pieces))), high_turn))
+            first = row_index((8, half)) % SENT == 0
+            high = [
+                jnp.concatenate([value, jnp.where(first, face[:, :half], face[:, half:])], axis=1)
+                for value, face in zip(high, faces)
             ]
-        put(up_ref, group * 8, windows(turned(top, up_turn)))
-        put(down_ref, group * 8, to_down)
-        put(own_ref, group * 8, windows(bottom))
-        put(own_ref, SLOT + group * 8, windows(top))
-    for d in range(peers):
-        target = part ^ d
-        up_refs[d][...] = up_ref[target]
-        down_refs[d][...] = down_ref[target]
-        own_refs[d][...] = own_ref[target]
+        put(3 * SLOT + group * 8, high)
 
 
 def cell_terms(state, next_face_x):
@@ -243,10 +228,9 @@
     return new
 
 
-def step_kernel(cells, peers, chunk, rows, shear_ref, shift_ref, frac_ref, *refs):
-    messages = [refs[i * peers : (i + 1) * peers] for i in range(3)]
-    out_refs = refs[3 * peers : 4 * peers]
-    low_ref, high_ref, own_ref, out_ref, state_ref, mid_ref = refs[4 * peers :]
+def step_kernel(
+    cells, peers, chunk, rows, shear_ref, shift_ref, frac_ref, in_ref, out_ref, state_ref, mid_ref
+):
     width = chunk + BELOW + ABOVE
     half = width // 2
     place = lax.axis_index("gx")
@@ -259,14 +243,8 @@
     upper = jnp.where(place == places - 1, upper, 0)
     column = part * chunk - BELOW + lane
 
-    for kind, ref in enumerate((low_ref, high_ref, own_ref)):
-        size = ref.shape[0] // peers
-        for d in range(peers):
-            at = pl.multiple_of((part ^ d) * size, 8)
-            ref[pl.ds(at, size), :] = messages[kind][d][...]
-
-    def load(ref, row):
-        return ref[pl.ds(row, peers, stride=ref.shape[0] // peers), :]
+    def load(row):
+        return in_ref[pl.ds(row, peers, stride=in_ref.shape[0] // peers), :]
 
     def turn(value, amount):
         return pltpu.roll(value, amount, 0)
@@ -287,14 +265,14 @@
         for z in range(PLANES):
             for g in range(SENT):
                 at = (f * PLANES + z) * SENT + g
-                state_ref[g, f, z] = strips(load(low_ref, at), lower)
-                state_ref[SENT + g, f, z] = own_strips(load(own_ref, at))
-                state_ref[rows + g, f, z] = own_strips(load(own_ref, SLOT + at))
-                state_ref[SENT + rows + g, f, z] = strips(load(high_ref, at), upper)
+                state_ref[g, f, z] = strips(load(2 * SLOT + at), lower)
+                state_ref[SENT + g, f, z] = own_strips(load(at))
+                state_ref[rows + g, f, z] = own_strips(load(SLOT + at))
+                state_ref[SENT + rows + g, f, z] = strips(load(3 * SLOT + at), upper)
     face_high = []
     for z in range(PLANES):
         parts = [
-            pltpu.roll(load(high_ref, z * SENT + g), LANES - width + g * half, 1)
+            pltpu.roll(load(3 * SLOT + z * SENT + g), LANES - width + g * half, 1)
             for g in range(SENT)
         ]
         face_high.append(strips(jnp.where(lane < half, parts[0], parts[1]), upper))
@@ -341,25 +319,17 @@
             sent = jnp.where(crossing, turn(packed, (hop + 1) % peers), turn(packed, hop % peers))
             out_ref[pl.ds(f * rows + row, peers, stride=FIELDS * rows), :] = sent
         low, here = here, high
-    size = FIELDS * rows
-    for d in range(peers):
-        at = pl.multiple_of((part ^ d) * size, 8)
-        out_refs[d][...] = out_ref[pl.ds(at, size), :]
-
-
-def place_kernel(cells, peers, chunk, shift_ref, *refs):
-    in_refs, out_ref, in_ref = (refs[:peers], refs[peers], refs[peers + 1])
+
+
+def place_kernel(cells, peers, chunk, shift_ref, in_ref, out_ref):
     rows = out_ref.shape[2]
-    block = FIELDS * rows
     part = lax.axis_index("gy")
-    for d in range(peers):
-        in_ref[pl.ds(pl.multiple_of((part ^ d) * block, 8), block), :] = in_refs[d][...]
     per_group = 8 // rows
     amounts = [shift_ref[x] % cells for x in range(rows)]
     lanes = peers * chunk
     member = row_index((8, LANES)) % rows
     for group in range(FIELDS // per_group):
-        pieces = [in_ref[k * block + group * 8 : k * block + group * 8 + 8, :] for k in range(peers)]
+        pieces = [in_ref[k, part, group * 8 : group * 8 + 8, :] for k in range(peers)]
         for z in range(PLANES):
             joined = jnp.concatenate(
                 [piece[:, z * chunk : (z + 1) * chunk] for piece in pieces], axis=1
@@ -385,56 +355,41 @@
     def scratch(*shape):
         return pltpu.VMEM(shape, jnp.float32)
 
-    def exchange(message, step, bits):
-        if step == 0 and bits == 0:
-            return message
-        route = [
-            (x * peers + y, (x + step) % places * peers + (y ^ bits))
-            for x in range(places)
-            for y in range(peers)
-        ]
-        return lax.ppermute(message, ("gx", "gy"), route)
-
     def shards(state, shear_offset, remap_shift, frac_index):
         rows, cells = state.shape[2:]
         chunk = -(-cells // peers)
-        own = FIELDS * PLANES * rows
-        messages = pl.pallas_call(
+        up = [(x, (x + 1) % places) for x in range(places)]
+        low = lax.ppermute(state[:, :, rows - SENT :], "gx", up)
+        high = lax.ppermute(state[:, :, : SENT + 1], "gx", [(j, i) for i, j in up])
+        size = 2 * SLOT + FIELDS * PLANES * rows
+        message = pl.pallas_call(
             lambda *refs: pack_kernel(cells, peers, chunk, *refs),
-            out_shape=[array(size, LANES) for size in (SLOT, SLOT, own) for d in range(peers)],
-            in_specs=[smem, vmem],
-            out_specs=[vmem] * (3 * peers),
-            scratch_shapes=[scratch(peers, size, LANES) for size in (SLOT, SLOT, own)],
+            out_shape=array(peers, size, LANES),
+            in_specs=[smem] + [vmem] * 3,
+            out_specs=vmem,
             name="pack",
-        )(shear_offset, state)
-        steps = [step for step in (1, -1, 0) for d in range(peers)]
-        bits = list(range(peers)) * 3
-        messages = [exchange(*each) for each in zip(messages, steps, bits)]
+        )(shear_offset, state, low, high)
+        message = lax.all_to_all(message, "gy", 0, 0, tiled=True)
         block = FIELDS * rows
         moved = pl.pallas_call(
             lambda *refs: step_kernel(cells, peers, chunk, rows, *refs),
-            out_shape=[array(block, LANES) for d in range(peers)],
-            in_specs=[smem] * 3 + [vmem] * (3 * peers),
-            out_specs=[vmem] * peers,
+            out_shape=array(peers * block, LANES),
+            in_specs=[smem] * 3 + [vmem],
+            out_specs=vmem,
             scratch_shapes=[
-                scratch(peers * SLOT, LANES),
-                scratch(peers * SLOT, LANES),
-                scratch(peers * own, LANES),
-                scratch(peers * block, LANES),
                 scratch(rows + 2 * SENT, FIELDS, PLANES, peers, LANES),
                 scratch(rows + 2, FIELDS, PLANES, peers, LANES),
             ],
             name="step",
-        )(shear_offset, remap_shift, frac_index, *messages)
-        moved = [exchange(message, 0, d) for d, message in enumerate(moved)]
+        )(shear_offset, remap_shift, frac_index, message.reshape(peers * size, LANES))
+        moved = lax.all_gather(moved, "gy", axis=0)
         return pl.pallas_call(
             lambda *refs: place_kernel(cells, peers, chunk, *refs),
             out_shape=array(*state.shape),
-            in_specs=[smem] + [vmem] * peers,
+            in_specs=[smem, vmem],
             out_specs=vmem,
-            scratch_shapes=[scratch(peers * block, LANES)],
             name="place",
-        )(remap_shift, *moved)
+        )(remap_shift, moved.reshape(peers, peers, block, LANES))
 
     placed = (P(None, None, "gx", "gy"), P(), P("gx"), P("gx"))
     return jax.shard_map(

time: 58.6 us -> 69.1 us (1.18)
  starting transfers between devices: 41.3 us -> 5.11 us
  waiting for transfers between devices: 7.29 us -> 25.4 us
  blocking collectives: 0 us -> 13.9 us
  between operations: 0.93 us -> 14.1 us
  local copies, waits for them, and re-layouts: 1.1 us -> 2.25 us
    ppermute x30 -> x2, starting transfers between devices: 41.3 us -> 5.11 us  [the longest x1 5.05 us: shards(): high = lax.ppermute(state[:, :, :SENT + 1], 'gx', [(j, i) for i, j in up])]
    all_gather x0 -> x1, waiting for transfers between devices: none -> 20 us  [shards(): moved = lax.all_gather(moved, 'gy', axis=0)]
    all_to_all x0 -> x1, blocking collectives: none -> 13.9 us  [shards(): message = lax.all_to_all(message, 'gy', 0, 0, tiled=True)]
    ppermute x30 -> x2, waiting for transfers between devices: 7.29 us -> 5.41 us  [the longest x1 5.4 us: shards(): low = lax.ppermute(state[:, :, rows - SENT:], 'gx', up)]
    slice x0 -> x1, local copies, waits for them, and re-layouts: none -> 0.97 us  [shards(): low = lax.ppermute(state[:, :, rows - SENT:], 'gx', up)]
  transfers between devices with their start and end apart: 30 -> 3, of which waited for: 7 -> 2; matrix products, arithmetic and copies ran while one was open for 0% -> 1% of each run, Pallas kernels for 0% -> 0%
where the time goes in v3:
time: 69.1 us; the launch traced here: 68.9 us
  waiting for transfers between devices  25.4 us (37%)
  between operations  14.1 us (20%)
  blocking collectives  13.9 us (20%)
  Pallas kernels  8.18 us (12%)
  starting transfers between devices  5.11 us (7%)
  local copies, waits for them, and re-layouts  2.25 us (3%)
    all_gather x1, waiting for transfers between devices, shards(): moved = lax.all_gather(moved, 'gy', axis=0)  20 us
    all_to_all x1, blocking collectives, shards(): message = lax.all_to_all(message, 'gy', 0, 0, tiled=True)  13.9 us
    ppermute x1, waiting for transfers between devices, shards(): low = lax.ppermute(state[:, :, rows - SENT:], 'gx', up)  5.4 us
    ppermute x1, starting transfers between devices, shards(): high = lax.ppermute(state[:, :, :SENT + 1], 'gx', [(j, i) for i, j in up])  5.05 us
    pallas_call x1, Pallas kernels, shards(): pl.pallas_call(lambda *refs: step_kernel(cells, peers, chunk, rows, *refs...  2.96 us
    pallas_call x1, Pallas kernels, shards(): pl.pallas_call(lambda *refs: place_kernel(cells, peers, chunk, *refs), ou...  2.65 us
    pallas_call x1, Pallas kernels, shards(): pl.pallas_call(lambda *refs: pack_kernel(cells, peers, chunk, *refs), out...  2.57 us
  transfers between devices with their start and end apart: 3, of which 2 were waited for; matrix products, arithmetic and copies ran while one was open for 1% of the time, Pallas kernels for 0%

profile of v3, /device:TPU:0, one launch (start us, length us, event | category | flops | bytes accessed | tf_op | source)
XLA Modules:
  0.0 68.9 jit_solution(2140001231295616324)
XLA Ops:
  6.5 0.0 all-gather.3.cloned.1.call-start
  6.5 5.0 %collective-permute-start.1 = (f32[8,2,3,508]{3,2,1,0:T(4,128)}, f32[8,2,3,508]{3,2,1,0:T(4,128)S(1)}, u32[]{:S(2)}, u32[]{:S(2)}) collective-permute-start(f32[8,2,3,508]{3,2,1,0:T(4,128)} %bitcast.5), channel_id=1, source_target_pairs={{8,0},{16,8},{24,16},{0,24},{9,1},{17,9},{25,17},{1,25},{10,2},{18... | collective-permute-start | bytes 292616 | tf_op jit(solution)/shard_map/ppermute | solution.py:363
  11.6 1.0 %slice.6 = f32[8,2,2,508]{3,2,1,0:T(2,128)S(1)} slice(f32[8,2,4,508]{3,2,1,0:T(4,128)} %refs_1_.2), slice={[0:8], [0:2], [2:4], [0:508]} | slice | bytes 130048 | tf_op jit(solution)/shard_map/slice | solution.py:362
  12.6 0.1 collective-permute-start
  13.3 5.4 %collective-permute-done.refs_2_ = f32[8,2,2,508]{3,2,1,0:T(2,128)S(1)} collective-permute-done((f32[8,2,2,508]{3,2,1,0:T(2,128)S(1)}, f32[8,2,2,508]{3,2,1,0:T(2,128)S(1)}, u32[]{:S(2)}, u32[]{:S(2)}) %collective-permute-start) | collective-permute-done | bytes 65056 | tf_op jit(solution)/shard_map/ppermute | solution.py:362
  18.7 0.0 copy-start.1
  18.7 0.0 collective-permute-done.1.refs_3_
  18.7 0.6 copy-done.1
  19.3 0.0 copy-start
  19.3 0.7 copy-done
  20.0 2.6 %pack.1 = f32[8,128,128]{2,1,0:T(8,128)} custom-call(s32[1]{0:T(128)S(6)} %copy.5.refs_0_, f32[8,2,4,508]{3,2,1,0:T(4,128)} %refs_1_.2, f32[8,2,2,508]{3,2,1,0:T(2,128)} %copy-done.1, f32[8,2,3,508]{3,2,1,0:T(4,128)} %copy-done), custom_call_target="tpu_custom_call" | custom-call | tf_op jit(solution)/shard_map/pack/pallas_call | solution.py:365
  22.5 13.9 %all_to_all.5 = f32[8,128,128]{2,1,0:T(8,128)} all-to-all(f32[8,128,128]{2,1,0:T(8,128)} %pack.1), channel_id=1, replica_groups=mesh['gx'=4,'gy'=8] {'gy'}, dimensions={0} | all-to-all | bytes 1048576 | tf_op jit(solution)/shard_map/all_to_all | solution.py:372
  36.4 3.0 %step.1 = f32[256,128]{1,0:T(8,128)} custom-call(s32[1]{0:T(128)S(6)} %copy.5.refs_0_, s32[4]{0:T(128)} %refs_0_.3, s32[4]{0:T(128)} %refs_2_.1, f32[1024,128]{1,0:T(8,128)} %bitcast.3), custom_call_target="tpu_custom_call" | custom-call | tf_op jit(solution)/shard_map/step/pallas_call | solution.py:374
  39.4 0.0 all-gather.3.cloned.1.call-update
  39.4 20.0 %all-gather.3.cloned.1.call-done = f32[2048,128]{1,0:T(8,128)} async-done(((f32[256,128]{1,0:T(8,128)}), f32[2048,128]{1,0:T(8,128)}) %all-gather.3.cloned.1.call-update) | async-done | bytes 1048592 | tf_op jit(solution)/shard_map/all_gather | solution.py:385
  59.4 2.7 %place.1 = f32[8,2,4,508]{3,2,1,0:T(4,128)} custom-call(s32[4]{0:T(128)} %refs_0_.3, f32[8,8,32,128]{3,2,1,0:T(8,128)} %bitcast.4), custom_call_target="tpu_custom_call" | custom-call | tf_op jit(solution)/shard_map/place/pallas_call | solution.py:386
Async XLA Ops:
  6.5 52.8 %all-gather.3.cloned.1.call-start = ((), (), s32[]{:S(2)}) async-start(), calls=%async_computation.1 | async-start | bytes 1179648 | tf_op jit(solution)/shard_map/all_gather | solution.py:385
  6.5 12.1 %collective-permute-start.1 = (f32[8,2,3,508]{3,2,1,0:T(4,128)}, f32[8,2,3,508]{3,2,1,0:T(4,128)S(1)}, u32[]{:S(2)}, u32[]{:S(2)}) collective-permute-start(f32[8,2,3,508]{3,2,1,0:T(4,128)} %bitcast.5), channel_id=1, source_target_pairs={{8,0},{16,8},{24,16},{0,24},{9,1},{17,9},{25,17},{1,25},{10,2},{18... | collective-permute-start | bytes 292616 | tf_op jit(solution)/shard_map/ppermute | solution.py:363
  12.6 6.1 %collective-permute-start = (f32[8,2,2,508]{3,2,1,0:T(2,128)S(1)}, f32[8,2,2,508]{3,2,1,0:T(2,128)S(1)}, u32[]{:S(2)}, u32[]{:S(2)}) collective-permute-start(f32[8,2,2,508]{3,2,1,0:T(2,128)S(1)} %slice.6), channel_id=1, source_target_pairs={{0,8},{8,16},{16,24},{24,0},{1,9},{9,17},{17,25},{25,1},{2,10},{10... | collective-permute-start | bytes 195080 | tf_op jit(solution)/shard_map/ppermute | solution.py:362
  18.7 0.6 copy-start.1
  19.3 0.7 copy-start
Sparse Core Ops, SparseCore 0:
  39.5 19.8 all-gather.2

commit v4 on v0

v4 whole, which is shorter than its diff:
```python
import jax
import jax.numpy as jnp
from jax import lax
from jax.experimental import pallas as pl
from jax.experimental.pallas import tpu as pltpu
from jax.sharding import PartitionSpec as P

FRAC = 16

ADIABATIC = 5.0 / 3.0
ROTATION = 1.0
SHEAR_RATE = 1.5
MAX_SPEED = 5.0
TIME_STEP = 0.05

LANES = 128
SUBLANES = 8
FIELDS = 8
PLANES = 2
FACE_X = 5
BELOW = 3
ABOVE = 3
SENT = 2
HALF_STEP = 0.5 * TIME_STEP
DIFFUSE = 0.5 * MAX_SPEED * TIME_STEP
EDGE = 0.25 * TIME_STEP


def lane_index():
    return lax.broadcasted_iota(jnp.int32, (SUBLANES, LANES), 1)


def row_index():
    return lax.broadcasted_iota(jnp.int32, (SUBLANES, LANES), 0)


def turn_lanes(value, amount):
    return pltpu.roll(value, amount, 1)


def turn_rows(value, amount):
    amount %= SUBLANES
    return pltpu.roll(value, amount, 0) if amount else value


def radial_next(value):
    return turn_rows(value, -1)


def radial_prev(value):
    return turn_rows(value, 1)


def tiles_for(columns):
    return -(-columns // LANES)


def plan(shear, cells, peers):
    rest = shear % cells
    middle = cells // 2
    near = (rest >= middle - 5) & (rest <= middle + 5)
    own = jnp.where(near, middle - 12, middle)
    up = (own - shear) % cells
    down = (own + shear) % cells
    up_hop = (shear - own + up) // cells
    down_hop = (shear + own) // cells
    return own, up, down, up_hop, down_hop


def pair_kernel(cells, peers, shear_ref, state_ref, below_ref, joined_ref, up_ref, down_ref):
    place = lax.axis_index("gx")
    places = lax.axis_size("gx")
    own, up, down, _, _ = plan(shear_ref[0], cells, peers)
    up = jnp.where(place == places - 1, up, own)
    down = jnp.where(place == 0, down, own)
    lane = lane_index()
    row = row_index()
    single = tiles_for(cells)
    gap = cells % LANES
    double = joined_ref.shape[1]
    window = up_ref.shape[1]

    def tiles_of(ref, f):
        both = [ref[f, z] for z in range(PLANES)]
        value = jnp.concatenate(both, axis=0)
        return [value[:, i * LANES : min((i + 1) * LANES, cells)] for i in range(single)]

    def widened(tile):
        spare = LANES - tile.shape[1]
        if spare == 0:
            return tile
        return jnp.concatenate([tile, jnp.zeros((SUBLANES, spare), tile.dtype)], axis=1)

    for f in range(FIELDS):
        lower = [widened(t) for t in tiles_of(below_ref, f)]
        upper = [turn_lanes(widened(t), gap) for t in tiles_of(state_ref, f)]
        for i in range(single):
            if i < single - 1:
                joined_ref[f, i] = lower[i]
            else:
                joined_ref[f, i] = jnp.where(lane < gap, lower[i], upper[0])
        for i in range(single, double):
            k = i - single
            joined_ref[f, i] = jnp.where(lane < gap, upper[k], upper[min(k + 1, single - 1)])

    def cut(f, start):
        return cut_window(joined_ref, f, start, window)

    late = row % 4 >= SENT
    for pair in range(FIELDS // 2):
        ups = [cut(2 * pair + i, up) for i in range(2)]
        downs = [cut(2 * pair + i, down) for i in range(2)]
        for t in range(window):
            up_ref[pair, t] = jnp.where(late, ups[0][t], turn_rows(ups[1][t], -SENT))
            down_ref[pair, t] = jnp.where(late, turn_rows(downs[1][t], SENT), downs[0][t])
    for t, value in enumerate(cut(FACE_X, down)):
        down_ref[FIELDS // 2, t] = value


def cut_window(joined_ref, f, start, count):
    whole = start // LANES
    part = start % LANES
    last = joined_ref.shape[1] - 1
    tiles = [joined_ref[f, jnp.minimum(whole + t, last)] for t in range(count + 1)]
    turned = [turn_lanes(tile, (LANES - part) % LANES) for tile in tiles]
    here = lane_index() < LANES - part
    return [jnp.where(here, turned[t], turned[t + 1]) for t in range(count)]


def cell_terms(state, next_face_x, next_face_y):
    planes = range(PLANES)
    face_z = state[7]
    out = []
    for z in planes:
        density, mom_x, mom_y, mom_z, energy, face_x, face_y = (state[f][z] for f in range(7))
        cen_x = 0.5 * (face_x + next_face_x[z])
        cen_y = 0.5 * (face_y + next_face_y[z])
        cen_z = 0.5 * (face_z[z] + face_z[(z + 1) % PLANES])
        inverse = 1.0 / density
        vel_x, vel_y, vel_z = (mom_x * inverse, mom_y * inverse, mom_z * inverse)
        magnetic = 0.5 * (cen_x * cen_x + cen_y * cen_y + cen_z * cen_z)
        kinetic = 0.5 * (mom_x * vel_x + mom_y * vel_y + mom_z * vel_z)
        pressure = (ADIABATIC - 1.0) * (energy - kinetic - magnetic) + magnetic
        vel_dot = vel_x * cen_x + vel_y * cen_y + vel_z * cen_z
        scaled_p = HALF_STEP * pressure
        total = energy + pressure
        sv_x, sv_y, sv_z = (HALF_STEP * vel_x, HALF_STEP * vel_y, HALF_STEP * vel_z)
        sb_x, sb_y, sb_z = (HALF_STEP * cen_x, HALF_STEP * cen_y, HALF_STEP * cen_z)
        xx = mom_x * sv_x - cen_x * sb_x + scaled_p
        yy = mom_y * sv_y - cen_y * sb_y + scaled_p
        zz = mom_z * sv_z - cen_z * sb_z + scaled_p
        xy = mom_x * sv_y - cen_x * sb_y
        xz = mom_x * sv_z - cen_x * sb_z
        yz = mom_y * sv_z - cen_y * sb_z
        diffuse = [DIFFUSE * state[f][z] for f in range(5)]
        flux_x = [HALF_STEP * mom_x, xx, xy, xz, total * sv_x - sb_x * vel_dot]
        flux_y = [HALF_STEP * mom_y, xy, yy, yz, total * sv_y - sb_y * vel_dot]
        flux_z = [HALF_STEP * mom_z, xz, yz, zz, total * sv_z - sb_z * vel_dot]
        e_z = EDGE * (vel_y * cen_x - vel_x * cen_y)
        pair = e_z + radial_prev(e_z)
        out.append(
            dict(
                diffuse=diffuse,
                along_x=[
                    radial_next(f - d) - radial_prev(f + d) for f, d in zip(flux_x, diffuse)
                ],
                low_y=[turn_lanes(f + d, 1) for f, d in zip(flux_y, diffuse)],
                high_y=[turn_lanes(f - d, LANES - 1) for f, d in zip(flux_y, diffuse)],
                flux_z=flux_z,
                shear=xy,
                e_x=EDGE * (vel_z * cen_y - vel_y * cen_z),
                e_y=EDGE * (vel_x * cen_z - vel_z * cen_x),
                pair=pair,
                low_pair=turn_lanes(pair, 1),
                high_pair=turn_lanes(pair, LANES - 1),
            )
        )
    e_x, e_y = (
        [sum((cell[name] for cell in out[1:]), out[0][name]) for name in ("e_x", "e_y")]
    )
    shared = dict(
        e_x=e_x,
        low_e_x=turn_lanes(e_x, 1),
        high_e_x=turn_lanes(e_x, LANES - 1),
        edge_y=[e_y + radial_prev(e_y)] * PLANES,
        along_x=radial_next(e_y) - radial_prev(e_y),
    )
    return out, shared


def tile_step(state, low, here, high):
    lane = lane_index()
    cells_low, shared_low = low
    cells, shared = here
    cells_high, shared_high = high

    def before(turned_low, turned):
        return jnp.where(lane > 0, turned, turned_low)

    def after(turned, turned_high):
        return jnp.where(lane < LANES - 1, turned, turned_high)

    new = [[None] * PLANES for f in range(FIELDS)]
    faces = [
        [
            (cells[z - 1]["flux_z"][f] + cells[z]["flux_z"][f])
            - (cells[z]["diffuse"][f] - cells[z - 1]["diffuse"][f])
            for f in range(5)
        ]
        for z in range(PLANES)
    ]
    low_e_x = before(shared_low["low_e_x"], shared["low_e_x"])
    along_y = after(shared["high_e_x"], shared_high["high_e_x"]) - low_e_x
    edge_x = [shared["e_x"] + low_e_x] * PLANES
    edge_y = shared["edge_y"]
    for z in range(PLANES):
        cell = cells[z]
        up = (z + 1) % PLANES
        for f in range(5):
            high_y = after(cell["high_y"][f], cells_high[z]["high_y"][f])
            low_y = before(cells_low[z]["low_y"][f], cell["low_y"][f])
            along_z = faces[up][f] - faces[z][f]
            kept = state[f][z] - 4.0 * cell["diffuse"][f]
            new[f][z] = kept - (cell["along_x"][f] + (high_y - low_y) + along_z)
        mom_x, mom_y = (state[1][z], state[2][z])
        new[1][z] = new[1][z] + (TIME_STEP * 2.0 * ROTATION) * mom_y
        new[2][z] = new[2][z] - (TIME_STEP * (2.0 - SHEAR_RATE) * ROTATION) * mom_x
        new[4][z] = new[4][z] + (2.0 * SHEAR_RATE * ROTATION) * cell["shear"]
        low_pair = before(cells_low[z]["low_pair"], cell["low_pair"])
        high_pair = after(cell["high_pair"], cells_high[z]["high_pair"])
        edge_z = cell["pair"] + low_pair
        new[5][z] = state[5][z] + ((edge_y[up] - edge_y[z]) - (high_pair - low_pair))
        new[6][z] = state[6][z] + ((radial_next(edge_z) - edge_z) - (edge_x[up] - edge_x[z]))
        new[7][z] = state[7][z] + (along_y - shared["along_x"])
    return new


def step_kernel(
    cells, peers, rows,
    shear_ref, frac_ref, joined_ref, up_ref, down_ref, out_ref, state_ref, mid_ref,
):
    own = plan(shear_ref[0], cells, peers)[0]
    lane = lane_index()
    row = row_index()
    window = up_ref.shape[1]
    single = tiles_for(cells)

    for f in range(FIELDS):
        pair, second = divmod(f, 2)
        for t, tile in enumerate(cut_window(joined_ref, f, own, window)):
            up = up_ref[pair, t]
            down = down_ref[pair, t]
            for z in range(PLANES):
                up_at = z * 4 + (0 if second else SENT)
                down_at = z * 4 + (SENT if second else 0)
                value = turn_rows(tile, -z * 4)
                value = jnp.where(row < rows, value, turn_rows(down, rows - down_at))
                value = jnp.where(row < rows + SENT, value, turn_rows(up, rows + SENT - up_at))
                state_ref[t, f, z] = value
    last = rows + SENT - 1

    def faces_beyond(t, face_x):
        beyond = down_ref[FIELDS // 2, t]
        return [
            jnp.where(row == last, turn_rows(beyond, last - (z * 4 + SENT)), radial_next(face_x[z]))
            for z in range(PLANES)
        ]

    def terms(ref, t, count, beyond):
        state = [[ref[t, f, z] for z in range(PLANES)] for f in range(FIELDS)]
        if beyond:
            next_face_x = faces_beyond(t, state[FACE_X])
        else:
            next_face_x = [radial_next(face) for face in state[FACE_X]]
        next_face_y = []
        for z in range(PLANES):
            here = turn_lanes(state[6][z], LANES - 1)
            if t + 1 < count:
                there = turn_lanes(ref[t + 1, 6, z], LANES - 1)
                here = jnp.where(lane < LANES - 1, here, there)
            next_face_y.append(here)
        return state, cell_terms(state, next_face_x, next_face_y)

    low = here = terms(state_ref, 0, window, True)
    for t in range(window):
        high = terms(state_ref, t + 1, window, True) if t + 1 < window else here
        new = tile_step(here[0], low[1], here[1], high[1])
        for f in range(FIELDS):
            for z in range(PLANES):
                if t < single or f == 6:
                    mid_ref[t, f, z] = new[f][z]
        low, here = here, high

    weight = jnp.zeros((SUBLANES, LANES), jnp.float32)
    for x in range(rows):
        level = (frac_ref[x].astype(jnp.float32) + 0.5) / FRAC
        weight = jnp.where(row == x, level, weight)
    keep = 1.0 - weight
    low = here = terms(mid_ref, 0, window, False)
    low_done = None
    low_moved = None

    def emit(t, moved):
        for f in range(FIELDS):
            out_ref[f, t] = moved[f]

    for t in range(single):
        high = terms(mid_ref, t + 1, window, False) if t + 1 < single else here
        new = tile_step(here[0], low[1], here[1], high[1])
        done = []
        moved = []
        for f in range(FIELDS):
            mixed = []
            turned = []
            for z in range(PLANES):
                value = 0.5 * (state_ref[t, f, z] + new[f][z])
                below = turn_lanes(value, 1)
                turned.append(below)
                if t:
                    below = jnp.where(lane > 0, below, low_done[f][z])
                mixed.append(keep * value + weight * below)
            done.append(turned)
            both = jnp.where(row < rows, mixed[0], turn_rows(mixed[1], 4))
            moved.append(turn_lanes(both, LANES - BELOW))
        if t:
            emit(
                t - 1,
                [jnp.where(lane < LANES - BELOW, a, b) for a, b in zip(low_moved, moved)],
            )
        low_done, low_moved = done, moved
        low, here = here, high
    emit(single - 1, low_moved)


def row_sources(shift, own, cells, peers, target):
    total = cells * peers
    offset = cells - BELOW - own
    shift = (shift + total - offset) % total
    hop = shift // cells
    rest = shift % cells
    upper = (target + 2 * peers - hop) % peers
    lower = (target + 2 * peers - hop - 1) % peers
    return upper, lower, rest


def turned_rows(cells, peers, rows, shift_ref, own, part, target, block_ref, out_ref):
    row = row_index()
    lane = lane_index()
    count = out_ref.shape[1]
    spare = count * LANES - cells
    plans = []
    for x in range(rows):
        upper, lower, rest = row_sources(shift_ref[x], own, cells, peers, target)
        first = upper % 2 == part % 2
        block = jnp.where(first, upper, lower) // 2
        amount = jnp.where(first, rest, rest + spare)
        plans.append((block, amount // LANES, amount % LANES))
    for f in range(FIELDS):
        result = None
        for x, (block, whole, fine) in enumerate(plans):
            tiles = [block_ref[block, f, (t + count - whole) % count] for t in range(count)]
            tiles = [turn_lanes(tile, fine) for tile in tiles]
            tiles = [jnp.where(lane < fine, tiles[t - 1], tiles[t]) for t in range(count)]
            if x == 0:
                result = tiles
            else:
                result = [jnp.where(row % rows == x, a, b) for a, b in zip(tiles, result)]
        for t in range(count):
            out_ref[f, t] = result[t]


def gather_kernel(cells, peers, rows, shear_ref, shift_ref, *refs):
    in_refs, block_ref, out_ref = (refs[:-2], refs[-2], refs[-1])
    part = lax.axis_index("gy")
    own = plan(shear_ref[0], cells, peers)[0]
    for i, ref in enumerate(in_refs):
        block_ref[(part // 2) ^ i] = ref[...]
    turned_rows(cells, peers, rows, shift_ref, own, part, part ^ 1, block_ref, out_ref)


def keep_kernel(cells, peers, rows, shear_ref, shift_ref, block_ref, out_ref):
    part = lax.axis_index("gy")
    own = plan(shear_ref[0], cells, peers)[0]
    turned_rows(cells, peers, rows, shift_ref, own, part, part, block_ref, out_ref)


def merge_kernel(cells, peers, rows, shear_ref, shift_ref, mine_ref, other_ref, out_ref):
    part = lax.axis_index("gy")
    own = plan(shear_ref[0], cells, peers)[0]
    row = row_index() % rows
    lane = lane_index()
    count = mine_ref.shape[1]
    border = jnp.zeros((SUBLANES, LANES), jnp.int32)
    first = jnp.zeros((SUBLANES, LANES), jnp.int32)
    for x in range(rows):
        upper, _, rest = row_sources(shift_ref[x], own, cells, peers, part)
        border = jnp.where(row == x, rest, border)
        first = jnp.where(row == x, (upper + part + 1) % 2, first)
    masks = [(lane + t * LANES >= border) == (first == 1) for t in range(count)]
    for f in range(FIELDS):
        tiles = [jnp.where(masks[t], mine_ref[f, t], other_ref[f, t]) for t in range(count)]
        value = jnp.concatenate(tiles, axis=1)[:, :cells]
        for z in range(PLANES):
            out_ref[f, z] = value[z * rows : (z + 1) * rows]


def solution(mesh):
    places, peers = (mesh.shape["gx"], mesh.shape["gy"])
    smem = pl.BlockSpec(memory_space=pltpu.SMEM)
    vmem = pl.BlockSpec(memory_space=pltpu.VMEM)
    axes = ("gx", "gy")

    def array(*shape):
        return jax.ShapeDtypeStruct(shape + (SUBLANES, LANES), jnp.float32)

    def scratch(*shape):
        return pltpu.VMEM(shape + (SUBLANES, LANES), jnp.float32)

    def device(x, y):
        return x % places * peers + y % peers

    devices = [(x, y) for x in range(places) for y in range(peers)]

    def ghosts(up_hop, down_hop, up, down):
        rise = [(device(x, y), device(x + 1, y + up_hop * (x == places - 1))) for x, y in devices]
        fall = [(device(x, y), device(x - 1, y - down_hop * (x == 0))) for x, y in devices]
        return lax.ppermute(up, axes, rise), lax.ppermute(down, axes, fall)

    def shards(state, shear_offset, remap_shift, frac_index):
        rows, cells = state.shape[2:]
        single = tiles_for(cells)
        double = tiles_for(2 * cells)
        window = tiles_for(BELOW + cells + ABOVE)
        below = lax.ppermute(state, "gy", [(i, (i + 1) % peers) for i in range(peers)])
        joined, up, down = pl.pallas_call(
            lambda *refs: pair_kernel(cells, peers, *refs),
            out_shape=[
                array(FIELDS, double),
                array(FIELDS // 2, window),
                array(FIELDS // 2 + 1, window),
            ],
            in_specs=[smem, vmem, vmem],
            out_specs=[vmem] * 3,
            name="pair",
        )(shear_offset, state, below)
        _, _, _, up_hop, down_hop = plan(shear_offset[0], cells, peers)
        branches = [
            lambda u, d, i=i: ghosts(i // 2 + i % 2, i // 2, u, d) for i in range(2 * peers)
        ]
        which = (2 * down_hop + (up_hop - down_hop)) % (2 * peers)
        up, down = lax.switch(which, branches, up, down)
        block = pl.pallas_call(
            lambda *refs: step_kernel(cells, peers, rows, *refs),
            out_shape=array(FIELDS, single),
            in_specs=[smem] * 2 + [vmem] * 3,
            out_specs=vmem,
            scratch_shapes=[scratch(window, FIELDS, PLANES)] * 2,
            name="step",
        )(shear_offset, frac_index, joined, up, down)

        def exchange(value, bits):
            return lax.ppermute(value, "gy", [(i, i ^ bits) for i in range(peers)])

        blocks = [block] + [exchange(block, bits) for bits in range(2, peers, 2)]
        blocks, other = pl.pallas_call(
            lambda *refs: gather_kernel(cells, peers, rows, *refs),
            out_shape=[array(peers // 2, FIELDS, single), array(FIELDS, single)],
            in_specs=[smem] * 2 + [vmem] * (peers // 2),
            out_specs=[vmem] * 2,
            name="gather",
        )(shear_offset, remap_shift, *blocks)
        other = exchange(other, 1)
        mine = pl.pallas_call(
            lambda *refs: keep_kernel(cells, peers, rows, *refs),
            out_shape=array(FIELDS, single),
            in_specs=[smem] * 2 + [vmem],
            out_specs=vmem,
            name="keep",
        )(shear_offset, remap_shift, blocks)
        return pl.pallas_call(
            lambda *refs: merge_kernel(cells, peers, rows, *refs),
            out_shape=jax.ShapeDtypeStruct(state.shape, jnp.float32),
            in_specs=[smem] * 2 + [vmem] * 2,
            out_specs=vmem,
            name="merge",
        )(shear_offset, remap_shift, mine, other)

    placed = (P(None, None, "gx", "gy"), P(), P("gx"), P("gx"))
    return jax.shard_map(
        shards, mesh=mesh, in_specs=placed, out_specs=P(None, None, "gx", "gy"), check_vma=False
    )
```

time: 80.9 us -> 39 us (0.48); the launches traced: 80.3 us -> 39.5 us
  waiting for transfers between devices: 42.2 us -> 17.7 us
  Pallas kernels: 0 us -> 10.4 us
  other arithmetic: 10.1 us -> 0 us
  between operations: 9.67 us -> 0.78 us
  local copies, waits for them, and re-layouts: 6.48 us -> 2.58 us
  starting transfers between devices: 11.8 us -> 7.93 us
    ppermute x16 -> x7, waiting for transfers between devices: 42.2 us -> 17.7 us  [the longest x2 6.67 us: ghosts(): return (lax.ppermute(up, axes, rise), lax.ppermute(down, axes, fall))]
    pallas_call x0 -> x5, Pallas kernels: none -> 10.4 us  [the longest x1 2.61 us: shards(): pl.pallas_call(lambda *refs: step_kernel(cells, peers, rows, *refs), out_...]
    ppermute x16 -> x7, starting transfers between devices: 11.8 us -> 7.93 us  [the longest x4 4.22 us: exchange(): return lax.ppermute(value, 'gy', [(i, i ^ bits) for i in range(peers)])]
    concatenate x166 -> x0, local copies, waits for them, and re-layouts: 3.72 us -> none  [the longest x92 2.27 us: prev_cell(): return jnp.roll(value, 1, grid_axis)]
    another operation x7 -> x0, other arithmetic: 2.96 us -> none  [the longest x5 2.78 us: shards(): return jnp.stack(outputs, axis=2)]
    unnamed x6 -> x10, local copies, waits for them, and re-layouts: 0.1 us -> 2.58 us
    unnamed x14 -> x0, other arithmetic: 2.04 us -> none
    slice x8 -> x0, local copies, waits for them, and re-layouts: 1.82 us -> none  [the longest x1 0.64 us: shards(): start = cells - 1 - remainders[row_pos]]
  transfers between devices with their start and end apart: 16 -> 7, of which waited for: 14 -> 4; matrix products, arithmetic and copies ran while one was open for 2% -> 0% of each run, Pallas kernels for 0% -> 5%
where the time goes in v4:
time: 39 us; the launch traced here: 39.5 us
  waiting for transfers between devices  17.7 us (45%)
  Pallas kernels  10.4 us (27%)
  starting transfers between devices  7.93 us (20%)
  local copies, waits for them, and re-layouts  2.58 us (7%)
  between operations  0.78 us (2%)
    ppermute x2, waiting for transfers between devices, ghosts(): return (lax.ppermute(up, axes, rise), lax.ppermute(down, axes, fall))  6.67 us
    ppermute x4, waiting for transfers between devices, exchange(): return lax.ppermute(value, 'gy', [(i, i ^ bits) for i in range(peers)])  6.1 us
    ppermute x1, waiting for transfers between devices, shards(): lax.ppermute(state, 'gy', [(i, (i + 1) % peers) for i in range(peers)])  4.98 us
    ppermute x4, starting transfers between devices, exchange(): return lax.ppermute(value, 'gy', [(i, i ^ bits) for i in range(peers)])  4.22 us
    ppermute x2, starting transfers between devices, ghosts(): return (lax.ppermute(up, axes, rise), lax.ppermute(down, axes, fall))  3.26 us
    pallas_call x1, Pallas kernels, shards(): pl.pallas_call(lambda *refs: step_kernel(cells, peers, rows, *refs), out_...  2.61 us
    unnamed x10, local copies, waits for them, and re-layouts  2.58 us
    pallas_call x1, Pallas kernels, shards(): pl.pallas_call(lambda *refs: gather_kernel(cells, peers, rows, *refs), ou...  2.24 us
  transfers between devices with their start and end apart: 7, of which 4 were waited for; matrix products, arithmetic and copies ran while one was open for 0% of the time, Pallas kernels for 5%

profile of v4, /device:TPU:0, one launch (start us, length us, event | category | flops | bytes accessed | tf_op | source)
XLA Modules:
  0.0 39.5 jit_solution(16313944652102623984)
XLA Ops:
  0.0 0.5 %collective-permute-start.32 = (f32[8,2,4,508]{3,2,1,0:T(4,128)}, f32[8,2,4,508]{3,2,1,0:T(4,128)S(1)}, u32[]{:S(2)}, u32[]{:S(2)}) collective-permute-start(f32[8,2,4,508]{3,2,1,0:T(4,128)} %refs_1_.5), channel_id=1, source_target_pairs={{0,1},{1,2},{2,3},{3,4},{4,5},{5,6},{6,7},{7,0},{8,9},{9,10},{10,1... | collective-permute-start | bytes 390152 | tf_op jit(solution)/shard_map/ppermute | solution.py:434
  1.2 5.0 %collective-permute-done.32.refs_2_ = f32[8,2,4,508]{3,2,1,0:T(4,128)S(1)} collective-permute-done((f32[8,2,4,508]{3,2,1,0:T(4,128)}, f32[8,2,4,508]{3,2,1,0:T(4,128)S(1)}, u32[]{:S(2)}, u32[]{:S(2)}) %collective-permute-start.32) | collective-permute-done | bytes 130080 | tf_op jit(solution)/shard_map/ppermute | solution.py:434
  6.2 0.0 copy-start.1
  6.2 0.7 %copy-done.1 = f32[8,2,4,508]{3,2,1,0:T(4,128)} copy-done((f32[8,2,4,508]{3,2,1,0:T(4,128)}, f32[8,2,4,508]{3,2,1,0:T(4,128)S(1)}, u32[]{:S(2)}) %copy-start.1) | copy-done | bytes 130072
  6.9 1.8 %pair.1 = (f32[8,8,8,128]{3,2,1,0:T(8,128)}, f32[4,5,8,128]{3,2,1,0:T(8,128)S(1)}, f32[5,5,8,128]{3,2,1,0:T(8,128)S(1)}) custom-call(s32[1]{0:T(128)} %copy.37.refs_0_, f32[8,2,4,508]{3,2,1,0:T(4,128)} %refs_1_.5, f32[8,2,4,508]{3,2,1,0:T(4,128)} %copy-done.1), custom_call_target="tpu_custom_call" | custom-call | tf_op jit(solution)/shard_map/pair/pallas_call | solution.py:435
  8.6 9.9 %conditional.1 = (f32[4,5,8,128]{3,2,1,0:T(8,128)}, f32[5,5,8,128]{3,2,1,0:T(8,128)}) conditional(s32[]{:T(128)} %clamp.3, (f32[4,5,8,128]{3,2,1,0:T(8,128)S(1)}, f32[5,5,8,128]{3,2,1,0:T(8,128)S(1)}) %tuple.69, (f32[4,5,8,128]{3,2,1,0:T(8,128)S(1)}, f32[5,5,8,128]{3,2,1,0:T(8,128)S(1)}) %tuple.69, ...), branch_computations={%region_0.1_spmd, %region_1.2_spmd, %region_2.3_spmd, %region_3.4_... | conditional | bytes 737376 | solution.py:451
  8.6 3.3 %collective-permute-start.21 = (f32[5,5,8,128]{3,2,1,0:T(8,128)S(1)}, f32[5,5,8,128]{3,2,1,0:T(8,128)}, u32[]{:S(2)}, u32[]{:S(2)}) collective-permute-start(f32[5,5,8,128]{3,2,1,0:T(8,128)S(1)} %get-tuple-element.90), channel_id=1, source_target_pairs={{0,27},{1,28},{2,29},{3,30},{4,31},{5,24},{6,25},{7,26},{8,0},{9,1... | collective-permute-start | bytes 307208 | tf_op jit(solution)/shard_map/cond/branch_10_fun/ppermute | solution.py:427
  11.9 0.0 collective-permute-start.20
  11.9 6.7 %collective-permute-done.20 = f32[4,5,8,128]{3,2,1,0:T(8,128)} collective-permute-done((f32[4,5,8,128]{3,2,1,0:T(8,128)S(1)}, f32[4,5,8,128]{3,2,1,0:T(8,128)}, u32[]{:S(2)}, u32[]{:S(2)}) %collective-permute-start.20) | collective-permute-done | bytes 81952 | tf_op jit(solution)/shard_map/cond/branch_10_fun/ppermute | solution.py:427
  18.6 0.0 collective-permute-done.21
  18.6 2.6 %step.1.refs_2_ = f32[8,4,8,128]{3,2,1,0:T(8,128)} custom-call(s32[1]{0:T(128)} %copy.37.refs_0_, s32[4]{0:T(128)} %refs_1_.6, f32[8,8,8,128]{3,2,1,0:T(8,128)} %get-tuple-element.108.refs_2_, f32[4,5,8,128]{3,2,1,0:T(8,128)} %get-tuple-element.111.refs_3_, f32[5,5,8,128]{3,2,1,0:T(8,128)} %get-tuple-element.112.refs_4_), custom_call_target="tpu_custom_call" | custom-call | tf_op jit(solution)/shard_map/step/pallas_call | solution.py:452
  21.2 2.7 %collective-permute-start.35 = (f32[8,4,8,128]{3,2,1,0:T(8,128)}, f32[8,4,8,128]{3,2,1,0:T(8,128)S(1)}, u32[]{:S(2)}, u32[]{:S(2)}) collective-permute-start(f32[8,4,8,128]{3,2,1,0:T(8,128)} %step.1.refs_2_), channel_id=1, source_target_pairs={{0,6},{1,7},{2,4},{3,5},{4,2},{5,3},{6,0},{7,1},{8,14},{9,15},{10,... | collective-permute-start | bytes 393224 | tf_op jit(solution)/shard_map/ppermute | solution.py:462
  23.8 1.5 %collective-permute-start.34 = (f32[8,4,8,128]{3,2,1,0:T(8,128)}, f32[8,4,8,128]{3,2,1,0:T(8,128)S(1)}, u32[]{:S(2)}, u32[]{:S(2)}) collective-permute-start(f32[8,4,8,128]{3,2,1,0:T(8,128)} %step.1.refs_2_), channel_id=1, source_target_pairs={{0,4},{1,5},{2,6},{3,7},{4,0},{5,1},{6,2},{7,3},{8,12},{9,13},{10,... | collective-permute-start | bytes 393224 | tf_op jit(solution)/shard_map/ppermute | solution.py:462
  25.4 0.0 collective-permute-start.33
  25.4 2.7 %collective-permute-done.35.refs_5_ = f32[8,4,8,128]{3,2,1,0:T(8,128)S(1)} collective-permute-done((f32[8,4,8,128]{3,2,1,0:T(8,128)}, f32[8,4,8,128]{3,2,1,0:T(8,128)S(1)}, u32[]{:S(2)}, u32[]{:S(2)}) %collective-permute-start.35) | collective-permute-done | bytes 131104 | tf_op jit(solution)/shard_map/ppermute | solution.py:462
  28.0 0.0 copy-start.2
  28.0 3.4 %collective-permute-done.34.refs_4_ = f32[8,4,8,128]{3,2,1,0:T(8,128)S(1)} collective-permute-done((f32[8,4,8,128]{3,2,1,0:T(8,128)}, f32[8,4,8,128]{3,2,1,0:T(8,128)S(1)}, u32[]{:S(2)}, u32[]{:S(2)}) %collective-permute-start.34) | collective-permute-done | bytes 131104 | tf_op jit(solution)/shard_map/ppermute | solution.py:462
  31.5 0.0 copy-start.3
  31.5 0.0 collective-permute-done.33.refs_3_
  31.5 0.0 copy-done.2
  31.5 0.6 %copy-done.3 = f32[8,4,8,128]{3,2,1,0:T(8,128)} copy-done((f32[8,4,8,128]{3,2,1,0:T(8,128)}, f32[8,4,8,128]{3,2,1,0:T(8,128)S(1)}, u32[]{:S(2)}) %copy-start.3) | copy-done | bytes 131096
  32.1 0.0 copy-start.4
  32.1 0.6 %copy-done.4 = f32[8,4,8,128]{3,2,1,0:T(8,128)} copy-done((f32[8,4,8,128]{3,2,1,0:T(8,128)}, f32[8,4,8,128]{3,2,1,0:T(8,128)S(1)}, u32[]{:S(2)}) %copy-start.4) | copy-done | bytes 131096
  32.7 2.2 %gather.1 = (f32[4,8,4,8,128]{4,3,2,1,0:T(8,128)}, f32[8,4,8,128]{3,2,1,0:T(8,128)}) custom-call(s32[1]{0:T(128)} %copy.37.refs_0_, s32[4]{0:T(128)} %refs_1_.9, f32[8,4,8,128]{3,2,1,0:T(8,128)} %step.1.refs_2_, f32[8,4,8,128]{3,2,1,0:T(8,128)} %copy-done.4, f32[8,4,8,128]{3,2,1,0:T(8,128)} %copy-done.3, f32[8,4,8,128]{3,2,1,0:T(8,128)} %copy-done.2), custom_call_target="tpu_custom_call" | custom-call | tf_op jit(solution)/shard_map/gather/pallas_call | solution.py:465
  35.0 0.0 collective-permute-start.36
  35.0 2.1 %keep.1.refs_2_ = f32[8,4,8,128]{3,2,1,0:T(8,128)} custom-call(s32[1]{0:T(128)} %copy.37.refs_0_, s32[4]{0:T(128)} %refs_1_.9, f32[4,8,4,8,128]{4,3,2,1,0:T(8,128)} %get-tuple-element.113.refs_2_), custom_call_target="tpu_custom_call" | custom-call | tf_op jit(solution)/shard_map/keep/pallas_call | solution.py:473
  37.1 0.0 collective-permute-done.36.refs_3_
  37.1 0.0 copy-start
  37.1 0.6 %copy-done = f32[8,4,8,128]{3,2,1,0:T(8,128)} copy-done((f32[8,4,8,128]{3,2,1,0:T(8,128)}, f32[8,4,8,128]{3,2,1,0:T(8,128)S(1)}, u32[]{:S(2)}) %copy-start) | copy-done | bytes 131096
  37.7 1.7 %merge.1 = f32[8,2,4,508]{3,2,1,0:T(4,128)} custom-call(s32[1]{0:T(128)} %copy.37.refs_0_, s32[4]{0:T(128)} %refs_1_.9, f32[8,4,8,128]{3,2,1,0:T(8,128)} %keep.1.refs_2_, f32[8,4,8,128]{3,2,1,0:T(8,128)} %copy-done), custom_call_target="tpu_custom_call" | custom-call | tf_op jit(solution)/shard_map/merge/pallas_call | solution.py:480
Async XLA Ops:
  0.0 6.2 %collective-permute-start.32 = (f32[8,2,4,508]{3,2,1,0:T(4,128)}, f32[8,2,4,508]{3,2,1,0:T(4,128)S(1)}, u32[]{:S(2)}, u32[]{:S(2)}) collective-permute-start(f32[8,2,4,508]{3,2,1,0:T(4,128)} %refs_1_.5), channel_id=1, source_target_pairs={{0,1},{1,2},{2,3},{3,4},{4,5},{5,6},{6,7},{7,0},{8,9},{9,10},{10,1... | collective-permute-start | bytes 390152 | tf_op jit(solution)/shard_map/ppermute | solution.py:434
  6.2 0.7 %copy-start.1 = (f32[8,2,4,508]{3,2,1,0:T(4,128)}, f32[8,2,4,508]{3,2,1,0:T(4,128)S(1)}, u32[]{:S(2)}) copy-start(f32[8,2,4,508]{3,2,1,0:T(4,128)S(1)} %collective-permute-done.32.refs_2_) | copy-start | bytes 390148
  8.6 9.9 %collective-permute-start.21 = (f32[5,5,8,128]{3,2,1,0:T(8,128)S(1)}, f32[5,5,8,128]{3,2,1,0:T(8,128)}, u32[]{:S(2)}, u32[]{:S(2)}) collective-permute-start(f32[5,5,8,128]{3,2,1,0:T(8,128)S(1)} %get-tuple-element.90), channel_id=1, source_target_pairs={{0,27},{1,28},{2,29},{3,30},{4,31},{5,24},{6,25},{7,26},{8,0},{9,1... | collective-permute-start | bytes 307208 | tf_op jit(solution)/shard_map/cond/branch_10_fun/ppermute | solution.py:427
  11.9 6.7 %collective-permute-start.20 = (f32[4,5,8,128]{3,2,1,0:T(8,128)S(1)}, f32[4,5,8,128]{3,2,1,0:T(8,128)}, u32[]{:S(2)}, u32[]{:S(2)}) collective-permute-start(f32[4,5,8,128]{3,2,1,0:T(8,128)S(1)} %get-tuple-element.89), channel_id=1, source_target_pairs={{0,8},{1,9},{2,10},{3,11},{4,12},{5,13},{6,14},{7,15},{8,16},{9,17... | collective-permute-start | bytes 245768 | tf_op jit(solution)/shard_map/cond/branch_10_fun/ppermute | solution.py:427
  21.2 6.9 %collective-permute-start.35 = (f32[8,4,8,128]{3,2,1,0:T(8,128)}, f32[8,4,8,128]{3,2,1,0:T(8,128)S(1)}, u32[]{:S(2)}, u32[]{:S(2)}) collective-permute-start(f32[8,4,8,128]{3,2,1,0:T(8,128)} %step.1.refs_2_), channel_id=1, source_target_pairs={{0,6},{1,7},{2,4},{3,5},{4,2},{5,3},{6,0},{7,1},{8,14},{9,15},{10,... | collective-permute-start | bytes 393224 | tf_op jit(solution)/shard_map/ppermute | solution.py:462
  23.8 7.6 %collective-permute-start.34 = (f32[8,4,8,128]{3,2,1,0:T(8,128)}, f32[8,4,8,128]{3,2,1,0:T(8,128)S(1)}, u32[]{:S(2)}, u32[]{:S(2)}) collective-permute-start(f32[8,4,8,128]{3,2,1,0:T(8,128)} %step.1.refs_2_), channel_id=1, source_target_pairs={{0,4},{1,5},{2,6},{3,7},{4,0},{5,1},{6,2},{7,3},{8,12},{9,13},{10,... | collective-permute-start | bytes 393224 | tf_op jit(solution)/shard_map/ppermute | solution.py:462
  25.4 6.1 %collective-permute-start.33 = (f32[8,4,8,128]{3,2,1,0:T(8,128)}, f32[8,4,8,128]{3,2,1,0:T(8,128)S(1)}, u32[]{:S(2)}, u32[]{:S(2)}) collective-permute-start(f32[8,4,8,128]{3,2,1,0:T(8,128)} %step.1.refs_2_), channel_id=1, source_target_pairs={{0,2},{1,3},{2,0},{3,1},{4,6},{5,7},{6,4},{7,5},{8,10},{9,11},{10,... | collective-permute-start | bytes 393224 | tf_op jit(solution)/shard_map/ppermute | solution.py:462
  28.0 3.4 %copy-start.2 = (f32[8,4,8,128]{3,2,1,0:T(8,128)}, f32[8,4,8,128]{3,2,1,0:T(8,128)S(1)}, u32[]{:S(2)}) copy-start(f32[8,4,8,128]{3,2,1,0:T(8,128)S(1)} %collective-permute-done.35.refs_5_) | copy-start | bytes 393220
  31.5 0.6 %copy-start.3 = (f32[8,4,8,128]{3,2,1,0:T(8,128)}, f32[8,4,8,128]{3,2,1,0:T(8,128)S(1)}, u32[]{:S(2)}) copy-start(f32[8,4,8,128]{3,2,1,0:T(8,128)S(1)} %collective-permute-done.34.refs_4_) | copy-start | bytes 393220
  32.1 0.7 %copy-start.4 = (f32[8,4,8,128]{3,2,1,0:T(8,128)}, f32[8,4,8,128]{3,2,1,0:T(8,128)S(1)}, u32[]{:S(2)}) copy-start(f32[8,4,8,128]{3,2,1,0:T(8,128)S(1)} %collective-permute-done.33.refs_3_) | copy-start | bytes 393220
  35.0 2.1 %collective-permute-start.36 = (f32[8,4,8,128]{3,2,1,0:T(8,128)}, f32[8,4,8,128]{3,2,1,0:T(8,128)S(1)}, u32[]{:S(2)}, u32[]{:S(2)}) collective-permute-start(f32[8,4,8,128]{3,2,1,0:T(8,128)} %get-tuple-element.114), channel_id=1, source_target_pairs={{0,1},{1,0},{2,3},{3,2},{4,5},{5,4},{6,7},{7,6},{8,9},{9,8},{10,11... | collective-permute-start | bytes 393224 | tf_op jit(solution)/shard_map/ppermute | solution.py:462
  37.1 0.6 %copy-start = (f32[8,4,8,128]{3,2,1,0:T(8,128)}, f32[8,4,8,128]{3,2,1,0:T(8,128)S(1)}, u32[]{:S(2)}) copy-start(f32[8,4,8,128]{3,2,1,0:T(8,128)S(1)} %collective-permute-done.36.refs_3_) | copy-start | bytes 393220

commit v5 on v4

--- a/solution.py
+++ b/solution.py
@@ -408,6 +408,7 @@
     places, peers = (mesh.shape["gx"], mesh.shape["gy"])
     smem = pl.BlockSpec(memory_space=pltpu.SMEM)
     vmem = pl.BlockSpec(memory_space=pltpu.VMEM)
+    params = pltpu.CompilerParams(vmem_limit_bytes=8 * 2**20)
     axes = ("gx", "gy")
 
     def array(*shape):
@@ -441,6 +442,7 @@
             ],
             in_specs=[smem, vmem, vmem],
             out_specs=[vmem] * 3,
+            compiler_params=params,
             name="pair",
         )(shear_offset, state, below)
         _, _, _, up_hop, down_hop = plan(shear_offset[0], cells, peers)
@@ -455,6 +457,7 @@
             in_specs=[smem] * 2 + [vmem] * 3,
             out_specs=vmem,
             scratch_shapes=[scratch(window, FIELDS, PLANES)] * 2,
+            compiler_params=params,
             name="step",
         )(shear_offset, frac_index, joined, up, down)
 
@@ -467,6 +470,7 @@
             out_shape=[array(peers // 2, FIELDS, single), array(FIELDS, single)],
             in_specs=[smem] * 2 + [vmem] * (peers // 2),
             out_specs=[vmem] * 2,
+            compiler_params=params,
             name="gather",
         )(shear_offset, remap_shift, *blocks)
         other = exchange(other, 1)
@@ -475,6 +479,7 @@
             out_shape=array(FIELDS, single),
             in_specs=[smem] * 2 + [vmem],
             out_specs=vmem,
+            compiler_params=params,
             name="keep",
         )(shear_offset, remap_shift, blocks)
         return pl.pallas_call(
@@ -482,6 +487,7 @@
             out_shape=jax.ShapeDtypeStruct(state.shape, jnp.float32),
             in_specs=[smem] * 2 + [vmem] * 2,
             out_specs=vmem,
+            compiler_params=params,
             name="merge",
         )(shear_offset, remap_shift, mine, other)
 

time: 39 us -> 33.5 us (0.86); the launches traced: 39.5 us -> 33.3 us
  Pallas kernels: 10.4 us -> 5.31 us
  starting transfers between devices: 7.93 us -> 9.45 us
  waiting for transfers between devices: 17.7 us -> 16.2 us
  local copies, waits for them, and re-layouts: 2.58 us -> 1.56 us
    ppermute x4, waiting for transfers between devices: 6.1 us -> 3.94 us  [exchange(): return lax.ppermute(value, 'gy', [(i, i ^ bits) for i in range(peers)])]
    ppermute x2, starting transfers between devices: 3.26 us -> 5.37 us  [ghosts(): return (lax.ppermute(up, axes, rise), lax.ppermute(down, axes, fall))]
    pallas_call x1, Pallas kernels: 1.77 us -> 0.27 us  [shards(): pl.pallas_call(lambda *refs: pair_kernel(cells, peers, *refs), out_shape=...]
    pallas_call x1, Pallas kernels: 2.24 us -> 0.94 us  [shards(): pl.pallas_call(lambda *refs: gather_kernel(cells, peers, rows, *refs), ou...]
    pallas_call x1, Pallas kernels: 2.08 us -> 0.92 us  [shards(): pl.pallas_call(lambda *refs: keep_kernel(cells, peers, rows, *refs), out_...]
    unnamed x10 -> x6, local copies, waits for them, and re-layouts: 2.58 us -> 1.56 us
    pallas_call x1, Pallas kernels: 2.61 us -> 1.89 us  [shards(): pl.pallas_call(lambda *refs: step_kernel(cells, peers, rows, *refs), out_...]
    ppermute x4, starting transfers between devices: 4.22 us -> 3.62 us  [exchange(): return lax.ppermute(value, 'gy', [(i, i ^ bits) for i in range(peers)])]
  transfers between devices with their start and end apart: 7 -> 7, of which waited for: 4 -> 6; matrix products, arithmetic and copies ran while one was open for 0% -> 0% of each run, Pallas kernels for 5% -> 3%
where the time goes in v5:
time: 33.5 us; the launch traced here: 33.3 us
  waiting for transfers between devices  16.2 us (48%)
  starting transfers between devices  9.45 us (28%)
  Pallas kernels  5.31 us (16%)
  local copies, waits for them, and re-layouts  1.56 us (5%)
  between operations  0.81 us (2%)
    ppermute x2, waiting for transfers between devices, ghosts(): return (lax.ppermute(up, axes, rise), lax.ppermute(down, axes, fall))  7.24 us
    ppermute x2, starting transfers between devices, ghosts(): return (lax.ppermute(up, axes, rise), lax.ppermute(down, axes, fall))  5.37 us
    ppermute x1, waiting for transfers between devices, shards(): lax.ppermute(state, 'gy', [(i, (i + 1) % peers) for i in range(peers)])  4.98 us
    ppermute x4, waiting for transfers between devices, exchange(): return lax.ppermute(value, 'gy', [(i, i ^ bits) for i in range(peers)])  3.94 us
    ppermute x4, starting transfers between devices, exchange(): return lax.ppermute(value, 'gy', [(i, i ^ bits) for i in range(peers)])  3.62 us
    pallas_call x1, Pallas kernels, shards(): pl.pallas_call(lambda *refs: step_kernel(cells, peers, rows, *refs), out_...  1.89 us
    unnamed x6, local copies, waits for them, and re-layouts  1.56 us
    pallas_call x1, Pallas kernels, shards(): pl.pallas_call(lambda *refs: merge_kernel(cells, peers, rows, *refs), out...  1.29 us
  transfers between devices with their start and end apart: 7, of which 6 were waited for; matrix products, arithmetic and copies ran while one was open for 0% of the time, Pallas kernels for 3%

profile of v5, /device:TPU:0, one launch (start us, length us, event | category | flops | bytes accessed | tf_op | source)
XLA Modules:
  0.0 33.3 jit_solution(2883784104963716240)
XLA Ops:
  0.0 0.5 %collective-permute-start.32 = (f32[8,2,4,508]{3,2,1,0:T(4,128)}, f32[8,2,4,508]{3,2,1,0:T(4,128)S(1)}, u32[]{:S(2)}, u32[]{:S(2)}) collective-permute-start(f32[8,2,4,508]{3,2,1,0:T(4,128)} %refs_1_.5), channel_id=1, source_target_pairs={{0,1},{1,2},{2,3},{3,4},{4,5},{5,6},{6,7},{7,0},{8,9},{9,10},{10,1... | collective-permute-start | bytes 390152 | tf_op jit(solution)/shard_map/ppermute | solution.py:435
  1.2 5.0 %collective-permute-done.32.refs_2_ = f32[8,2,4,508]{3,2,1,0:T(4,128)S(1)} collective-permute-done((f32[8,2,4,508]{3,2,1,0:T(4,128)}, f32[8,2,4,508]{3,2,1,0:T(4,128)S(1)}, u32[]{:S(2)}, u32[]{:S(2)}) %collective-permute-start.32) | collective-permute-done | bytes 130080 | tf_op jit(solution)/shard_map/ppermute | solution.py:435
  6.2 0.0 copy-start
  6.2 0.9 %copy-done = f32[8,2,4,508]{3,2,1,0:T(4,128)S(1)} copy-done((f32[8,2,4,508]{3,2,1,0:T(4,128)S(1)}, f32[8,2,4,508]{3,2,1,0:T(4,128)}, u32[]{:S(2)}) %copy-start) | copy-done | bytes 130072
  7.1 0.3 pair.1
  7.4 12.6 %conditional.1 = (f32[4,5,8,128]{3,2,1,0:T(8,128)}, f32[5,5,8,128]{3,2,1,0:T(8,128)}) conditional(s32[]{:T(128)} %clamp.3, (f32[4,5,8,128]{3,2,1,0:T(8,128)S(1)}, f32[5,5,8,128]{3,2,1,0:T(8,128)S(1)}) %tuple.69, (f32[4,5,8,128]{3,2,1,0:T(8,128)S(1)}, f32[5,5,8,128]{3,2,1,0:T(8,128)S(1)}) %tuple.69, ...), branch_computations={%region_0.1_spmd, %region_1.2_spmd, %region_2.3_spmd, %region_3.4_... | conditional | bytes 737376 | solution.py:453
  7.4 5.4 %collective-permute-start.17 = (f32[5,5,8,128]{3,2,1,0:T(8,128)S(1)}, f32[5,5,8,128]{3,2,1,0:T(8,128)}, u32[]{:S(2)}, u32[]{:S(2)}) collective-permute-start(f32[5,5,8,128]{3,2,1,0:T(8,128)S(1)} %get-tuple-element.86), channel_id=1, source_target_pairs={{0,28},{1,29},{2,30},{3,31},{4,24},{5,25},{6,26},{7,27},{8,0},{9,1... | collective-permute-start | bytes 307208 | tf_op jit(solution)/shard_map/cond/branch_8_fun/ppermute | solution.py:428
  12.8 0.0 collective-permute-start.16
  12.8 7.2 %collective-permute-done.16 = f32[4,5,8,128]{3,2,1,0:T(8,128)} collective-permute-done((f32[4,5,8,128]{3,2,1,0:T(8,128)S(1)}, f32[4,5,8,128]{3,2,1,0:T(8,128)}, u32[]{:S(2)}, u32[]{:S(2)}) %collective-permute-start.16) | collective-permute-done | bytes 81952 | tf_op jit(solution)/shard_map/cond/branch_8_fun/ppermute | solution.py:428
  20.0 0.0 collective-permute-done.17
  20.0 0.0 copy-start.2
  20.0 0.7 %copy-done.2 = s32[4]{0:T(128)S(1)} copy-done((s32[4]{0:T(128)S(1)}, s32[4]{0:T(128)}, u32[]{:S(2)}) %copy-start.2) | copy-done | bytes 40
  20.7 0.0 copy-start.1
  20.7 1.9 %step.1.refs_2_ = f32[8,4,8,128]{3,2,1,0:T(8,128)S(1)} custom-call(s32[1]{0:T(128)} %copy.37.refs_0_, s32[4]{0:T(128)S(1)} %copy-done.2, f32[8,8,8,128]{3,2,1,0:T(8,128)S(1)} %get-tuple-element.108.refs_2_, f32[4,5,8,128]{3,2,1,0:T(8,128)} %get-tuple-element.111.refs_3_, f32[5,5,8,128]{3,2,1,0:T(8,128)} %get-tuple-element.112.refs_4_), custom_call_target="tpu_custom_call" | custom-call | tf_op jit(solution)/shard_map/step/pallas_call | solution.py:454
  22.6 0.6 %collective-permute-start.35 = (f32[8,4,8,128]{3,2,1,0:T(8,128)S(1)}, f32[8,4,8,128]{3,2,1,0:T(8,128)S(1)}, u32[]{:S(2)}, u32[]{:S(2)}) collective-permute-start(f32[8,4,8,128]{3,2,1,0:T(8,128)S(1)} %step.1.refs_2_), channel_id=1, source_target_pairs={{0,6},{1,7},{2,4},{3,5},{4,2},{5,3},{6,0},{7,1},{8,14},{9,15},{10,... | collective-permute-start | bytes 393224 | tf_op jit(solution)/shard_map/ppermute | solution.py:465
  23.2 1.5 %collective-permute-start.34 = (f32[8,4,8,128]{3,2,1,0:T(8,128)S(1)}, f32[8,4,8,128]{3,2,1,0:T(8,128)S(1)}, u32[]{:S(2)}, u32[]{:S(2)}) collective-permute-start(f32[8,4,8,128]{3,2,1,0:T(8,128)S(1)} %step.1.refs_2_), channel_id=1, source_target_pairs={{0,4},{1,5},{2,6},{3,7},{4,0},{5,1},{6,2},{7,3},{8,12},{9,13},{10,... | collective-permute-start | bytes 393224 | tf_op jit(solution)/shard_map/ppermute | solution.py:465
  24.7 1.4 %collective-permute-start.33 = (f32[8,4,8,128]{3,2,1,0:T(8,128)S(1)}, f32[8,4,8,128]{3,2,1,0:T(8,128)S(1)}, u32[]{:S(2)}, u32[]{:S(2)}) collective-permute-start(f32[8,4,8,128]{3,2,1,0:T(8,128)S(1)} %step.1.refs_2_), channel_id=1, source_target_pairs={{0,2},{1,3},{2,0},{3,1},{4,6},{5,7},{6,4},{7,5},{8,10},{9,11},{10,... | collective-permute-start | bytes 393224 | tf_op jit(solution)/shard_map/ppermute | solution.py:465
  26.1 2.5 %collective-permute-done.35.refs_5_ = f32[8,4,8,128]{3,2,1,0:T(8,128)S(1)} collective-permute-done((f32[8,4,8,128]{3,2,1,0:T(8,128)S(1)}, f32[8,4,8,128]{3,2,1,0:T(8,128)S(1)}, u32[]{:S(2)}, u32[]{:S(2)}) %collective-permute-start.35) | collective-permute-done | bytes 131104 | tf_op jit(solution)/shard_map/ppermute | solution.py:465
  28.6 0.9 %collective-permute-done.34.refs_4_ = f32[8,4,8,128]{3,2,1,0:T(8,128)S(1)} collective-permute-done((f32[8,4,8,128]{3,2,1,0:T(8,128)S(1)}, f32[8,4,8,128]{3,2,1,0:T(8,128)S(1)}, u32[]{:S(2)}, u32[]{:S(2)}) %collective-permute-start.34) | collective-permute-done | bytes 131104 | tf_op jit(solution)/shard_map/ppermute | solution.py:465
  29.6 0.1 collective-permute-done.33.refs_3_
  29.7 0.0 copy-done.1
  29.7 0.9 %gather.1 = (f32[4,8,4,8,128]{4,3,2,1,0:T(8,128)S(1)}, f32[8,4,8,128]{3,2,1,0:T(8,128)S(1)}) custom-call(s32[1]{0:T(128)} %copy.37.refs_0_, s32[4]{0:T(128)S(1)} %copy-done.1, f32[8,4,8,128]{3,2,1,0:T(8,128)S(1)} %step.1.refs_2_, f32[8,4,8,128]{3,2,1,0:T(8,128)S(1)} %collective-permute-done.33.refs_3_, f32[8,4,8,128]{3,2,1,0:T(8,128)S(1)} %collective-permute-done.34.refs_4_, ...), custom_call_target="tpu_custom_call" | custom-call | tf_op jit(solution)/shard_map/gather/pallas_call | solution.py:468
  30.6 0.1 collective-permute-start.36
  30.7 0.9 %keep.1.refs_2_ = f32[8,4,8,128]{3,2,1,0:T(8,128)S(1)} custom-call(s32[1]{0:T(128)} %copy.37.refs_0_, s32[4]{0:T(128)S(1)} %copy-done.1, f32[4,8,4,8,128]{4,3,2,1,0:T(8,128)S(1)} %get-tuple-element.113.refs_2_), custom_call_target="tpu_custom_call" | custom-call | tf_op jit(solution)/shard_map/keep/pallas_call | solution.py:477
  31.6 0.4 %collective-permute-done.36.refs_3_ = f32[8,4,8,128]{3,2,1,0:T(8,128)S(1)} collective-permute-done((f32[8,4,8,128]{3,2,1,0:T(8,128)S(1)}, f32[8,4,8,128]{3,2,1,0:T(8,128)S(1)}, u32[]{:S(2)}, u32[]{:S(2)}) %collective-permute-start.36) | collective-permute-done | bytes 131104 | tf_op jit(solution)/shard_map/ppermute | solution.py:465
  32.0 1.3 %merge.1 = f32[8,2,4,508]{3,2,1,0:T(4,128)} custom-call(s32[1]{0:T(128)} %copy.37.refs_0_, s32[4]{0:T(128)S(1)} %copy-done.1, f32[8,4,8,128]{3,2,1,0:T(8,128)S(1)} %keep.1.refs_2_, f32[8,4,8,128]{3,2,1,0:T(8,128)S(1)} %collective-permute-done.36.refs_3_), custom_call_target="tpu_custom_call" | custom-call | tf_op jit(solution)/shard_map/merge/pallas_call | solution.py:485
Async XLA Ops:
  0.0 6.2 %collective-permute-start.32 = (f32[8,2,4,508]{3,2,1,0:T(4,128)}, f32[8,2,4,508]{3,2,1,0:T(4,128)S(1)}, u32[]{:S(2)}, u32[]{:S(2)}) collective-permute-start(f32[8,2,4,508]{3,2,1,0:T(4,128)} %refs_1_.5), channel_id=1, source_target_pairs={{0,1},{1,2},{2,3},{3,4},{4,5},{5,6},{6,7},{7,0},{8,9},{9,10},{10,1... | collective-permute-start | bytes 390152 | tf_op jit(solution)/shard_map/ppermute | solution.py:435
  6.2 0.9 %copy-start = (f32[8,2,4,508]{3,2,1,0:T(4,128)S(1)}, f32[8,2,4,508]{3,2,1,0:T(4,128)}, u32[]{:S(2)}) copy-start(f32[8,2,4,508]{3,2,1,0:T(4,128)} %refs_1_.5) | copy-start | bytes 390148
  7.4 12.6 %collective-permute-start.17 = (f32[5,5,8,128]{3,2,1,0:T(8,128)S(1)}, f32[5,5,8,128]{3,2,1,0:T(8,128)}, u32[]{:S(2)}, u32[]{:S(2)}) collective-permute-start(f32[5,5,8,128]{3,2,1,0:T(8,128)S(1)} %get-tuple-element.86), channel_id=1, source_target_pairs={{0,28},{1,29},{2,30},{3,31},{4,24},{5,25},{6,26},{7,27},{8,0},{9,1... | collective-permute-start | bytes 307208 | tf_op jit(solution)/shard_map/cond/branch_8_fun/ppermute | solution.py:428
  12.8 7.2 %collective-permute-start.16 = (f32[4,5,8,128]{3,2,1,0:T(8,128)S(1)}, f32[4,5,8,128]{3,2,1,0:T(8,128)}, u32[]{:S(2)}, u32[]{:S(2)}) collective-permute-start(f32[4,5,8,128]{3,2,1,0:T(8,128)S(1)} %get-tuple-element.85), channel_id=1, source_target_pairs={{0,8},{1,9},{2,10},{3,11},{4,12},{5,13},{6,14},{7,15},{8,16},{9,17... | collective-permute-start | bytes 245768 | tf_op jit(solution)/shard_map/cond/branch_8_fun/ppermute | solution.py:428
  20.0 0.7 %copy-start.2 = (s32[4]{0:T(128)S(1)}, s32[4]{0:T(128)}, u32[]{:S(2)}) copy-start(s32[4]{0:T(128)} %refs_1_.6) | copy-start | bytes 52
  20.7 9.0 %copy-start.1 = (s32[4]{0:T(128)S(1)}, s32[4]{0:T(128)}, u32[]{:S(2)}) copy-start(s32[4]{0:T(128)} %refs_1_.9) | copy-start | bytes 52
  22.6 6.0 %collective-permute-start.35 = (f32[8,4,8,128]{3,2,1,0:T(8,128)S(1)}, f32[8,4,8,128]{3,2,1,0:T(8,128)S(1)}, u32[]{:S(2)}, u32[]{:S(2)}) collective-permute-start(f32[8,4,8,128]{3,2,1,0:T(8,128)S(1)} %step.1.refs_2_), channel_id=1, source_target_pairs={{0,6},{1,7},{2,4},{3,5},{4,2},{5,3},{6,0},{7,1},{8,14},{9,15},{10,... | collective-permute-start | bytes 393224 | tf_op jit(solution)/shard_map/ppermute | solution.py:465
  23.2 6.4 %collective-permute-start.34 = (f32[8,4,8,128]{3,2,1,0:T(8,128)S(1)}, f32[8,4,8,128]{3,2,1,0:T(8,128)S(1)}, u32[]{:S(2)}, u32[]{:S(2)}) collective-permute-start(f32[8,4,8,128]{3,2,1,0:T(8,128)S(1)} %step.1.refs_2_), channel_id=1, source_target_pairs={{0,4},{1,5},{2,6},{3,7},{4,0},{5,1},{6,2},{7,3},{8,12},{9,13},{10,... | collective-permute-start | bytes 393224 | tf_op jit(solution)/shard_map/ppermute | solution.py:465
  24.7 5.0 %collective-permute-start.33 = (f32[8,4,8,128]{3,2,1,0:T(8,128)S(1)}, f32[8,4,8,128]{3,2,1,0:T(8,128)S(1)}, u32[]{:S(2)}, u32[]{:S(2)}) collective-permute-start(f32[8,4,8,128]{3,2,1,0:T(8,128)S(1)} %step.1.refs_2_), channel_id=1, source_target_pairs={{0,2},{1,3},{2,0},{3,1},{4,6},{5,7},{6,4},{7,5},{8,10},{9,11},{10,... | collective-permute-start | bytes 393224 | tf_op jit(solution)/shard_map/ppermute | solution.py:465
  30.6 1.4 %collective-permute-start.36 = (f32[8,4,8,128]{3,2,1,0:T(8,128)S(1)}, f32[8,4,8,128]{3,2,1,0:T(8,128)S(1)}, u32[]{:S(2)}, u32[]{:S(2)}) collective-permute-start(f32[8,4,8,128]{3,2,1,0:T(8,128)S(1)} %get-tuple-element.114), channel_id=1, source_target_pairs={{0,1},{1,0},{2,3},{3,2},{4,5},{5,4},{6,7},{7,6},{8,9},{9,8},{10,11... | collective-permute-start | bytes 393224 | tf_op jit(solution)/shard_map/ppermute | solution.py:465

commit v6 on v5

--- a/solution.py
+++ b/solution.py
@@ -67,54 +67,28 @@
     return own, up, down, up_hop, down_hop
 
 
-def pair_kernel(cells, peers, shear_ref, state_ref, below_ref, joined_ref, up_ref, down_ref):
-    place = lax.axis_index("gx")
-    places = lax.axis_size("gx")
-    own, up, down, _, _ = plan(shear_ref[0], cells, peers)
-    up = jnp.where(place == places - 1, up, own)
-    down = jnp.where(place == 0, down, own)
+def block_tiles(ref, f, cells):
+    value = jnp.concatenate([ref[f, z] for z in range(PLANES)], axis=0)
+    tiles = []
+    for i in range(0, cells, LANES):
+        tile = value[:, i : min(i + LANES, cells)]
+        spare = LANES - tile.shape[1]
+        if spare:
+            tile = jnp.concatenate([tile, jnp.zeros((SUBLANES, spare), tile.dtype)], axis=1)
+        tiles.append(tile)
+    return tiles
+
+
+def join_tiles(lower, upper, cells, put):
+    gap = cells % LANES
     lane = lane_index()
-    row = row_index()
-    single = tiles_for(cells)
-    gap = cells % LANES
-    double = joined_ref.shape[1]
-    window = up_ref.shape[1]
-
-    def tiles_of(ref, f):
-        both = [ref[f, z] for z in range(PLANES)]
-        value = jnp.concatenate(both, axis=0)
-        return [value[:, i * LANES : min((i + 1) * LANES, cells)] for i in range(single)]
-
-    def widened(tile):
-        spare = LANES - tile.shape[1]
-        if spare == 0:
-            return tile
-        return jnp.concatenate([tile, jnp.zeros((SUBLANES, spare), tile.dtype)], axis=1)
-
-    for f in range(FIELDS):
-        lower = [widened(t) for t in tiles_of(below_ref, f)]
-        upper = [turn_lanes(widened(t), gap) for t in tiles_of(state_ref, f)]
-        for i in range(single):
-            if i < single - 1:
-                joined_ref[f, i] = lower[i]
-            else:
-                joined_ref[f, i] = jnp.where(lane < gap, lower[i], upper[0])
-        for i in range(single, double):
-            k = i - single
-            joined_ref[f, i] = jnp.where(lane < gap, upper[k], upper[min(k + 1, single - 1)])
-
-    def cut(f, start):
-        return cut_window(joined_ref, f, start, window)
-
-    late = row % 4 >= SENT
-    for pair in range(FIELDS // 2):
-        ups = [cut(2 * pair + i, up) for i in range(2)]
-        downs = [cut(2 * pair + i, down) for i in range(2)]
-        for t in range(window):
-            up_ref[pair, t] = jnp.where(late, ups[0][t], turn_rows(ups[1][t], -SENT))
-            down_ref[pair, t] = jnp.where(late, turn_rows(downs[1][t], SENT), downs[0][t])
-    for t, value in enumerate(cut(FACE_X, down)):
-        down_ref[FIELDS // 2, t] = value
+    single = len(lower)
+    upper = [turn_lanes(tile, gap) for tile in upper]
+    for i in range(single - 1):
+        put(i, lower[i])
+    put(single - 1, jnp.where(lane < gap, lower[-1], upper[0]))
+    for k in range(single):
+        put(single + k, jnp.where(lane < gap, upper[k], upper[min(k + 1, single - 1)]))
 
 
 def cut_window(joined_ref, f, start, count):
@@ -125,6 +99,37 @@
     turned = [turn_lanes(tile, (LANES - part) % LANES) for tile in tiles]
     here = lane_index() < LANES - part
     return [jnp.where(here, turned[t], turned[t + 1]) for t in range(count)]
+
+
+def edge_kernel(cells, rows, state_ref, up_ref, down_ref):
+    row = row_index()
+    late = row % rows >= SENT
+    single = tiles_for(cells)
+    faces = jnp.zeros((SUBLANES, LANES), jnp.float32)
+    for pair in range(FIELDS // 2):
+        first, second = (block_tiles(state_ref, 2 * pair + i, cells) for i in range(2))
+        for t in range(single):
+            up_ref[pair * single + t] = jnp.where(late, first[t], turn_rows(second[t], -SENT))
+            down_ref[pair * single + t] = jnp.where(late, turn_rows(second[t], SENT), first[t])
+        if FACE_X // 2 == pair:
+            for t, tile in enumerate((first, second)[FACE_X % 2]):
+                for z in range(PLANES):
+                    at = t * PLANES + z
+                    faces = jnp.where(row == at, turn_rows(tile, at - (z * rows + SENT)), faces)
+    down_ref[FIELDS // 2 * single] = faces
+
+
+def join_kernel(cells, peers, shear_ref, state_ref, below_ref, out_ref, joined_ref):
+    own = plan(shear_ref[0], cells, peers)[0]
+    for f in range(FIELDS):
+
+        def put(i, tile):
+            joined_ref[f, i] = tile
+
+        lower, upper = (block_tiles(ref, f, cells) for ref in (below_ref, state_ref))
+        join_tiles(lower, upper, cells, put)
+        for t, tile in enumerate(cut_window(joined_ref, f, own, out_ref.shape[1])):
+            out_ref[f, t] = tile
 
 
 def cell_terms(state, next_face_x, next_face_y):
@@ -237,32 +242,56 @@
 
 def step_kernel(
     cells, peers, rows,
-    shear_ref, frac_ref, joined_ref, up_ref, down_ref, out_ref, state_ref, mid_ref,
+    shear_ref, frac_ref, block_ref, up_ref, up_below_ref, down_ref, down_below_ref,
+    out_ref, state_ref, mid_ref, joined_ref, ghost_ref,
 ):
-    own = plan(shear_ref[0], cells, peers)[0]
+    place = lax.axis_index("gx")
+    places = lax.axis_size("gx")
+    own, up_start, down_start, _, _ = plan(shear_ref[0], cells, peers)
+    up_start = jnp.where(place == 0, up_start, own)
+    down_start = jnp.where(place == places - 1, down_start, own)
     lane = lane_index()
     row = row_index()
-    window = up_ref.shape[1]
+    window = block_ref.shape[1]
     single = tiles_for(cells)
+    pairs = FIELDS // 2
+
+    def ghosts(index, tiles, start):
+        def put(i, tile):
+            joined_ref[index, i] = tile
+
+        join_tiles(*tiles, cells, put)
+        for t, tile in enumerate(cut_window(joined_ref, index, start, window)):
+            ghost_ref[index, t] = tile
+
+    for pair in range(pairs):
+        span = range(pair * single, (pair + 1) * single)
+        ghosts(pair, [[ref[i] for i in span] for ref in (up_below_ref, up_ref)], up_start)
+        tiles = [[ref[i] for i in span] for ref in (down_below_ref, down_ref)]
+        ghosts(pairs + pair, tiles, down_start)
+    faces = [ref[pairs * single] for ref in (down_below_ref, down_ref)]
+    tiles = [[turn_rows(face, -t * PLANES) for t in range(single)] for face in faces]
+    ghosts(2 * pairs, tiles, down_start)
 
     for f in range(FIELDS):
         pair, second = divmod(f, 2)
-        for t, tile in enumerate(cut_window(joined_ref, f, own, window)):
-            up = up_ref[pair, t]
-            down = down_ref[pair, t]
+        for t in range(window):
+            tile = block_ref[f, t]
+            up = ghost_ref[pair, t]
+            down = ghost_ref[pairs + pair, t]
             for z in range(PLANES):
-                up_at = z * 4 + (0 if second else SENT)
-                down_at = z * 4 + (SENT if second else 0)
-                value = turn_rows(tile, -z * 4)
+                up_at = z * rows + (0 if second else SENT)
+                down_at = z * rows + (SENT if second else 0)
+                value = turn_rows(tile, -z * rows)
                 value = jnp.where(row < rows, value, turn_rows(down, rows - down_at))
                 value = jnp.where(row < rows + SENT, value, turn_rows(up, rows + SENT - up_at))
                 state_ref[t, f, z] = value
     last = rows + SENT - 1
 
     def faces_beyond(t, face_x):
-        beyond = down_ref[FIELDS // 2, t]
+        beyond = ghost_ref[2 * pairs, t]
         return [
-            jnp.where(row == last, turn_rows(beyond, last - (z * 4 + SENT)), radial_next(face_x[z]))
+            jnp.where(row == last, turn_rows(beyond, last - z), radial_next(face_x[z]))
             for z in range(PLANES)
         ]
 
@@ -320,7 +349,7 @@
                     below = jnp.where(lane > 0, below, low_done[f][z])
                 mixed.append(keep * value + weight * below)
             done.append(turned)
-            both = jnp.where(row < rows, mixed[0], turn_rows(mixed[1], 4))
+            both = jnp.where(row < rows, mixed[0], turn_rows(mixed[1], rows))
             moved.append(turn_lanes(both, LANES - BELOW))
         if t:
             emit(
@@ -432,34 +461,46 @@
         single = tiles_for(cells)
         double = tiles_for(2 * cells)
         window = tiles_for(BELOW + cells + ABOVE)
-        below = lax.ppermute(state, "gy", [(i, (i + 1) % peers) for i in range(peers)])
-        joined, up, down = pl.pallas_call(
-            lambda *refs: pair_kernel(cells, peers, *refs),
-            out_shape=[
-                array(FIELDS, double),
-                array(FIELDS // 2, window),
-                array(FIELDS // 2 + 1, window),
-            ],
-            in_specs=[smem, vmem, vmem],
-            out_specs=[vmem] * 3,
+        pairs = FIELDS // 2
+
+        def onward(value):
+            return lax.ppermute(value, "gy", [(i, (i + 1) % peers) for i in range(peers)])
+
+        below = onward(state)
+        up, down = pl.pallas_call(
+            lambda *refs: edge_kernel(cells, rows, *refs),
+            out_shape=[array(pairs * single), array(pairs * single + 1)],
+            in_specs=[vmem],
+            out_specs=[vmem] * 2,
             compiler_params=params,
-            name="pair",
-        )(shear_offset, state, below)
+            name="edge",
+        )(state)
         _, _, _, up_hop, down_hop = plan(shear_offset[0], cells, peers)
         branches = [
             lambda u, d, i=i: ghosts(i // 2 + i % 2, i // 2, u, d) for i in range(2 * peers)
         ]
         which = (2 * down_hop + (up_hop - down_hop)) % (2 * peers)
         up, down = lax.switch(which, branches, up, down)
+        up_below, down_below = onward(up), onward(down)
+        block = pl.pallas_call(
+            lambda *refs: join_kernel(cells, peers, *refs),
+            out_shape=array(FIELDS, window),
+            in_specs=[smem, vmem, vmem],
+            out_specs=vmem,
+            scratch_shapes=[scratch(FIELDS, double)],
+            compiler_params=params,
+            name="join",
+        )(shear_offset, state, below)
         block = pl.pallas_call(
             lambda *refs: step_kernel(cells, peers, rows, *refs),
             out_shape=array(FIELDS, single),
-            in_specs=[smem] * 2 + [vmem] * 3,
+            in_specs=[smem] * 2 + [vmem] * 5,
             out_specs=vmem,
-            scratch_shapes=[scratch(window, FIELDS, PLANES)] * 2,
+            scratch_shapes=[scratch(window, FIELDS, PLANES)] * 2
+            + [scratch(FIELDS + 1, double), scratch(FIELDS + 1, window)],
             compiler_params=params,
             name="step",
-        )(shear_offset, frac_index, joined, up, down)
+        )(shear_offset, frac_index, block, up, up_below, down, down_below)
 
         def exchange(value, bits):
             return lax.ppermute(value, "gy", [(i, i ^ bits) for i in range(peers)])

time: 33.5 us -> 33.8 us (level)
  starting transfers between devices: 9.45 us -> 10.9 us
  local copies, waits for them, and re-layouts: 1.56 us -> 0.91 us
  waiting for transfers between devices: 16.2 us -> 15.6 us
    ppermute x1 -> x3, starting transfers between devices: 0.45 us -> 1.66 us  [onward(): lax.ppermute(value, 'gy', [(i, (i + 1) % peers) for i in range(peers)])]
    ppermute x1 -> x3, waiting for transfers between devices: 4.98 us -> 4.1 us  [onward(): lax.ppermute(value, 'gy', [(i, (i + 1) % peers) for i in range(peers)])]
    unnamed x6 -> x8, local copies, waits for them, and re-layouts: 1.56 us -> 0.91 us
  transfers between devices with their start and end apart: 7 -> 9, of which waited for: 6 -> 5; matrix products, arithmetic and copies ran while one was open for 0% -> 0% of each run, Pallas kernels for 3% -> 3%
where the time goes in v6:
time: 33.8 us; the launch traced here: 33.6 us
  waiting for transfers between devices  15.6 us (46%)
  starting transfers between devices  10.9 us (32%)
  Pallas kernels  5.31 us (16%)
  local copies, waits for them, and re-layouts  0.91 us (3%)
  between operations  0.84 us (2%)
    ppermute x2, waiting for transfers between devices, ghosts(): return (lax.ppermute(up, axes, rise), lax.ppermute(down, axes, fall))  7.51 us
    ppermute x2, starting transfers between devices, ghosts(): return (lax.ppermute(up, axes, rise), lax.ppermute(down, axes, fall))  5.61 us
    ppermute x3, waiting for transfers between devices, onward(): lax.ppermute(value, 'gy', [(i, (i + 1) % peers) for i in range(peers)])  4.1 us
    ppermute x4, waiting for transfers between devices, exchange(): return lax.ppermute(value, 'gy', [(i, i ^ bits) for i in range(peers)])  4 us
    ppermute x4, starting transfers between devices, exchange(): return lax.ppermute(value, 'gy', [(i, i ^ bits) for i in range(peers)])  3.62 us
    pallas_call x1, Pallas kernels, shards(): pl.pallas_call(lambda *refs: step_kernel(cells, peers, rows, *refs), out_...  1.92 us
    ppermute x3, starting transfers between devices, onward(): lax.ppermute(value, 'gy', [(i, (i + 1) % peers) for i in range(peers)])  1.66 us
    pallas_call x1, Pallas kernels, shards(): pl.pallas_call(lambda *refs: merge_kernel(cells, peers, rows, *refs), out...  1.29 us
  transfers between devices with their start and end apart: 9, of which 5 were waited for; matrix products, arithmetic and copies ran while one was open for 0% of the time, Pallas kernels for 3%

profile of v6, /device:TPU:0, one launch (start us, length us, event | category | flops | bytes accessed | tf_op | source)
XLA Modules:
  0.0 33.6 jit_solution(15813193995459191254)
XLA Ops:
  0.0 0.5 %collective-permute-start.32 = (f32[8,2,4,508]{3,2,1,0:T(4,128)}, f32[8,2,4,508]{3,2,1,0:T(4,128)S(1)}, u32[]{:S(2)}, u32[]{:S(2)}) collective-permute-start(f32[8,2,4,508]{3,2,1,0:T(4,128)} %refs_0_.6), channel_id=1, source_target_pairs={{0,1},{1,2},{2,3},{3,4},{4,5},{5,6},{6,7},{7,0},{8,9},{9,10},{10,1... | collective-permute-start | bytes 390152 | tf_op jit(solution)/shard_map/ppermute | solution.py:467
  1.2 0.0 copy-start
  1.2 0.9 %copy-done = f32[8,2,4,508]{3,2,1,0:T(4,128)S(1)} copy-done((f32[8,2,4,508]{3,2,1,0:T(4,128)S(1)}, f32[8,2,4,508]{3,2,1,0:T(4,128)}, u32[]{:S(2)}) %copy-start) | copy-done | bytes 130072
  2.1 0.0 copy-start.1
  2.2 13.1 %conditional.1 = (f32[16,8,128]{2,1,0:T(8,128)}, f32[17,8,128]{2,1,0:T(8,128)}) conditional(s32[]{:T(128)} %clamp.3, (f32[16,8,128]{2,1,0:T(8,128)S(1)}, f32[17,8,128]{2,1,0:T(8,128)S(1)}) %edge.1, (f32[16,8,128]{2,1,0:T(8,128)S(1)}, f32[17,8,128]{2,1,0:T(8,128)S(1)}) %edge.1, (f32[16,8,128]{2,1,0:T(8,128)S(1)}, ...), branch_computations={%region_0.1_spmd, %region_1.2_spmd, %region_2.3_spmd, %region_3.4_... | conditional | bytes 540768 | solution.py:483
  2.2 5.6 %collective-permute-start.17 = (f32[17,8,128]{2,1,0:T(8,128)S(1)}, f32[17,8,128]{2,1,0:T(8,128)}, u32[]{:S(2)}, u32[]{:S(2)}) collective-permute-start(f32[17,8,128]{2,1,0:T(8,128)S(1)} %get-tuple-element.86), channel_id=1, source_target_pairs={{0,28},{1,29},{2,30},{3,31},{4,24},{5,25},{6,26},{7,27},{8,0},{9,1... | collective-permute-start | bytes 208904 | tf_op jit(solution)/shard_map/cond/branch_8_fun/ppermute | solution.py:457
  7.8 0.0 collective-permute-start.16
  7.8 7.5 %collective-permute-done.16 = f32[16,8,128]{2,1,0:T(8,128)} collective-permute-done((f32[16,8,128]{2,1,0:T(8,128)S(1)}, f32[16,8,128]{2,1,0:T(8,128)}, u32[]{:S(2)}, u32[]{:S(2)}) %collective-permute-start.16) | collective-permute-done | bytes 65568 | tf_op jit(solution)/shard_map/cond/branch_8_fun/ppermute | solution.py:457
  15.3 0.0 collective-permute-done.17
  15.3 0.1 collective-permute-start.34
  15.4 0.0 copy-start.3
  15.4 1.1 %collective-permute-start.33 = (f32[16,8,128]{2,1,0:T(8,128)}, f32[16,8,128]{2,1,0:T(8,128)S(1)}, u32[]{:S(2)}, u32[]{:S(2)}) collective-permute-start(f32[16,8,128]{2,1,0:T(8,128)} %get-tuple-element.105.refs_3_), channel_id=1, source_target_pairs={{0,1},{1,2},{2,3},{3,4},{4,5},{5,6},{6,7},{7,0},{8,9},{9,10},{10,1... | collective-permute-start | bytes 196616 | tf_op jit(solution)/shard_map/ppermute | solution.py:467
  16.5 0.0 collective-permute-done.32.refs_2_
  16.5 0.0 copy-done.1
  16.5 0.2 join.1.refs_2_
  16.7 0.0 copy-start.2
  16.7 4.1 %collective-permute-done.33.refs_4_ = f32[16,8,128]{2,1,0:T(8,128)S(1)} collective-permute-done((f32[16,8,128]{2,1,0:T(8,128)}, f32[16,8,128]{2,1,0:T(8,128)S(1)}, u32[]{:S(2)}, u32[]{:S(2)}) %collective-permute-start.33) | collective-permute-done | bytes 65568 | tf_op jit(solution)/shard_map/ppermute | solution.py:467
  20.8 0.0 collective-permute-done.34.refs_6_
  20.8 0.0 copy-done.3
  20.9 1.9 %step.1.refs_2_ = f32[8,4,8,128]{3,2,1,0:T(8,128)S(1)} custom-call(s32[1]{0:T(128)} %copy.37.refs_0_, s32[4]{0:T(128)S(1)} %copy-done.3, f32[8,5,8,128]{3,2,1,0:T(8,128)S(1)} %join.1.refs_2_, f32[16,8,128]{2,1,0:T(8,128)} %get-tuple-element.105.refs_3_, f32[16,8,128]{2,1,0:T(8,128)S(1)} %collective-permute-done.33.refs_4_, ...), custom_call_target="tpu_custom_call" | custom-call | tf_op jit(solution)/shard_map/step/pallas_call | solution.py:494
  22.8 0.6 %collective-permute-start.37 = (f32[8,4,8,128]{3,2,1,0:T(8,128)S(1)}, f32[8,4,8,128]{3,2,1,0:T(8,128)S(1)}, u32[]{:S(2)}, u32[]{:S(2)}) collective-permute-start(f32[8,4,8,128]{3,2,1,0:T(8,128)S(1)} %step.1.refs_2_), channel_id=1, source_target_pairs={{0,6},{1,7},{2,4},{3,5},{4,2},{5,3},{6,0},{7,1},{8,14},{9,15},{10,... | collective-permute-start | bytes 393224 | tf_op jit(solution)/shard_map/ppermute | solution.py:506
  23.4 1.1 %collective-permute-start.36 = (f32[8,4,8,128]{3,2,1,0:T(8,128)S(1)}, f32[8,4,8,128]{3,2,1,0:T(8,128)S(1)}, u32[]{:S(2)}, u32[]{:S(2)}) collective-permute-start(f32[8,4,8,128]{3,2,1,0:T(8,128)S(1)} %step.1.refs_2_), channel_id=1, source_target_pairs={{0,4},{1,5},{2,6},{3,7},{4,0},{5,1},{6,2},{7,3},{8,12},{9,13},{10,... | collective-permute-start | bytes 393224 | tf_op jit(solution)/shard_map/ppermute | solution.py:506
  24.5 1.8 %collective-permute-start.35 = (f32[8,4,8,128]{3,2,1,0:T(8,128)S(1)}, f32[8,4,8,128]{3,2,1,0:T(8,128)S(1)}, u32[]{:S(2)}, u32[]{:S(2)}) collective-permute-start(f32[8,4,8,128]{3,2,1,0:T(8,128)S(1)} %step.1.refs_2_), channel_id=1, source_target_pairs={{0,2},{1,3},{2,0},{3,1},{4,6},{5,7},{6,4},{7,5},{8,10},{9,11},{10,... | collective-permute-start | bytes 393224 | tf_op jit(solution)/shard_map/ppermute | solution.py:506
  26.3 2.7 %collective-permute-done.37.refs_5_ = f32[8,4,8,128]{3,2,1,0:T(8,128)S(1)} collective-permute-done((f32[8,4,8,128]{3,2,1,0:T(8,128)S(1)}, f32[8,4,8,128]{3,2,1,0:T(8,128)S(1)}, u32[]{:S(2)}, u32[]{:S(2)}) %collective-permute-start.37) | collective-permute-done | bytes 131104 | tf_op jit(solution)/shard_map/ppermute | solution.py:506
  29.1 0.9 %collective-permute-done.36.refs_4_ = f32[8,4,8,128]{3,2,1,0:T(8,128)S(1)} collective-permute-done((f32[8,4,8,128]{3,2,1,0:T(8,128)S(1)}, f32[8,4,8,128]{3,2,1,0:T(8,128)S(1)}, u32[]{:S(2)}, u32[]{:S(2)}) %collective-permute-start.36) | collective-permute-done | bytes 131104 | tf_op jit(solution)/shard_map/ppermute | solution.py:506
  29.9 0.0 collective-permute-done.35.refs_3_
  29.9 0.0 copy-done.2
  29.9 0.9 %gather.1 = (f32[4,8,4,8,128]{4,3,2,1,0:T(8,128)S(1)}, f32[8,4,8,128]{3,2,1,0:T(8,128)S(1)}) custom-call(s32[1]{0:T(128)} %copy.37.refs_0_, s32[4]{0:T(128)S(1)} %copy-done.2, f32[8,4,8,128]{3,2,1,0:T(8,128)S(1)} %step.1.refs_2_, f32[8,4,8,128]{3,2,1,0:T(8,128)S(1)} %collective-permute-done.35.refs_3_, f32[8,4,8,128]{3,2,1,0:T(8,128)S(1)} %collective-permute-done.36.refs_4_, ...), custom_call_target="tpu_custom_call" | custom-call | tf_op jit(solution)/shard_map/gather/pallas_call | solution.py:509
  30.9 0.1 collective-permute-start.38
  31.0 0.9 %keep.1.refs_2_ = f32[8,4,8,128]{3,2,1,0:T(8,128)S(1)} custom-call(s32[1]{0:T(128)} %copy.37.refs_0_, s32[4]{0:T(128)S(1)} %copy-done.2, f32[4,8,4,8,128]{4,3,2,1,0:T(8,128)S(1)} %get-tuple-element.107.refs_2_), custom_call_target="tpu_custom_call" | custom-call | tf_op jit(solution)/shard_map/keep/pallas_call | solution.py:518
  31.9 0.4 %collective-permute-done.38.refs_3_ = f32[8,4,8,128]{3,2,1,0:T(8,128)S(1)} collective-permute-done((f32[8,4,8,128]{3,2,1,0:T(8,128)S(1)}, f32[8,4,8,128]{3,2,1,0:T(8,128)S(1)}, u32[]{:S(2)}, u32[]{:S(2)}) %collective-permute-start.38) | collective-permute-done | bytes 131104 | tf_op jit(solution)/shard_map/ppermute | solution.py:506
  32.3 1.3 %merge.1 = f32[8,2,4,508]{3,2,1,0:T(4,128)} custom-call(s32[1]{0:T(128)} %copy.37.refs_0_, s32[4]{0:T(128)S(1)} %copy-done.2, f32[8,4,8,128]{3,2,1,0:T(8,128)S(1)} %keep.1.refs_2_, f32[8,4,8,128]{3,2,1,0:T(8,128)S(1)} %collective-permute-done.38.refs_3_), custom_call_target="tpu_custom_call" | custom-call | tf_op jit(solution)/shard_map/merge/pallas_call | solution.py:526
  (1 shorter events, 0.0 us)
Async XLA Ops:
  0.0 16.5 %collective-permute-start.32 = (f32[8,2,4,508]{3,2,1,0:T(4,128)}, f32[8,2,4,508]{3,2,1,0:T(4,128)S(1)}, u32[]{:S(2)}, u32[]{:S(2)}) collective-permute-start(f32[8,2,4,508]{3,2,1,0:T(4,128)} %refs_0_.6), channel_id=1, source_target_pairs={{0,1},{1,2},{2,3},{3,4},{4,5},{5,6},{6,7},{7,0},{8,9},{9,10},{10,1... | collective-permute-start | bytes 390152 | tf_op jit(solution)/shard_map/ppermute | solution.py:467
  1.2 0.9 %copy-start = (f32[8,2,4,508]{3,2,1,0:T(4,128)S(1)}, f32[8,2,4,508]{3,2,1,0:T(4,128)}, u32[]{:S(2)}) copy-start(f32[8,2,4,508]{3,2,1,0:T(4,128)} %refs_0_.6) | copy-start | bytes 390148
  2.1 14.4 %copy-start.1 = (f32[8,2,4,508]{3,2,1,0:T(4,128)S(1)}, f32[8,2,4,508]{3,2,1,0:T(4,128)}, u32[]{:S(2)}) copy-start(f32[8,2,4,508]{3,2,1,0:T(4,128)} %refs_0_.6) | copy-start | bytes 390148
  2.2 13.1 %collective-permute-start.17 = (f32[17,8,128]{2,1,0:T(8,128)S(1)}, f32[17,8,128]{2,1,0:T(8,128)}, u32[]{:S(2)}, u32[]{:S(2)}) collective-permute-start(f32[17,8,128]{2,1,0:T(8,128)S(1)} %get-tuple-element.86), channel_id=1, source_target_pairs={{0,28},{1,29},{2,30},{3,31},{4,24},{5,25},{6,26},{7,27},{8,0},{9,1... | collective-permute-start | bytes 208904 | tf_op jit(solution)/shard_map/cond/branch_8_fun/ppermute | solution.py:457
  7.8 7.5 %collective-permute-start.16 = (f32[16,8,128]{2,1,0:T(8,128)S(1)}, f32[16,8,128]{2,1,0:T(8,128)}, u32[]{:S(2)}, u32[]{:S(2)}) collective-permute-start(f32[16,8,128]{2,1,0:T(8,128)S(1)} %get-tuple-element.85), channel_id=1, source_target_pairs={{0,8},{1,9},{2,10},{3,11},{4,12},{5,13},{6,14},{7,15},{8,16},{9,17... | collective-permute-start | bytes 196616 | tf_op jit(solution)/shard_map/cond/branch_8_fun/ppermute | solution.py:457
  15.3 5.6 %collective-permute-start.34 = (f32[17,8,128]{2,1,0:T(8,128)}, f32[17,8,128]{2,1,0:T(8,128)S(1)}, u32[]{:S(2)}, u32[]{:S(2)}) collective-permute-start(f32[17,8,128]{2,1,0:T(8,128)} %get-tuple-element.106.refs_5_), channel_id=1, source_target_pairs={{0,1},{1,2},{2,3},{3,4},{4,5},{5,6},{6,7},{7,0},{8,9},{9,10},{10,1... | collective-permute-start | bytes 208904 | tf_op jit(solution)/shard_map/ppermute | solution.py:467
  15.4 5.4 %copy-start.3 = (s32[4]{0:T(128)S(1)}, s32[4]{0:T(128)}, u32[]{:S(2)}) copy-start(s32[4]{0:T(128)} %refs_1_.6) | copy-start | bytes 52
  15.4 5.4 %collective-permute-start.33 = (f32[16,8,128]{2,1,0:T(8,128)}, f32[16,8,128]{2,1,0:T(8,128)S(1)}, u32[]{:S(2)}, u32[]{:S(2)}) collective-permute-start(f32[16,8,128]{2,1,0:T(8,128)} %get-tuple-element.105.refs_3_), channel_id=1, source_target_pairs={{0,1},{1,2},{2,3},{3,4},{4,5},{5,6},{6,7},{7,0},{8,9},{9,10},{10,1... | collective-permute-start | bytes 196616 | tf_op jit(solution)/shard_map/ppermute | solution.py:467
  16.7 13.2 %copy-start.2 = (s32[4]{0:T(128)S(1)}, s32[4]{0:T(128)}, u32[]{:S(2)}) copy-start(s32[4]{0:T(128)} %refs_1_.9) | copy-start | bytes 52
  22.8 6.3 %collective-permute-start.37 = (f32[8,4,8,128]{3,2,1,0:T(8,128)S(1)}, f32[8,4,8,128]{3,2,1,0:T(8,128)S(1)}, u32[]{:S(2)}, u32[]{:S(2)}) collective-permute-start(f32[8,4,8,128]{3,2,1,0:T(8,128)S(1)} %step.1.refs_2_), channel_id=1, source_target_pairs={{0,6},{1,7},{2,4},{3,5},{4,2},{5,3},{6,0},{7,1},{8,14},{9,15},{10,... | collective-permute-start | bytes 393224 | tf_op jit(solution)/shard_map/ppermute | solution.py:506
  23.4 6.5 %collective-permute-start.36 = (f32[8,4,8,128]{3,2,1,0:T(8,128)S(1)}, f32[8,4,8,128]{3,2,1,0:T(8,128)S(1)}, u32[]{:S(2)}, u32[]{:S(2)}) collective-permute-start(f32[8,4,8,128]{3,2,1,0:T(8,128)S(1)} %step.1.refs_2_), channel_id=1, source_target_pairs={{0,4},{1,5},{2,6},{3,7},{4,0},{5,1},{6,2},{7,3},{8,12},{9,13},{10,... | collective-permute-start | bytes 393224 | tf_op jit(solution)/shard_map/ppermute | solution.py:506
  24.5 5.4 %collective-permute-start.35 = (f32[8,4,8,128]{3,2,1,0:T(8,128)S(1)}, f32[8,4,8,128]{3,2,1,0:T(8,128)S(1)}, u32[]{:S(2)}, u32[]{:S(2)}) collective-permute-start(f32[8,4,8,128]{3,2,1,0:T(8,128)S(1)} %step.1.refs_2_), channel_id=1, source_target_pairs={{0,2},{1,3},{2,0},{3,1},{4,6},{5,7},{6,4},{7,5},{8,10},{9,11},{10,... | collective-permute-start | bytes 393224 | tf_op jit(solution)/shard_map/ppermute | solution.py:506
  30.9 1.4 %collective-permute-start.38 = (f32[8,4,8,128]{3,2,1,0:T(8,128)S(1)}, f32[8,4,8,128]{3,2,1,0:T(8,128)S(1)}, u32[]{:S(2)}, u32[]{:S(2)}) collective-permute-start(f32[8,4,8,128]{3,2,1,0:T(8,128)S(1)} %get-tuple-element.108), channel_id=1, source_target_pairs={{0,1},{1,0},{2,3},{3,2},{4,5},{5,4},{6,7},{7,6},{8,9},{9,8},{10,11... | collective-permute-start | bytes 393224 | tf_op jit(solution)/shard_map/ppermute | solution.py:506

commit v7 on v5

--- a/solution.py
+++ b/solution.py
@@ -20,6 +20,7 @@
 FACE_X = 5
 BELOW = 3
 ABOVE = 3
+TAIL = 4
 SENT = 2
 HALF_STEP = 0.5 * TIME_STEP
 DIFFUSE = 0.5 * MAX_SPEED * TIME_STEP
@@ -67,7 +68,25 @@
     return own, up, down, up_hop, down_hop
 
 
-def pair_kernel(cells, peers, shear_ref, state_ref, below_ref, joined_ref, up_ref, down_ref):
+def block_tiles(ref, f, cells):
+    value = jnp.concatenate([ref[f, z] for z in range(PLANES)], axis=0)
+    tiles = []
+    for i in range(0, cells, LANES):
+        tile = value[:, i : min(i + LANES, cells)]
+        spare = LANES - tile.shape[1]
+        if spare:
+            tile = jnp.concatenate([tile, jnp.zeros((SUBLANES, spare), tile.dtype)], axis=1)
+        tiles.append(tile)
+    return tiles
+
+
+def lay_kernel(cells, state_ref, out_ref):
+    for f in range(FIELDS):
+        for t, tile in enumerate(block_tiles(state_ref, f, cells)):
+            out_ref[f, t] = turn_lanes(tile, cells % LANES)
+
+
+def pair_kernel(cells, peers, rows, shear_ref, upper_ref, below_ref, joined_ref, up_ref, down_ref):
     place = lax.axis_index("gx")
     places = lax.axis_size("gx")
     own, up, down, _, _ = plan(shear_ref[0], cells, peers)
@@ -77,44 +96,43 @@
     row = row_index()
     single = tiles_for(cells)
     gap = cells % LANES
-    double = joined_ref.shape[1]
-    window = up_ref.shape[1]
-
-    def tiles_of(ref, f):
-        both = [ref[f, z] for z in range(PLANES)]
-        value = jnp.concatenate(both, axis=0)
-        return [value[:, i * LANES : min((i + 1) * LANES, cells)] for i in range(single)]
-
-    def widened(tile):
-        spare = LANES - tile.shape[1]
-        if spare == 0:
-            return tile
-        return jnp.concatenate([tile, jnp.zeros((SUBLANES, spare), tile.dtype)], axis=1)
-
-    for f in range(FIELDS):
-        lower = [widened(t) for t in tiles_of(below_ref, f)]
-        upper = [turn_lanes(widened(t), gap) for t in tiles_of(state_ref, f)]
-        for i in range(single):
-            if i < single - 1:
-                joined_ref[f, i] = lower[i]
-            else:
-                joined_ref[f, i] = jnp.where(lane < gap, lower[i], upper[0])
-        for i in range(single, double):
-            k = i - single
-            joined_ref[f, i] = jnp.where(lane < gap, upper[k], upper[min(k + 1, single - 1)])
-
-    def cut(f, start):
-        return cut_window(joined_ref, f, start, window)
-
-    late = row % 4 >= SENT
-    for pair in range(FIELDS // 2):
-        ups = [cut(2 * pair + i, up) for i in range(2)]
-        downs = [cut(2 * pair + i, down) for i in range(2)]
-        for t in range(window):
-            up_ref[pair, t] = jnp.where(late, ups[0][t], turn_rows(ups[1][t], -SENT))
-            down_ref[pair, t] = jnp.where(late, turn_rows(downs[1][t], SENT), downs[0][t])
-    for t, value in enumerate(cut(FACE_X, down)):
-        down_ref[FIELDS // 2, t] = value
+    window = single + 1
+    for f in range(FIELDS):
+        lower = block_tiles(below_ref, f, cells)
+        upper = [upper_ref[f, t] for t in range(single)]
+        for i in range(single - 1):
+            joined_ref[f, i] = lower[i]
+        joined_ref[f, single - 1] = jnp.where(lane < gap, lower[-1], upper[0])
+        for k in range(single):
+            following = upper[min(k + 1, single - 1)]
+            joined_ref[f, single + k] = jnp.where(lane < gap, upper[k], following)
+
+    late = row % rows >= SENT
+    pairs = FIELDS // 2
+    up_tail = down_tail = jnp.zeros((SUBLANES, LANES), jnp.float32)
+
+    def tail(tile, index, so_far):
+        return jnp.where(lane // TAIL == index, turn_lanes(tile, index * TAIL), so_far)
+
+    for pair in range(pairs):
+        ups = [cut_window(joined_ref, 2 * pair + i, up, window) for i in range(2)]
+        downs = [cut_window(joined_ref, 2 * pair + i, down, window) for i in range(2)]
+        ups = [jnp.where(late, a, turn_rows(b, -SENT)) for a, b in zip(*ups)]
+        downs = [jnp.where(late, turn_rows(b, SENT), a) for a, b in zip(*downs)]
+        for t in range(single):
+            up_ref[pair * single + t] = ups[t]
+            down_ref[pair * single + t] = downs[t]
+        up_tail = tail(ups[single], pair, up_tail)
+        down_tail = tail(downs[single], pair, down_tail)
+    faces = jnp.zeros((SUBLANES, LANES), jnp.float32)
+    tiles = cut_window(joined_ref, FACE_X, down, window)
+    for t in range(single):
+        for z in range(PLANES):
+            at = t * PLANES + z
+            faces = jnp.where(row == at, turn_rows(tiles[t], at - (z * rows + SENT)), faces)
+    down_ref[pairs * single] = faces
+    up_ref[pairs * single] = up_tail
+    down_ref[pairs * single + 1] = tail(tiles[single], pairs, down_tail)
 
 
 def cut_window(joined_ref, f, start, count):
@@ -237,34 +255,52 @@
 
 def step_kernel(
     cells, peers, rows,
-    shear_ref, frac_ref, joined_ref, up_ref, down_ref, out_ref, state_ref, mid_ref,
+    shear_ref, frac_ref, joined_ref, up_hbm, down_hbm,
+    out_ref, state_ref, mid_ref, up_ref, down_ref, up_sem, down_sem,
 ):
+    up_copy = pltpu.make_async_copy(up_hbm, up_ref, up_sem)
+    down_copy = pltpu.make_async_copy(down_hbm, down_ref, down_sem)
+    up_copy.start()
+    down_copy.start()
     own = plan(shear_ref[0], cells, peers)[0]
     lane = lane_index()
     row = row_index()
-    window = up_ref.shape[1]
     single = tiles_for(cells)
-
+    window = single + 1
+    pairs = FIELDS // 2
+
+    for f in range(FIELDS):
+        for t, tile in enumerate(cut_window(joined_ref, f, own, window)):
+            for z in range(PLANES):
+                state_ref[t, f, z] = turn_rows(tile, -z * rows)
+    up_copy.wait()
+    down_copy.wait()
     for f in range(FIELDS):
         pair, second = divmod(f, 2)
-        for t, tile in enumerate(cut_window(joined_ref, f, own, window)):
-            up = up_ref[pair, t]
-            down = down_ref[pair, t]
+        for t in range(window):
+            if t < single:
+                up = up_ref[pair * single + t]
+                down = down_ref[pair * single + t]
+            else:
+                back = (LANES - pair * TAIL) % LANES
+                up = turn_lanes(up_ref[pairs * single], back)
+                down = turn_lanes(down_ref[pairs * single + 1], back)
             for z in range(PLANES):
-                up_at = z * 4 + (0 if second else SENT)
-                down_at = z * 4 + (SENT if second else 0)
-                value = turn_rows(tile, -z * 4)
+                up_at = z * rows + (0 if second else SENT)
+                down_at = z * rows + (SENT if second else 0)
+                value = state_ref[t, f, z]
                 value = jnp.where(row < rows, value, turn_rows(down, rows - down_at))
                 value = jnp.where(row < rows + SENT, value, turn_rows(up, rows + SENT - up_at))
                 state_ref[t, f, z] = value
     last = rows + SENT - 1
 
     def faces_beyond(t, face_x):
-        beyond = down_ref[FIELDS // 2, t]
-        return [
-            jnp.where(row == last, turn_rows(beyond, last - (z * 4 + SENT)), radial_next(face_x[z]))
-            for z in range(PLANES)
-        ]
+        if t < single:
+            beyond = [turn_rows(down_ref[pairs * single], last - t * PLANES - z) for z in range(PLANES)]
+        else:
+            tile = turn_lanes(down_ref[pairs * single + 1], LANES - pairs * TAIL)
+            beyond = [turn_rows(tile, last - (z * rows + SENT)) for z in range(PLANES)]
+        return [jnp.where(row == last, b, radial_next(face)) for b, face in zip(beyond, face_x)]
 
     def terms(ref, t, count, beyond):
         state = [[ref[t, f, z] for z in range(PLANES)] for f in range(FIELDS)]
@@ -320,7 +356,7 @@
                     below = jnp.where(lane > 0, below, low_done[f][z])
                 mixed.append(keep * value + weight * below)
             done.append(turned)
-            both = jnp.where(row < rows, mixed[0], turn_rows(mixed[1], 4))
+            both = jnp.where(row < rows, mixed[0], turn_rows(mixed[1], rows))
             moved.append(turn_lanes(both, LANES - BELOW))
         if t:
             emit(
@@ -384,7 +420,9 @@
     turned_rows(cells, peers, rows, shift_ref, own, part, part, block_ref, out_ref)
 
 
-def merge_kernel(cells, peers, rows, shear_ref, shift_ref, mine_ref, other_ref, out_ref):
+def merge_kernel(
+    cells, peers, rows, shear_ref, shift_ref, mine_ref, other_ref, out_hbm, out_ref, out_sem
+):
     part = lax.axis_index("gy")
     own = plan(shear_ref[0], cells, peers)[0]
     row = row_index() % rows
@@ -402,12 +440,16 @@
         value = jnp.concatenate(tiles, axis=1)[:, :cells]
         for z in range(PLANES):
             out_ref[f, z] = value[z * rows : (z + 1) * rows]
+        pltpu.make_async_copy(out_ref.at[f], out_hbm.at[f], out_sem.at[f]).start()
+    for f in range(FIELDS):
+        pltpu.make_async_copy(out_ref.at[f], out_hbm.at[f], out_sem.at[f]).wait()
 
 
 def solution(mesh):
     places, peers = (mesh.shape["gx"], mesh.shape["gy"])
     smem = pl.BlockSpec(memory_space=pltpu.SMEM)
     vmem = pl.BlockSpec(memory_space=pltpu.VMEM)
+    hbm = pl.BlockSpec(memory_space=pltpu.HBM)
     params = pltpu.CompilerParams(vmem_limit_bytes=8 * 2**20)
     axes = ("gx", "gy")
 
@@ -425,7 +467,8 @@
     def ghosts(up_hop, down_hop, up, down):
         rise = [(device(x, y), device(x + 1, y + up_hop * (x == places - 1))) for x, y in devices]
         fall = [(device(x, y), device(x - 1, y - down_hop * (x == 0))) for x, y in devices]
-        return lax.ppermute(up, axes, rise), lax.ppermute(down, axes, fall)
+        up = lax.ppermute(up, axes, rise)
+        return up, lax.ppermute(down, axes, fall)
 
     def shards(state, shear_offset, remap_shift, frac_index):
         rows, cells = state.shape[2:]
@@ -433,18 +476,23 @@
         double = tiles_for(2 * cells)
         window = tiles_for(BELOW + cells + ABOVE)
         below = lax.ppermute(state, "gy", [(i, (i + 1) % peers) for i in range(peers)])
+        upper = pl.pallas_call(
+            lambda *refs: lay_kernel(cells, *refs),
+            out_shape=array(FIELDS, single),
+            in_specs=[vmem],
+            out_specs=vmem,
+            compiler_params=params,
+            name="lay",
+        )(state)
+        edge = FIELDS // 2 * single + 2
         joined, up, down = pl.pallas_call(
-            lambda *refs: pair_kernel(cells, peers, *refs),
-            out_shape=[
-                array(FIELDS, double),
-                array(FIELDS // 2, window),
-                array(FIELDS // 2 + 1, window),
-            ],
+            lambda *refs: pair_kernel(cells, peers, rows, *refs),
+            out_shape=[array(FIELDS, double), array(edge), array(edge)],
             in_specs=[smem, vmem, vmem],
             out_specs=[vmem] * 3,
             compiler_params=params,
             name="pair",
-        )(shear_offset, state, below)
+        )(shear_offset, upper, below)
         _, _, _, up_hop, down_hop = plan(shear_offset[0], cells, peers)
         branches = [
             lambda u, d, i=i: ghosts(i // 2 + i % 2, i // 2, u, d) for i in range(2 * peers)
@@ -454,9 +502,11 @@
         block = pl.pallas_call(
             lambda *refs: step_kernel(cells, peers, rows, *refs),
             out_shape=array(FIELDS, single),
-            in_specs=[smem] * 2 + [vmem] * 3,
+            in_specs=[smem] * 2 + [vmem] + [hbm] * 2,
             out_specs=vmem,
-            scratch_shapes=[scratch(window, FIELDS, PLANES)] * 2,
+            scratch_shapes=[scratch(window, FIELDS, PLANES)] * 2
+            + [scratch(edge), scratch(edge)]
+            + [pltpu.SemaphoreType.DMA] * 2,
             compiler_params=params,
             name="step",
         )(shear_offset, frac_index, joined, up, down)
@@ -486,7 +536,11 @@
             lambda *refs: merge_kernel(cells, peers, rows, *refs),
             out_shape=jax.ShapeDtypeStruct(state.shape, jnp.float32),
             in_specs=[smem] * 2 + [vmem] * 2,
-            out_specs=vmem,
+            out_specs=hbm,
+            scratch_shapes=[
+                pltpu.VMEM(state.shape, jnp.float32),
+                pltpu.SemaphoreType.DMA((FIELDS,)),
+            ],
             compiler_params=params,
             name="merge",
         )(shear_offset, remap_shift, mine, other)

time: 33.5 us -> 30.6 us (0.913)
  waiting for transfers between devices: 16.2 us -> 13.6 us
  starting transfers between devices: 9.45 us -> 8.58 us
  Pallas kernels: 5.31 us -> 5.89 us
    ppermute x2, waiting for transfers between devices: 7.24 us -> 3.93 us  [the longest x1 2.83 us: ghosts(): up = lax.ppermute(up, axes, rise)]
    ppermute x4, waiting for transfers between devices: 3.94 us -> 5.68 us  [exchange(): return lax.ppermute(value, 'gy', [(i, i ^ bits) for i in range(peers)])]
    ppermute x1, waiting for transfers between devices: 4.98 us -> 3.96 us  [shards(): lax.ppermute(state, 'gy', [(i, (i + 1) % peers) for i in range(peers)])]
    ppermute x2, starting transfers between devices: 5.37 us -> 4.5 us  [the longest x1 2.39 us: ghosts(): up = lax.ppermute(up, axes, rise)]
    pallas_call x1, Pallas kernels: 1.89 us -> 2.36 us  [shards(): pl.pallas_call(lambda *refs: step_kernel(cells, peers, rows, *refs), out_...]
where the time goes in v7:
time: 30.6 us; the launch traced here: 30.4 us
  waiting for transfers between devices  13.6 us (44%)
  starting transfers between devices  8.58 us (28%)
  Pallas kernels  5.89 us (19%)
  local copies, waits for them, and re-layouts  1.56 us (5%)
  between operations  0.83 us (3%)
    ppermute x4, waiting for transfers between devices, exchange(): return lax.ppermute(value, 'gy', [(i, i ^ bits) for i in range(peers)])  5.68 us
    ppermute x1, waiting for transfers between devices, shards(): lax.ppermute(state, 'gy', [(i, (i + 1) % peers) for i in range(peers)])  3.96 us
    ppermute x4, starting transfers between devices, exchange(): return lax.ppermute(value, 'gy', [(i, i ^ bits) for i in range(peers)])  3.62 us
    ppermute x1, waiting for transfers between devices, ghosts(): up = lax.ppermute(up, axes, rise)  2.83 us
    ppermute x1, starting transfers between devices, ghosts(): up = lax.ppermute(up, axes, rise)  2.39 us
    pallas_call x1, Pallas kernels, shards(): pl.pallas_call(lambda *refs: step_kernel(cells, peers, rows, *refs), out_...  2.36 us
    ppermute x1, starting transfers between devices, ghosts(): return (up, lax.ppermute(down, axes, fall))  2.11 us
    unnamed x6, local copies, waits for them, and re-layouts  1.56 us
  transfers between devices with their start and end apart: 7, of which 6 were waited for; matrix products, arithmetic and copies ran while one was open for 0% of the time, Pallas kernels for 3%

profile of v7, /device:TPU:0, one launch (start us, length us, event | category | flops | bytes accessed | tf_op | source)
XLA Modules:
  0.0 30.4 jit_solution(2194669793348710468)
XLA Ops:
  0.0 0.5 %collective-permute-start.32 = (f32[8,2,4,508]{3,2,1,0:T(4,128)}, f32[8,2,4,508]{3,2,1,0:T(4,128)S(1)}, u32[]{:S(2)}, u32[]{:S(2)}) collective-permute-start(f32[8,2,4,508]{3,2,1,0:T(4,128)} %refs_0_.6), channel_id=1, source_target_pairs={{0,1},{1,2},{2,3},{3,4},{4,5},{5,6},{6,7},{7,0},{8,9},{9,10},{10,1... | collective-permute-start | bytes 390152 | tf_op jit(solution)/shard_map/ppermute | solution.py:478
  1.2 0.0 copy-start
  1.2 0.9 %copy-done = f32[8,2,4,508]{3,2,1,0:T(4,128)S(1)} copy-done((f32[8,2,4,508]{3,2,1,0:T(4,128)S(1)}, f32[8,2,4,508]{3,2,1,0:T(4,128)}, u32[]{:S(2)}) %copy-start) | copy-done | bytes 130072
  2.1 0.1 lay.1.refs_1_
  2.2 4.0 %collective-permute-done.32.refs_2_ = f32[8,2,4,508]{3,2,1,0:T(4,128)S(1)} collective-permute-done((f32[8,2,4,508]{3,2,1,0:T(4,128)}, f32[8,2,4,508]{3,2,1,0:T(4,128)S(1)}, u32[]{:S(2)}, u32[]{:S(2)}) %collective-permute-start.32) | collective-permute-done | bytes 130080 | tf_op jit(solution)/shard_map/ppermute | solution.py:478
  6.2 0.2 pair.1
  6.4 8.5 %conditional.1 = (f32[18,8,128]{2,1,0:T(8,128)}, f32[18,8,128]{2,1,0:T(8,128)}) conditional(s32[]{:T(128)} %clamp.3, (f32[18,8,128]{2,1,0:T(8,128)S(1)}, f32[18,8,128]{2,1,0:T(8,128)S(1)}) %tuple.69, (f32[18,8,128]{2,1,0:T(8,128)S(1)}, f32[18,8,128]{2,1,0:T(8,128)S(1)}) %tuple.69, (f32[18,8,128]{2,1,0:T(8,128)S(1)}, ...), branch_computations={%region_0.1_spmd, %region_1.2_spmd, %region_2.3_spmd, %region_3.4_... | conditional | bytes 589920 | solution.py:501
  6.5 2.4 %collective-permute-start.20 = (f32[18,8,128]{2,1,0:T(8,128)S(1)}, f32[18,8,128]{2,1,0:T(8,128)}, u32[]{:S(2)}, u32[]{:S(2)}) collective-permute-start(f32[18,8,128]{2,1,0:T(8,128)S(1)} %get-tuple-element.89), channel_id=1, source_target_pairs={{0,8},{1,9},{2,10},{3,11},{4,12},{5,13},{6,14},{7,15},{8,16},{9,17... | collective-permute-start | bytes 221192 | tf_op jit(solution)/shard_map/cond/branch_10_fun/ppermute | solution.py:470
  8.8 2.1 %collective-permute-start.21 = (f32[18,8,128]{2,1,0:T(8,128)S(1)}, f32[18,8,128]{2,1,0:T(8,128)}, u32[]{:S(2)}, u32[]{:S(2)}) collective-permute-start(f32[18,8,128]{2,1,0:T(8,128)S(1)} %get-tuple-element.90), channel_id=1, source_target_pairs={{0,27},{1,28},{2,29},{3,30},{4,31},{5,24},{6,25},{7,26},{8,0},{9,1... | collective-permute-start | bytes 221192 | tf_op jit(solution)/shard_map/cond/branch_10_fun/ppermute | solution.py:471
  11.0 2.8 %collective-permute-done.20 = f32[18,8,128]{2,1,0:T(8,128)} collective-permute-done((f32[18,8,128]{2,1,0:T(8,128)S(1)}, f32[18,8,128]{2,1,0:T(8,128)}, u32[]{:S(2)}, u32[]{:S(2)}) %collective-permute-start.20) | collective-permute-done | bytes 73760 | tf_op jit(solution)/shard_map/cond/branch_10_fun/ppermute | solution.py:470
  13.8 1.1 %collective-permute-done.21 = f32[18,8,128]{2,1,0:T(8,128)} collective-permute-done((f32[18,8,128]{2,1,0:T(8,128)S(1)}, f32[18,8,128]{2,1,0:T(8,128)}, u32[]{:S(2)}, u32[]{:S(2)}) %collective-permute-start.21) | collective-permute-done | bytes 73760 | tf_op jit(solution)/shard_map/cond/branch_10_fun/ppermute | solution.py:471
  14.9 0.0 copy-start.2
  14.9 0.7 %copy-done.2 = s32[4]{0:T(128)S(1)} copy-done((s32[4]{0:T(128)S(1)}, s32[4]{0:T(128)}, u32[]{:S(2)}) %copy-start.2) | copy-done | bytes 40
  15.5 0.0 copy-start.1
  15.5 2.4 %step.1.refs_2_ = f32[8,4,8,128]{3,2,1,0:T(8,128)S(1)} custom-call(s32[1]{0:T(128)} %copy.37.refs_0_, s32[4]{0:T(128)S(1)} %copy-done.2, f32[8,8,8,128]{3,2,1,0:T(8,128)S(1)} %get-tuple-element.108.refs_2_, f32[18,8,128]{2,1,0:T(8,128)} %get-tuple-element.111.refs_3_, f32[18,8,128]{2,1,0:T(8,128)} %get-tuple-element.112.refs_4_), custom_call_target="tpu_custom_call" | custom-call | tf_op jit(solution)/shard_map/step/pallas_call | solution.py:502
  17.9 1.9 %collective-permute-start.35 = (f32[8,4,8,128]{3,2,1,0:T(8,128)S(1)}, f32[8,4,8,128]{3,2,1,0:T(8,128)S(1)}, u32[]{:S(2)}, u32[]{:S(2)}) collective-permute-start(f32[8,4,8,128]{3,2,1,0:T(8,128)S(1)} %step.1.refs_2_), channel_id=1, source_target_pairs={{0,6},{1,7},{2,4},{3,5},{4,2},{5,3},{6,0},{7,1},{8,14},{9,15},{10,... | collective-permute-start | bytes 393224 | tf_op jit(solution)/shard_map/ppermute | solution.py:515
  19.8 0.7 %collective-permute-start.34 = (f32[8,4,8,128]{3,2,1,0:T(8,128)S(1)}, f32[8,4,8,128]{3,2,1,0:T(8,128)S(1)}, u32[]{:S(2)}, u32[]{:S(2)}) collective-permute-start(f32[8,4,8,128]{3,2,1,0:T(8,128)S(1)} %step.1.refs_2_), channel_id=1, source_target_pairs={{0,4},{1,5},{2,6},{3,7},{4,0},{5,1},{6,2},{7,3},{8,12},{9,13},{10,... | collective-permute-start | bytes 393224 | tf_op jit(solution)/shard_map/ppermute | solution.py:515
  20.5 1.0 %collective-permute-start.33 = (f32[8,4,8,128]{3,2,1,0:T(8,128)S(1)}, f32[8,4,8,128]{3,2,1,0:T(8,128)S(1)}, u32[]{:S(2)}, u32[]{:S(2)}) collective-permute-start(f32[8,4,8,128]{3,2,1,0:T(8,128)S(1)} %step.1.refs_2_), channel_id=1, source_target_pairs={{0,2},{1,3},{2,0},{3,1},{4,6},{5,7},{6,4},{7,5},{8,10},{9,11},{10,... | collective-permute-start | bytes 393224 | tf_op jit(solution)/shard_map/ppermute | solution.py:515
  21.5 3.8 %collective-permute-done.35.refs_5_ = f32[8,4,8,128]{3,2,1,0:T(8,128)S(1)} collective-permute-done((f32[8,4,8,128]{3,2,1,0:T(8,128)S(1)}, f32[8,4,8,128]{3,2,1,0:T(8,128)S(1)}, u32[]{:S(2)}, u32[]{:S(2)}) %collective-permute-start.35) | collective-permute-done | bytes 131104 | tf_op jit(solution)/shard_map/ppermute | solution.py:515
  25.3 1.5 %collective-permute-done.34.refs_4_ = f32[8,4,8,128]{3,2,1,0:T(8,128)S(1)} collective-permute-done((f32[8,4,8,128]{3,2,1,0:T(8,128)S(1)}, f32[8,4,8,128]{3,2,1,0:T(8,128)S(1)}, u32[]{:S(2)}, u32[]{:S(2)}) %collective-permute-start.34) | collective-permute-done | bytes 131104 | tf_op jit(solution)/shard_map/ppermute | solution.py:515
  26.7 0.0 collective-permute-done.33.refs_3_
  26.7 0.0 copy-done.1
  26.7 0.9 %gather.1 = (f32[4,8,4,8,128]{4,3,2,1,0:T(8,128)S(1)}, f32[8,4,8,128]{3,2,1,0:T(8,128)S(1)}) custom-call(s32[1]{0:T(128)} %copy.37.refs_0_, s32[4]{0:T(128)S(1)} %copy-done.1, f32[8,4,8,128]{3,2,1,0:T(8,128)S(1)} %step.1.refs_2_, f32[8,4,8,128]{3,2,1,0:T(8,128)S(1)} %collective-permute-done.33.refs_3_, f32[8,4,8,128]{3,2,1,0:T(8,128)S(1)} %collective-permute-done.34.refs_4_, ...), custom_call_target="tpu_custom_call" | custom-call | tf_op jit(solution)/shard_map/gather/pallas_call | solution.py:518
  27.7 0.1 collective-permute-start.36
  27.8 0.9 %keep.1.refs_2_ = f32[8,4,8,128]{3,2,1,0:T(8,128)S(1)} custom-call(s32[1]{0:T(128)} %copy.37.refs_0_, s32[4]{0:T(128)S(1)} %copy-done.1, f32[4,8,4,8,128]{4,3,2,1,0:T(8,128)S(1)} %get-tuple-element.113.refs_2_), custom_call_target="tpu_custom_call" | custom-call | tf_op jit(solution)/shard_map/keep/pallas_call | solution.py:527
  28.7 0.4 %collective-permute-done.36.refs_3_ = f32[8,4,8,128]{3,2,1,0:T(8,128)S(1)} collective-permute-done((f32[8,4,8,128]{3,2,1,0:T(8,128)S(1)}, f32[8,4,8,128]{3,2,1,0:T(8,128)S(1)}, u32[]{:S(2)}, u32[]{:S(2)}) %collective-permute-start.36) | collective-permute-done | bytes 131104 | tf_op jit(solution)/shard_map/ppermute | solution.py:515
  29.1 1.3 %merge.1 = f32[8,2,4,508]{3,2,1,0:T(4,128)} custom-call(s32[1]{0:T(128)} %copy.37.refs_0_, s32[4]{0:T(128)S(1)} %copy-done.1, f32[8,4,8,128]{3,2,1,0:T(8,128)S(1)} %keep.1.refs_2_, f32[8,4,8,128]{3,2,1,0:T(8,128)S(1)} %collective-permute-done.36.refs_3_), custom_call_target="tpu_custom_call" | custom-call | tf_op jit(solution)/shard_map/merge/pallas_call | solution.py:535
Async XLA Ops:
  0.0 6.2 %collective-permute-start.32 = (f32[8,2,4,508]{3,2,1,0:T(4,128)}, f32[8,2,4,508]{3,2,1,0:T(4,128)S(1)}, u32[]{:S(2)}, u32[]{:S(2)}) collective-permute-start(f32[8,2,4,508]{3,2,1,0:T(4,128)} %refs_0_.6), channel_id=1, source_target_pairs={{0,1},{1,2},{2,3},{3,4},{4,5},{5,6},{6,7},{7,0},{8,9},{9,10},{10,1... | collective-permute-start | bytes 390152 | tf_op jit(solution)/shard_map/ppermute | solution.py:478
  1.2 0.9 %copy-start = (f32[8,2,4,508]{3,2,1,0:T(4,128)S(1)}, f32[8,2,4,508]{3,2,1,0:T(4,128)}, u32[]{:S(2)}) copy-start(f32[8,2,4,508]{3,2,1,0:T(4,128)} %refs_0_.6) | copy-start | bytes 390148
  6.5 7.3 %collective-permute-start.20 = (f32[18,8,128]{2,1,0:T(8,128)S(1)}, f32[18,8,128]{2,1,0:T(8,128)}, u32[]{:S(2)}, u32[]{:S(2)}) collective-permute-start(f32[18,8,128]{2,1,0:T(8,128)S(1)} %get-tuple-element.89), channel_id=1, source_target_pairs={{0,8},{1,9},{2,10},{3,11},{4,12},{5,13},{6,14},{7,15},{8,16},{9,17... | collective-permute-start | bytes 221192 | tf_op jit(solution)/shard_map/cond/branch_10_fun/ppermute | solution.py:470
  8.8 6.0 %collective-permute-start.21 = (f32[18,8,128]{2,1,0:T(8,128)S(1)}, f32[18,8,128]{2,1,0:T(8,128)}, u32[]{:S(2)}, u32[]{:S(2)}) collective-permute-start(f32[18,8,128]{2,1,0:T(8,128)S(1)} %get-tuple-element.90), channel_id=1, source_target_pairs={{0,27},{1,28},{2,29},{3,30},{4,31},{5,24},{6,25},{7,26},{8,0},{9,1... | collective-permute-start | bytes 221192 | tf_op jit(solution)/shard_map/cond/branch_10_fun/ppermute | solution.py:471
  14.9 0.7 %copy-start.2 = (s32[4]{0:T(128)S(1)}, s32[4]{0:T(128)}, u32[]{:S(2)}) copy-start(s32[4]{0:T(128)} %refs_1_.4) | copy-start | bytes 52
  15.5 11.2 %copy-start.1 = (s32[4]{0:T(128)S(1)}, s32[4]{0:T(128)}, u32[]{:S(2)}) copy-start(s32[4]{0:T(128)} %refs_1_.7) | copy-start | bytes 52
  17.9 7.3 %collective-permute-start.35 = (f32[8,4,8,128]{3,2,1,0:T(8,128)S(1)}, f32[8,4,8,128]{3,2,1,0:T(8,128)S(1)}, u32[]{:S(2)}, u32[]{:S(2)}) collective-permute-start(f32[8,4,8,128]{3,2,1,0:T(8,128)S(1)} %step.1.refs_2_), channel_id=1, source_target_pairs={{0,6},{1,7},{2,4},{3,5},{4,2},{5,3},{6,0},{7,1},{8,14},{9,15},{10,... | collective-permute-start | bytes 393224 | tf_op jit(solution)/shard_map/ppermute | solution.py:515
  19.8 7.0 %collective-permute-start.34 = (f32[8,4,8,128]{3,2,1,0:T(8,128)S(1)}, f32[8,4,8,128]{3,2,1,0:T(8,128)S(1)}, u32[]{:S(2)}, u32[]{:S(2)}) collective-permute-start(f32[8,4,8,128]{3,2,1,0:T(8,128)S(1)} %step.1.refs_2_), channel_id=1, source_target_pairs={{0,4},{1,5},{2,6},{3,7},{4,0},{5,1},{6,2},{7,3},{8,12},{9,13},{10,... | collective-permute-start | bytes 393224 | tf_op jit(solution)/shard_map/ppermute | solution.py:515
  20.5 6.3 %collective-permute-start.33 = (f32[8,4,8,128]{3,2,1,0:T(8,128)S(1)}, f32[8,4,8,128]{3,2,1,0:T(8,128)S(1)}, u32[]{:S(2)}, u32[]{:S(2)}) collective-permute-start(f32[8,4,8,128]{3,2,1,0:T(8,128)S(1)} %step.1.refs_2_), channel_id=1, source_target_pairs={{0,2},{1,3},{2,0},{3,1},{4,6},{5,7},{6,4},{7,5},{8,10},{9,11},{10,... | collective-permute-start | bytes 393224 | tf_op jit(solution)/shard_map/ppermute | solution.py:515
  27.7 1.4 %collective-permute-start.36 = (f32[8,4,8,128]{3,2,1,0:T(8,128)S(1)}, f32[8,4,8,128]{3,2,1,0:T(8,128)S(1)}, u32[]{:S(2)}, u32[]{:S(2)}) collective-permute-start(f32[8,4,8,128]{3,2,1,0:T(8,128)S(1)} %get-tuple-element.114), channel_id=1, source_target_pairs={{0,1},{1,0},{2,3},{3,2},{4,5},{5,4},{6,7},{7,6},{8,9},{9,8},{10,11... | collective-permute-start | bytes 393224 | tf_op jit(solution)/shard_map/ppermute | solution.py:515

commit v8 on v6

--- a/solution.py
+++ b/solution.py
@@ -14,6 +14,7 @@
 TIME_STEP = 0.05
 
 LANES = 128
+LANE_BITS = 7
 SUBLANES = 8
 FIELDS = 8
 PLANES = 2
@@ -55,16 +56,21 @@
     return -(-columns // LANES)
 
 
+def hops_of(columns, cells, peers):
+    hops = sum(jnp.where(columns >= k * cells, 1, 0) for k in range(1, peers))
+    return hops, columns - hops * cells
+
+
 def plan(shear, cells, peers):
-    rest = shear % cells
+    hops, rest = hops_of(shear, cells, peers)
     middle = cells // 2
     near = (rest >= middle - 5) & (rest <= middle + 5)
     own = jnp.where(near, middle - 12, middle)
-    up = (own - shear) % cells
-    down = (own + shear) % cells
-    up_hop = (shear - own + up) // cells
-    down_hop = (shear + own) // cells
-    return own, up, down, up_hop, down_hop
+    up_hop = jnp.where(rest > own, 1, 0)
+    down_hop = jnp.where(rest + own >= cells, 1, 0)
+    up = own - rest + up_hop * cells
+    down = own + rest - down_hop * cells
+    return own, up, down, hops + up_hop, hops + down_hop
 
 
 def block_tiles(ref, f, cells):
@@ -92,11 +98,11 @@
 
 
 def cut_window(joined_ref, f, start, count):
-    whole = start // LANES
-    part = start % LANES
+    whole = start >> LANE_BITS
+    part = start & (LANES - 1)
     last = joined_ref.shape[1] - 1
     tiles = [joined_ref[f, jnp.minimum(whole + t, last)] for t in range(count + 1)]
-    turned = [turn_lanes(tile, (LANES - part) % LANES) for tile in tiles]
+    turned = [turn_lanes(tile, (LANES - part) & (LANES - 1)) for tile in tiles]
     here = lane_index() < LANES - part
     return [jnp.where(here, turned[t], turned[t + 1]) for t in range(count)]
 
@@ -119,7 +125,14 @@
     down_ref[FIELDS // 2 * single] = faces
 
 
-def join_kernel(cells, peers, shear_ref, state_ref, below_ref, out_ref, joined_ref):
+def join_kernel(
+    cells, peers, shear_ref, frac_ref, state_ref, below_ref, out_ref, weight_ref, joined_ref
+):
+    weight = jnp.zeros((SUBLANES, LANES), jnp.float32)
+    for x in range(state_ref.shape[2]):
+        level = (frac_ref[x].astype(jnp.float32) + 0.5) / FRAC
+        weight = jnp.where(row_index() == x, level, weight)
+    weight_ref[...] = weight
     own = plan(shear_ref[0], cells, peers)[0]
     for f in range(FIELDS):
 
@@ -242,9 +255,18 @@
 
 def step_kernel(
     cells, peers, rows,
-    shear_ref, frac_ref, block_ref, up_ref, up_below_ref, down_ref, down_below_ref,
+    shear_ref, weight_ref, block_ref, up_hbm, up_below_hbm, down_hbm, down_below_hbm,
     out_ref, state_ref, mid_ref, joined_ref, ghost_ref,
+    up_ref, up_below_ref, down_ref, down_below_ref, sems,
 ):
+    sources = (up_hbm, up_below_hbm, down_hbm, down_below_hbm)
+    ghost_refs = (up_ref, up_below_ref, down_ref, down_below_ref)
+    copies = [
+        pltpu.make_async_copy(source, ref, sems.at[i])
+        for i, (source, ref) in enumerate(zip(sources, ghost_refs))
+    ]
+    for copy in copies:
+        copy.start()
     place = lax.axis_index("gx")
     places = lax.axis_size("gx")
     own, up_start, down_start, _, _ = plan(shear_ref[0], cells, peers)
@@ -264,6 +286,12 @@
         for t, tile in enumerate(cut_window(joined_ref, index, start, window)):
             ghost_ref[index, t] = tile
 
+    for f in range(FIELDS):
+        for t in range(window):
+            for z in range(PLANES):
+                state_ref[t, f, z] = turn_rows(block_ref[f, t], -z * rows)
+    for copy in copies:
+        copy.wait()
     for pair in range(pairs):
         span = range(pair * single, (pair + 1) * single)
         ghosts(pair, [[ref[i] for i in span] for ref in (up_below_ref, up_ref)], up_start)
@@ -276,13 +304,12 @@
     for f in range(FIELDS):
         pair, second = divmod(f, 2)
         for t in range(window):
-            tile = block_ref[f, t]
             up = ghost_ref[pair, t]
             down = ghost_ref[pairs + pair, t]
             for z in range(PLANES):
                 up_at = z * rows + (0 if second else SENT)
                 down_at = z * rows + (SENT if second else 0)
-                value = turn_rows(tile, -z * rows)
+                value = state_ref[t, f, z]
                 value = jnp.where(row < rows, value, turn_rows(down, rows - down_at))
                 value = jnp.where(row < rows + SENT, value, turn_rows(up, rows + SENT - up_at))
                 state_ref[t, f, z] = value
@@ -320,10 +347,7 @@
                     mid_ref[t, f, z] = new[f][z]
         low, here = here, high
 
-    weight = jnp.zeros((SUBLANES, LANES), jnp.float32)
-    for x in range(rows):
-        level = (frac_ref[x].astype(jnp.float32) + 0.5) / FRAC
-        weight = jnp.where(row == x, level, weight)
+    weight = weight_ref[...]
     keep = 1.0 - weight
     low = here = terms(mid_ref, 0, window, False)
     low_done = None
@@ -362,13 +386,11 @@
 
 
 def row_sources(shift, own, cells, peers, target):
-    total = cells * peers
-    offset = cells - BELOW - own
-    shift = (shift + total - offset) % total
-    hop = shift // cells
-    rest = shift % cells
-    upper = (target + 2 * peers - hop) % peers
-    lower = (target + 2 * peers - hop - 1) % peers
+    shift = shift - (cells - BELOW - own)
+    shift = jnp.where(shift < 0, shift + cells * peers, shift)
+    hops, rest = hops_of(shift, cells, peers)
+    upper = (target + peers - hops) & (peers - 1)
+    lower = (target + peers - 1 - hops) & (peers - 1)
     return upper, lower, rest
 
 
@@ -380,14 +402,17 @@
     plans = []
     for x in range(rows):
         upper, lower, rest = row_sources(shift_ref[x], own, cells, peers, target)
-        first = upper % 2 == part % 2
-        block = jnp.where(first, upper, lower) // 2
+        first = ((upper ^ part) & 1) == 0
+        block = jnp.where(first, upper, lower) >> 1
         amount = jnp.where(first, rest, rest + spare)
-        plans.append((block, amount // LANES, amount % LANES))
+        whole = amount >> LANE_BITS
+        sources = [t - whole for t in range(count)]
+        sources = [jnp.where(t < 0, t + count, t) for t in sources]
+        plans.append((block, sources, amount & (LANES - 1)))
     for f in range(FIELDS):
         result = None
-        for x, (block, whole, fine) in enumerate(plans):
-            tiles = [block_ref[block, f, (t + count - whole) % count] for t in range(count)]
+        for x, (block, sources, fine) in enumerate(plans):
+            tiles = [block_ref[block, f, t] for t in sources]
             tiles = [turn_lanes(tile, fine) for tile in tiles]
             tiles = [jnp.where(lane < fine, tiles[t - 1], tiles[t]) for t in range(count)]
             if x == 0:
@@ -402,8 +427,8 @@
     in_refs, block_ref, out_ref = (refs[:-2], refs[-2], refs[-1])
     part = lax.axis_index("gy")
     own = plan(shear_ref[0], cells, peers)[0]
-    for i, ref in enumerate(in_refs):
-        block_ref[(part // 2) ^ i] = ref[...]
+    for i, ref in enumerate(reversed(in_refs)):
+        block_ref[(part >> 1) ^ i] = ref[...]
     turned_rows(cells, peers, rows, shift_ref, own, part, part ^ 1, block_ref, out_ref)
 
 
@@ -413,7 +438,9 @@
     turned_rows(cells, peers, rows, shift_ref, own, part, part, block_ref, out_ref)
 
 
-def merge_kernel(cells, peers, rows, shear_ref, shift_ref, mine_ref, other_ref, out_ref):
+def merge_kernel(
+    cells, peers, rows, shear_ref, shift_ref, mine_ref, other_ref, out_hbm, out_ref, out_sem
+):
     part = lax.axis_index("gy")
     own = plan(shear_ref[0], cells, peers)[0]
     row = row_index() % rows
@@ -424,19 +451,23 @@
     for x in range(rows):
         upper, _, rest = row_sources(shift_ref[x], own, cells, peers, part)
         border = jnp.where(row == x, rest, border)
-        first = jnp.where(row == x, (upper + part + 1) % 2, first)
+        first = jnp.where(row == x, ((upper ^ part) & 1) ^ 1, first)
     masks = [(lane + t * LANES >= border) == (first == 1) for t in range(count)]
     for f in range(FIELDS):
         tiles = [jnp.where(masks[t], mine_ref[f, t], other_ref[f, t]) for t in range(count)]
         value = jnp.concatenate(tiles, axis=1)[:, :cells]
         for z in range(PLANES):
             out_ref[f, z] = value[z * rows : (z + 1) * rows]
+        pltpu.make_async_copy(out_ref.at[f], out_hbm.at[f], out_sem.at[f]).start()
+    for f in range(FIELDS):
+        pltpu.make_async_copy(out_ref.at[f], out_hbm.at[f], out_sem.at[f]).wait()
 
 
 def solution(mesh):
     places, peers = (mesh.shape["gx"], mesh.shape["gy"])
     smem = pl.BlockSpec(memory_space=pltpu.SMEM)
     vmem = pl.BlockSpec(memory_space=pltpu.VMEM)
+    hbm = pl.BlockSpec(memory_space=pltpu.HBM)
     params = pltpu.CompilerParams(vmem_limit_bytes=8 * 2**20)
     axes = ("gx", "gy")
 
@@ -452,24 +483,26 @@
     devices = [(x, y) for x in range(places) for y in range(peers)]
 
     def ghosts(up_hop, down_hop, up, down):
-        rise = [(device(x, y), device(x + 1, y + up_hop * (x == places - 1))) for x, y in devices]
-        fall = [(device(x, y), device(x - 1, y - down_hop * (x == 0))) for x, y in devices]
-        return lax.ppermute(up, axes, rise), lax.ppermute(down, axes, fall)
+        out = []
+        for message, step, edge, hop in ((up, 1, places - 1, up_hop), (down, -1, 0, -down_hop)):
+            for beside in range(2):
+                route = [
+                    (device(x, y), device(x + step, y + beside + hop * (x == edge)))
+                    for x, y in devices
+                ]
+                out.append(lax.ppermute(message, axes, route))
+        return out
 
     def shards(state, shear_offset, remap_shift, frac_index):
         rows, cells = state.shape[2:]
         single = tiles_for(cells)
         double = tiles_for(2 * cells)
         window = tiles_for(BELOW + cells + ABOVE)
-        pairs = FIELDS // 2
-
-        def onward(value):
-            return lax.ppermute(value, "gy", [(i, (i + 1) % peers) for i in range(peers)])
-
-        below = onward(state)
+        edge = FIELDS // 2 * single + 1
+        below = lax.ppermute(state, "gy", [(i, (i + 1) % peers) for i in range(peers)])
         up, down = pl.pallas_call(
             lambda *refs: edge_kernel(cells, rows, *refs),
-            out_shape=[array(pairs * single), array(pairs * single + 1)],
+            out_shape=[array(edge)] * 2,
             in_specs=[vmem],
             out_specs=[vmem] * 2,
             compiler_params=params,
@@ -479,33 +512,35 @@
         branches = [
             lambda u, d, i=i: ghosts(i // 2 + i % 2, i // 2, u, d) for i in range(2 * peers)
         ]
-        which = (2 * down_hop + (up_hop - down_hop)) % (2 * peers)
-        up, down = lax.switch(which, branches, up, down)
-        up_below, down_below = onward(up), onward(down)
-        block = pl.pallas_call(
+        which = (down_hop + up_hop) & (2 * peers - 1)
+        ghost_rows = lax.switch(which, branches, up, down)
+        block, weight = pl.pallas_call(
             lambda *refs: join_kernel(cells, peers, *refs),
-            out_shape=array(FIELDS, window),
-            in_specs=[smem, vmem, vmem],
-            out_specs=vmem,
+            out_shape=[array(FIELDS, window), array()],
+            in_specs=[smem] * 2 + [vmem] * 2,
+            out_specs=[vmem] * 2,
             scratch_shapes=[scratch(FIELDS, double)],
             compiler_params=params,
             name="join",
-        )(shear_offset, state, below)
+        )(shear_offset, frac_index, state, below)
         block = pl.pallas_call(
             lambda *refs: step_kernel(cells, peers, rows, *refs),
             out_shape=array(FIELDS, single),
-            in_specs=[smem] * 2 + [vmem] * 5,
+            in_specs=[smem] + [vmem] * 2 + [hbm] * 4,
             out_specs=vmem,
             scratch_shapes=[scratch(window, FIELDS, PLANES)] * 2
-            + [scratch(FIELDS + 1, double), scratch(FIELDS + 1, window)],
+            + [scratch(FIELDS + 1, double), scratch(FIELDS + 1, window)]
+            + [scratch(edge)] * 4
+            + [pltpu.SemaphoreType.DMA((4,))],
             compiler_params=params,
             name="step",
-        )(shear_offset, frac_index, block, up, up_below, down, down_below)
+        )(shear_offset, weight, block, *ghost_rows)
 
         def exchange(value, bits):
             return lax.ppermute(value, "gy", [(i, i ^ bits) for i in range(peers)])
 
-        blocks = [block] + [exchange(block, bits) for bits in range(2, peers, 2)]
+        far = [exchange(block, bits) for bits in range(peers - 2, 0, -2)]
+        blocks = far + [block]
         blocks, other = pl.pallas_call(
             lambda *refs: gather_kernel(cells, peers, rows, *refs),
             out_shape=[array(peers // 2, FIELDS, single), array(FIELDS, single)],
@@ -527,7 +562,11 @@
             lambda *refs: merge_kernel(cells, peers, rows, *refs),
             out_shape=jax.ShapeDtypeStruct(state.shape, jnp.float32),
             in_specs=[smem] * 2 + [vmem] * 2,
-            out_specs=vmem,
+            out_specs=hbm,
+            scratch_shapes=[
+                pltpu.VMEM(state.shape, jnp.float32),
+                pltpu.SemaphoreType.DMA((FIELDS,)),
+            ],
             compiler_params=params,
             name="merge",
         )(shear_offset, remap_shift, mine, other)

time: 33.8 us -> 35.3 us (1.044); the launches traced: 33.6 us -> 34.7 us
  starting transfers between devices: 10.9 us -> 15.4 us
  waiting for transfers between devices: 15.6 us -> 11.7 us
  Pallas kernels: 5.31 us -> 5.79 us
    ppermute x5, waiting for transfers between devices: 11.6 us -> 4.57 us  [the longest x4 4.57 us: ghosts(): out.append(lax.ppermute(message, axes, route))]
    ppermute x4, waiting for transfers between devices: 4 us -> 7.09 us  [exchange(): return lax.ppermute(value, 'gy', [(i, i ^ bits) for i in range(peers)])]
    ppermute x4, starting transfers between devices: 3.62 us -> 6.45 us  [exchange(): return lax.ppermute(value, 'gy', [(i, i ^ bits) for i in range(peers)])]
    ppermute x5, starting transfers between devices: 7.27 us -> 8.99 us  [the longest x4 8.54 us: ghosts(): out.append(lax.ppermute(message, axes, route))]
    pallas_call x1, Pallas kernels: 0.21 us -> 0.76 us  [shards(): pl.pallas_call(lambda *refs: join_kernel(cells, peers, *refs), out_shape=...]
  transfers between devices with their start and end apart: 9 -> 9, of which waited for: 5 -> 6; matrix products, arithmetic and copies ran while one was open for 0% -> 0% of each run, Pallas kernels for 3% -> 2%
where the time goes in v8:
time: 35.3 us; the launch traced here: 34.7 us
  starting transfers between devices  15.4 us (44%)
  waiting for transfers between devices  11.7 us (33%)
  Pallas kernels  5.79 us (16%)
  local copies, waits for them, and re-layouts  0.91 us (3%)
  between operations  0.81 us (2%)
    ppermute x4, starting transfers between devices, ghosts(): out.append(lax.ppermute(message, axes, route))  8.54 us
    ppermute x4, waiting for transfers between devices, exchange(): return lax.ppermute(value, 'gy', [(i, i ^ bits) for i in range(peers)])  7.09 us
    ppermute x4, starting transfers between devices, exchange(): return lax.ppermute(value, 'gy', [(i, i ^ bits) for i in range(peers)])  6.45 us
    ppermute x4, waiting for transfers between devices, ghosts(): out.append(lax.ppermute(message, axes, route))  4.57 us
    pallas_call x1, Pallas kernels, shards(): pl.pallas_call(lambda *refs: step_kernel(cells, peers, rows, *refs), out_...  2.02 us
    pallas_call x1, Pallas kernels, shards(): pl.pallas_call(lambda *refs: merge_kernel(cells, peers, rows, *refs), out...  1.32 us
    unnamed x8, local copies, waits for them, and re-layouts  0.91 us
    pallas_call x1, Pallas kernels, shards(): pl.pallas_call(lambda *refs: gather_kernel(cells, peers, rows, *refs), ou...  0.84 us
  transfers between devices with their start and end apart: 9, of which 6 were waited for; matrix products, arithmetic and copies ran while one was open for 0% of the time, Pallas kernels for 2%

profile of v8, /device:TPU:0, one launch (start us, length us, event | category | flops | bytes accessed | tf_op | source)
XLA Modules:
  0.0 34.7 jit_solution(512047932524461983)
XLA Ops:
  0.0 0.5 %collective-permute-start.64 = (f32[8,2,4,508]{3,2,1,0:T(4,128)}, f32[8,2,4,508]{3,2,1,0:T(4,128)S(1)}, u32[]{:S(2)}, u32[]{:S(2)}) collective-permute-start(f32[8,2,4,508]{3,2,1,0:T(4,128)} %refs_0_.6), channel_id=1, source_target_pairs={{0,1},{1,2},{2,3},{3,4},{4,5},{5,6},{6,7},{7,0},{8,9},{9,10},{10,1... | collective-permute-start | bytes 390152 | tf_op jit(solution)/shard_map/ppermute | solution.py:502
  1.1 0.0 copy-start
  1.2 0.9 %copy-done = f32[8,2,4,508]{3,2,1,0:T(4,128)S(1)} copy-done((f32[8,2,4,508]{3,2,1,0:T(4,128)S(1)}, f32[8,2,4,508]{3,2,1,0:T(4,128)}, u32[]{:S(2)}) %copy-start) | copy-done | bytes 130072
  2.1 0.0 copy-start.1
  2.1 0.0 copy-start.3
  2.1 13.1 %conditional.1 = (f32[17,8,128]{2,1,0:T(8,128)}, f32[17,8,128]{2,1,0:T(8,128)}, f32[17,8,128]{2,1,0:T(8,128)}, f32[17,8,128]{2,1,0:T(8,128)}) conditional(s32[]{:T(128)} %clamp.3, (f32[17,8,128]{2,1,0:T(8,128)S(1)}, f32[17,8,128]{2,1,0:T(8,128)S(1)}) %edge.1, (f32[17,8,128]{2,1,0:T(8,128)S(1)}, ...), branch_computations={%region_0.1_spmd, %region_1.2_spmd, %region_2.3_spmd, %region_3.4_... | conditional | bytes 1114304 | solution.py:516
  2.1 3.8 %collective-permute-start.57 = (f32[17,8,128]{2,1,0:T(8,128)S(1)}, f32[17,8,128]{2,1,0:T(8,128)}, u32[]{:S(2)}, u32[]{:S(2)}) collective-permute-start(f32[17,8,128]{2,1,0:T(8,128)S(1)} %get-tuple-element.97), channel_id=1, source_target_pairs={{0,9},{1,10},{2,11},{3,12},{4,13},{5,14},{6,15},{7,8},{8,17},{9,18... | collective-permute-start | bytes 208904 | tf_op jit(solution)/shard_map/cond/branch_14_fun/ppermute | solution.py:493
  6.0 1.6 %collective-permute-start.56 = (f32[17,8,128]{2,1,0:T(8,128)S(1)}, f32[17,8,128]{2,1,0:T(8,128)}, u32[]{:S(2)}, u32[]{:S(2)}) collective-permute-start(f32[17,8,128]{2,1,0:T(8,128)S(1)} %get-tuple-element.97), channel_id=1, source_target_pairs={{0,8},{1,9},{2,10},{3,11},{4,12},{5,13},{6,14},{7,15},{8,16},{9,17... | collective-permute-start | bytes 208904 | tf_op jit(solution)/shard_map/cond/branch_14_fun/ppermute | solution.py:493
  7.6 2.6 %collective-permute-start.59 = (f32[17,8,128]{2,1,0:T(8,128)S(1)}, f32[17,8,128]{2,1,0:T(8,128)}, u32[]{:S(2)}, u32[]{:S(2)}) collective-permute-start(f32[17,8,128]{2,1,0:T(8,128)S(1)} %get-tuple-element.98), channel_id=1, source_target_pairs={{0,26},{1,27},{2,28},{3,29},{4,30},{5,31},{6,24},{7,25},{8,1},{9,2... | collective-permute-start | bytes 208904 | tf_op jit(solution)/shard_map/cond/branch_14_fun/ppermute | solution.py:493
  10.1 0.5 %collective-permute-start.58 = (f32[17,8,128]{2,1,0:T(8,128)S(1)}, f32[17,8,128]{2,1,0:T(8,128)}, u32[]{:S(2)}, u32[]{:S(2)}) collective-permute-start(f32[17,8,128]{2,1,0:T(8,128)S(1)} %get-tuple-element.98), channel_id=1, source_target_pairs={{0,25},{1,26},{2,27},{3,28},{4,29},{5,30},{6,31},{7,24},{8,0},{9,1... | collective-permute-start | bytes 208904 | tf_op jit(solution)/shard_map/cond/branch_14_fun/ppermute | solution.py:493
  10.7 0.0 collective-permute-done.57
  10.7 1.0 %collective-permute-done.56 = f32[17,8,128]{2,1,0:T(8,128)} collective-permute-done((f32[17,8,128]{2,1,0:T(8,128)S(1)}, f32[17,8,128]{2,1,0:T(8,128)}, u32[]{:S(2)}, u32[]{:S(2)}) %collective-permute-start.56) | collective-permute-done | bytes 69664 | tf_op jit(solution)/shard_map/cond/branch_14_fun/ppermute | solution.py:493
  11.7 3.0 %collective-permute-done.59 = f32[17,8,128]{2,1,0:T(8,128)} collective-permute-done((f32[17,8,128]{2,1,0:T(8,128)S(1)}, f32[17,8,128]{2,1,0:T(8,128)}, u32[]{:S(2)}, u32[]{:S(2)}) %collective-permute-start.59) | collective-permute-done | bytes 69664 | tf_op jit(solution)/shard_map/cond/branch_14_fun/ppermute | solution.py:493
  14.7 0.5 %collective-permute-done.58 = f32[17,8,128]{2,1,0:T(8,128)} collective-permute-done((f32[17,8,128]{2,1,0:T(8,128)S(1)}, f32[17,8,128]{2,1,0:T(8,128)}, u32[]{:S(2)}, u32[]{:S(2)}) %collective-permute-start.58) | collective-permute-done | bytes 69664 | tf_op jit(solution)/shard_map/cond/branch_14_fun/ppermute | solution.py:493
  15.3 0.0 collective-permute-done.64.refs_3_
  15.3 0.0 copy-done.1
  15.3 0.0 copy-done.3
  15.3 0.8 %join.1 = (f32[8,5,8,128]{3,2,1,0:T(8,128)S(1)}, f32[8,128]{1,0:T(8,128)S(1)}) custom-call(s32[1]{0:T(128)} %copy.69.refs_0_, s32[4]{0:T(128)S(1)} %copy-done.3, f32[8,2,4,508]{3,2,1,0:T(4,128)S(1)} %copy-done.1, f32[8,2,4,508]{3,2,1,0:T(4,128)S(1)} %collective-permute-done.64.refs_3_), custom_call_target="tpu_custom_call" | custom-call | tf_op jit(solution)/shard_map/join/pallas_call | solution.py:517
  16.0 0.0 copy-start.2
  16.1 2.0 %step.1.refs_5_ = f32[8,4,8,128]{3,2,1,0:T(8,128)S(1)} custom-call(s32[1]{0:T(128)} %copy.69.refs_0_, f32[8,128]{1,0:T(8,128)S(1)} %get-tuple-element.109.refs_1_, f32[8,5,8,128]{3,2,1,0:T(8,128)S(1)} %get-tuple-element.110.refs_2_, f32[17,8,128]{2,1,0:T(8,128)} %get-tuple-element.111.refs_3_, f32[17,8,128]{2,1,0:T(8,128)} %get-tuple-element.112.refs_4_, ...), custom_call_target="tpu_custom_call" | custom-call | tf_op jit(solution)/shard_map/step/pallas_call | solution.py:526
  18.1 1.8 %collective-permute-start.67 = (f32[8,4,8,128]{3,2,1,0:T(8,128)S(1)}, f32[8,4,8,128]{3,2,1,0:T(8,128)S(1)}, u32[]{:S(2)}, u32[]{:S(2)}) collective-permute-start(f32[8,4,8,128]{3,2,1,0:T(8,128)S(1)} %step.1.refs_5_), channel_id=1, source_target_pairs={{0,2},{1,3},{2,0},{3,1},{4,6},{5,7},{6,4},{7,5},{8,10},{9,11},{10,... | collective-permute-start | bytes 393224 | tf_op jit(solution)/shard_map/ppermute | solution.py:540
  19.8 0.5 %collective-permute-start.66 = (f32[8,4,8,128]{3,2,1,0:T(8,128)S(1)}, f32[8,4,8,128]{3,2,1,0:T(8,128)S(1)}, u32[]{:S(2)}, u32[]{:S(2)}) collective-permute-start(f32[8,4,8,128]{3,2,1,0:T(8,128)S(1)} %step.1.refs_5_), channel_id=1, source_target_pairs={{0,4},{1,5},{2,6},{3,7},{4,0},{5,1},{6,2},{7,3},{8,12},{9,13},{10,... | collective-permute-start | bytes 393224 | tf_op jit(solution)/shard_map/ppermute | solution.py:540
  20.3 4.1 %collective-permute-start.65 = (f32[8,4,8,128]{3,2,1,0:T(8,128)S(1)}, f32[8,4,8,128]{3,2,1,0:T(8,128)S(1)}, u32[]{:S(2)}, u32[]{:S(2)}) collective-permute-start(f32[8,4,8,128]{3,2,1,0:T(8,128)S(1)} %step.1.refs_5_), channel_id=1, source_target_pairs={{0,6},{1,7},{2,4},{3,5},{4,2},{5,3},{6,0},{7,1},{8,14},{9,15},{10,... | collective-permute-start | bytes 393224 | tf_op jit(solution)/shard_map/ppermute | solution.py:540
  24.5 0.0 collective-permute-done.67.refs_4_
  24.5 0.3 collective-permute-done.66.refs_3_
  24.8 6.3 %collective-permute-done.65.refs_2_ = f32[8,4,8,128]{3,2,1,0:T(8,128)S(1)} collective-permute-done((f32[8,4,8,128]{3,2,1,0:T(8,128)S(1)}, f32[8,4,8,128]{3,2,1,0:T(8,128)S(1)}, u32[]{:S(2)}, u32[]{:S(2)}) %collective-permute-start.65) | collective-permute-done | bytes 131104 | tf_op jit(solution)/shard_map/ppermute | solution.py:540
  31.1 0.0 copy-done.2
  31.1 0.8 %gather.1 = (f32[4,8,4,8,128]{4,3,2,1,0:T(8,128)S(1)}, f32[8,4,8,128]{3,2,1,0:T(8,128)S(1)}) custom-call(s32[1]{0:T(128)} %copy.69.refs_0_, s32[4]{0:T(128)S(1)} %copy-done.2, f32[8,4,8,128]{3,2,1,0:T(8,128)S(1)} %collective-permute-done.65.refs_2_, f32[8,4,8,128]{3,2,1,0:T(8,128)S(1)} %collective-permute-done.66.refs_3_, ...), custom_call_target="tpu_custom_call" | custom-call | tf_op jit(solution)/shard_map/gather/pallas_call | solution.py:544
  31.9 0.1 collective-permute-start.68
  32.0 0.8 %keep.1.refs_2_ = f32[8,4,8,128]{3,2,1,0:T(8,128)S(1)} custom-call(s32[1]{0:T(128)} %copy.69.refs_0_, s32[4]{0:T(128)S(1)} %copy-done.2, f32[4,8,4,8,128]{4,3,2,1,0:T(8,128)S(1)} %get-tuple-element.115.refs_2_), custom_call_target="tpu_custom_call" | custom-call | tf_op jit(solution)/shard_map/keep/pallas_call | solution.py:553
  32.8 0.5 %collective-permute-done.68.refs_3_ = f32[8,4,8,128]{3,2,1,0:T(8,128)S(1)} collective-permute-done((f32[8,4,8,128]{3,2,1,0:T(8,128)S(1)}, f32[8,4,8,128]{3,2,1,0:T(8,128)S(1)}, u32[]{:S(2)}, u32[]{:S(2)}) %collective-permute-start.68) | collective-permute-done | bytes 131104 | tf_op jit(solution)/shard_map/ppermute | solution.py:540
  33.3 1.3 %merge.1 = f32[8,2,4,508]{3,2,1,0:T(4,128)} custom-call(s32[1]{0:T(128)} %copy.69.refs_0_, s32[4]{0:T(128)S(1)} %copy-done.2, f32[8,4,8,128]{3,2,1,0:T(8,128)S(1)} %keep.1.refs_2_, f32[8,4,8,128]{3,2,1,0:T(8,128)S(1)} %collective-permute-done.68.refs_3_), custom_call_target="tpu_custom_call" | custom-call | tf_op jit(solution)/shard_map/merge/pallas_call | solution.py:561
  (1 shorter events, 0.0 us)
Async XLA Ops:
  0.0 15.3 %collective-permute-start.64 = (f32[8,2,4,508]{3,2,1,0:T(4,128)}, f32[8,2,4,508]{3,2,1,0:T(4,128)S(1)}, u32[]{:S(2)}, u32[]{:S(2)}) collective-permute-start(f32[8,2,4,508]{3,2,1,0:T(4,128)} %refs_0_.6), channel_id=1, source_target_pairs={{0,1},{1,2},{2,3},{3,4},{4,5},{5,6},{6,7},{7,0},{8,9},{9,10},{10,1... | collective-permute-start | bytes 390152 | tf_op jit(solution)/shard_map/ppermute | solution.py:502
  1.1 0.9 %copy-start = (f32[8,2,4,508]{3,2,1,0:T(4,128)S(1)}, f32[8,2,4,508]{3,2,1,0:T(4,128)}, u32[]{:S(2)}) copy-start(f32[8,2,4,508]{3,2,1,0:T(4,128)} %refs_0_.6) | copy-start | bytes 390148
  2.1 13.2 %copy-start.1 = (f32[8,2,4,508]{3,2,1,0:T(4,128)S(1)}, f32[8,2,4,508]{3,2,1,0:T(4,128)}, u32[]{:S(2)}) copy-start(f32[8,2,4,508]{3,2,1,0:T(4,128)} %refs_0_.6) | copy-start | bytes 390148
  2.1 13.2 %copy-start.3 = (s32[4]{0:T(128)S(1)}, s32[4]{0:T(128)}, u32[]{:S(2)}) copy-start(s32[4]{0:T(128)} %refs_1_.4) | copy-start | bytes 52
  2.1 8.5 %collective-permute-start.57 = (f32[17,8,128]{2,1,0:T(8,128)S(1)}, f32[17,8,128]{2,1,0:T(8,128)}, u32[]{:S(2)}, u32[]{:S(2)}) collective-permute-start(f32[17,8,128]{2,1,0:T(8,128)S(1)} %get-tuple-element.97), channel_id=1, source_target_pairs={{0,9},{1,10},{2,11},{3,12},{4,13},{5,14},{6,15},{7,8},{8,17},{9,18... | collective-permute-start | bytes 208904 | tf_op jit(solution)/shard_map/cond/branch_14_fun/ppermute | solution.py:493
  6.0 5.7 %collective-permute-start.56 = (f32[17,8,128]{2,1,0:T(8,128)S(1)}, f32[17,8,128]{2,1,0:T(8,128)}, u32[]{:S(2)}, u32[]{:S(2)}) collective-permute-start(f32[17,8,128]{2,1,0:T(8,128)S(1)} %get-tuple-element.97), channel_id=1, source_target_pairs={{0,8},{1,9},{2,10},{3,11},{4,12},{5,13},{6,14},{7,15},{8,16},{9,17... | collective-permute-start | bytes 208904 | tf_op jit(solution)/shard_map/cond/branch_14_fun/ppermute | solution.py:493
  7.6 7.1 %collective-permute-start.59 = (f32[17,8,128]{2,1,0:T(8,128)S(1)}, f32[17,8,128]{2,1,0:T(8,128)}, u32[]{:S(2)}, u32[]{:S(2)}) collective-permute-start(f32[17,8,128]{2,1,0:T(8,128)S(1)} %get-tuple-element.98), channel_id=1, source_target_pairs={{0,26},{1,27},{2,28},{3,29},{4,30},{5,31},{6,24},{7,25},{8,1},{9,2... | collective-permute-start | bytes 208904 | tf_op jit(solution)/shard_map/cond/branch_14_fun/ppermute | solution.py:493
  10.1 5.1 %collective-permute-start.58 = (f32[17,8,128]{2,1,0:T(8,128)S(1)}, f32[17,8,128]{2,1,0:T(8,128)}, u32[]{:S(2)}, u32[]{:S(2)}) collective-permute-start(f32[17,8,128]{2,1,0:T(8,128)S(1)} %get-tuple-element.98), channel_id=1, source_target_pairs={{0,25},{1,26},{2,27},{3,28},{4,29},{5,30},{6,31},{7,24},{8,0},{9,1... | collective-permute-start | bytes 208904 | tf_op jit(solution)/shard_map/cond/branch_14_fun/ppermute | solution.py:493
  16.0 15.0 %copy-start.2 = (s32[4]{0:T(128)S(1)}, s32[4]{0:T(128)}, u32[]{:S(2)}) copy-start(s32[4]{0:T(128)} %refs_1_.7) | copy-start | bytes 52
  18.1 6.4 %collective-permute-start.67 = (f32[8,4,8,128]{3,2,1,0:T(8,128)S(1)}, f32[8,4,8,128]{3,2,1,0:T(8,128)S(1)}, u32[]{:S(2)}, u32[]{:S(2)}) collective-permute-start(f32[8,4,8,128]{3,2,1,0:T(8,128)S(1)} %step.1.refs_5_), channel_id=1, source_target_pairs={{0,2},{1,3},{2,0},{3,1},{4,6},{5,7},{6,4},{7,5},{8,10},{9,11},{10,... | collective-permute-start | bytes 393224 | tf_op jit(solution)/shard_map/ppermute | solution.py:540
  19.8 5.0 %collective-permute-start.66 = (f32[8,4,8,128]{3,2,1,0:T(8,128)S(1)}, f32[8,4,8,128]{3,2,1,0:T(8,128)S(1)}, u32[]{:S(2)}, u32[]{:S(2)}) collective-permute-start(f32[8,4,8,128]{3,2,1,0:T(8,128)S(1)} %step.1.refs_5_), channel_id=1, source_target_pairs={{0,4},{1,5},{2,6},{3,7},{4,0},{5,1},{6,2},{7,3},{8,12},{9,13},{10,... | collective-permute-start | bytes 393224 | tf_op jit(solution)/shard_map/ppermute | solution.py:540
  20.3 10.7 %collective-permute-start.65 = (f32[8,4,8,128]{3,2,1,0:T(8,128)S(1)}, f32[8,4,8,128]{3,2,1,0:T(8,128)S(1)}, u32[]{:S(2)}, u32[]{:S(2)}) collective-permute-start(f32[8,4,8,128]{3,2,1,0:T(8,128)S(1)} %step.1.refs_5_), channel_id=1, source_target_pairs={{0,6},{1,7},{2,4},{3,5},{4,2},{5,3},{6,0},{7,1},{8,14},{9,15},{10,... | collective-permute-start | bytes 393224 | tf_op jit(solution)/shard_map/ppermute | solution.py:540
  31.9 1.4 %collective-permute-start.68 = (f32[8,4,8,128]{3,2,1,0:T(8,128)S(1)}, f32[8,4,8,128]{3,2,1,0:T(8,128)S(1)}, u32[]{:S(2)}, u32[]{:S(2)}) collective-permute-start(f32[8,4,8,128]{3,2,1,0:T(8,128)S(1)} %get-tuple-element.116), channel_id=1, source_target_pairs={{0,1},{1,0},{2,3},{3,2},{4,5},{5,4},{6,7},{7,6},{8,9},{9,8},{10,11... | collective-permute-start | bytes 393224 | tf_op jit(solution)/shard_map/ppermute | solution.py:540
